TPU v7x, 768 devices: a whole 4x8x12 slice. The times are simulated.
768 devices in a mesh: ctx: 64 (over y, x, core), head: 12 (over z).
Axes of the slice: x: 4, y: 8, z: 12, core: 2. Of those that a mesh axis runs over, the one named last changes fastest.
Arguments:
- query_lin: bfloat16 [32768, 1536], P('ctx', 'head'), may hold values from -6 to 6
- key_lin: bfloat16 [32768, 1536], P('ctx', 'head'), may hold values from -6 to 6
- value_lin: bfloat16 [32768, 1536], P('ctx', 'head'), may hold values from -6 to 6
- norm_gain: float32 [1536], P('head'), may hold values from 0.5 to 2
- grad_normed: bfloat16 [32768, 1536], P('ctx', 'head'), may hold values from -6 to 6
- query_win: bfloat16 [32768, 1536], P('ctx', 'head'), may hold values from -5 to 5
- key_win: bfloat16 [32768, 1536], P('ctx', 'head'), may hold values from -5 to 5
- value_win: bfloat16 [32768, 1536], P('ctx', 'head'), may hold values from -6 to 6
- grad_win: bfloat16 [32768, 1536], P('ctx', 'head'), may hold values from -6 to 6
Outputs:
- grad_query_lin: bfloat16 [32768, 1536], P('ctx', 'head')
- grad_key_lin: bfloat16 [32768, 1536], P('ctx', 'head')
- grad_value_lin: bfloat16 [32768, 1536], P('ctx', 'head')
- grad_query_win: bfloat16 [32768, 1536], P('ctx', 'head')
- grad_key_win: bfloat16 [32768, 1536], P('ctx', 'head')
- grad_value_win: bfloat16 [32768, 1536], P('ctx', 'head')
All inputs are finite; a program needn't handle non-finite values.
Results may differ from a plain program's by a relative error of at most 0.012.
Values may be sent and summed in bfloat16 or wider, within the bound.
No kernel may reach another device: no remote copies, remote signals or barrier semaphores. Data moves between devices by JAX's collectives and lax.ppermute only.
A program may use at most 32 MiB of HBM per device.

v0:
```python
import math

import jax
import jax.numpy as jnp
from jax import lax
from jax.sharding import PartitionSpec as P

DH = 128
WINDOW = 512


norm_eps = 1e-06
highest = lax.Precision.HIGHEST


def carried_in(part, axis, combine, identity, reverse):
    count = lax.axis_size(axis)
    place = lax.axis_index(axis)
    ahead = count - 1 - place if reverse else place
    gathered = lax.all_gather(part, axis)
    state = jnp.zeros_like(part) + jnp.asarray(identity, part.dtype)

    def one(hop, state):
        source = count - 1 - hop if reverse else hop
        return combine(state, lax.dynamic_index_in_dim(gathered, source, 0, False))

    return lax.fori_loop(0, ahead, one, state)


def from_behind(value, axis, steps):
    count = lax.axis_size(axis)
    first, last = (max(0, -steps), min(count, count - steps))
    return lax.ppermute(value, axis, [(source, source + steps) for source in range(first, last)])


def add_states(earlier, later):
    return earlier + later


def local(
    query_lin, key_lin, value_lin, norm_gain, grad_normed, query_win, key_win, value_win, grad_win
):
    tokens_here, width_here = query_lin.shape
    head_count = width_here // DH
    shaped = (tokens_here, head_count, DH)
    my_index = lax.axis_index("ctx")
    queries = query_lin.reshape(shaped)
    keys_lin = key_lin.reshape(shaped)
    values_lin = value_lin.reshape(shaped)
    local_state = jnp.einsum(
        "tha,thb->hab", keys_lin, values_lin, preferred_element_type=jnp.float32
    )
    zero_states = jnp.zeros_like(local_state)
    prior = carried_in(local_state, "ctx", add_states, zero_states, False)
    lower = jnp.arange(tokens_here)[:, None] >= jnp.arange(tokens_here)[None, :]
    scores = jnp.einsum("ihd,jhd->hij", queries, keys_lin, preferred_element_type=jnp.float32)
    probs_lin = jnp.where(lower[None], scores, 0.0).astype(jnp.bfloat16)
    queries_wide = queries.astype(jnp.float32)
    lin_out = jnp.einsum("hij,jhd->ihd", probs_lin, values_lin, preferred_element_type=jnp.float32)
    lin_out = lin_out + jnp.einsum("ihd,hde->ihe", queries_wide, prior, precision=highest)
    flat_out = lin_out.reshape(tokens_here, width_here)
    scaled = grad_normed.astype(jnp.float32) * norm_gain[None, :]
    sum_squares, cross = lax.psum(
        (jnp.sum(flat_out * flat_out, axis=1), jnp.sum(scaled * flat_out, axis=1)), "head"
    )
    total_width = width_here * lax.axis_size("head")
    root_mean = jnp.sqrt(sum_squares / total_width + norm_eps)[:, None]
    grad_out = (
        (scaled / root_mean - flat_out * cross[:, None] / (total_width * root_mean**3))
        .astype(jnp.bfloat16)
        .reshape(shaped)
    )
    later_local = jnp.einsum("tha,thb->hab", queries, grad_out, preferred_element_type=jnp.float32)
    after = carried_in(later_local, "ctx", add_states, zero_states, True)
    mix_lin = jnp.where(
        lower[None],
        jnp.einsum("ihe,jhe->hij", grad_out, values_lin, preferred_element_type=jnp.float32),
        0.0,
    ).astype(jnp.bfloat16)
    grad_query = jnp.einsum("hij,jhd->ihd", mix_lin, keys_lin, preferred_element_type=jnp.float32)
    grad_query = grad_query + jnp.einsum(
        "ihe,hde->ihd", grad_out.astype(jnp.float32), prior, precision=highest
    )
    grad_key = jnp.einsum("hij,ihd->jhd", mix_lin, queries, preferred_element_type=jnp.float32)
    grad_key = grad_key + jnp.einsum(
        "jhb,hab->jha", values_lin.astype(jnp.float32), after, precision=highest
    )
    grad_value = jnp.einsum("hij,ihe->jhe", probs_lin, grad_out, preferred_element_type=jnp.float32)
    grad_value = grad_value + jnp.einsum(
        "jha,hab->jhb", keys_lin.astype(jnp.float32), after, precision=highest
    )
    span = WINDOW
    tiles = tokens_here // span
    halo_keys, halo_values = from_behind((key_win, value_win), "ctx", 1)
    keys_ext = jnp.concatenate([halo_keys, key_win], 0).reshape(tokens_here + span, head_count, DH)
    values_ext = jnp.concatenate([halo_values, value_win], 0).reshape(
        tokens_here + span, head_count, DH
    )
    tile_shape = (tiles, span, head_count, DH)
    keys_tiled = jnp.concatenate(
        [keys_ext[:tokens_here].reshape(tile_shape), keys_ext[span:].reshape(tile_shape)], 1
    )
    values_tiled = jnp.concatenate(
        [values_ext[:tokens_here].reshape(tile_shape), values_ext[span:].reshape(tile_shape)], 1
    )
    queries_win = query_win.reshape(tile_shape)
    grad_heads = grad_win.reshape(tile_shape)
    query_pos = jnp.arange(span)[None, :, None]
    key_pos = jnp.arange(2 * span)[None, None, :]
    tile_start = (jnp.arange(tiles) * span)[:, None, None]
    allowed = (
        (key_pos > query_pos)
        & (key_pos <= query_pos + span)
        & (key_pos + tile_start + my_index * tokens_here >= span)
    )
    scale_win = 1.0 / math.sqrt(DH)
    logits = scale_win * jnp.einsum(
        "nihd,njhd->nhij", queries_win, keys_tiled, preferred_element_type=jnp.float32
    )
    logits = jnp.where(allowed[:, None], logits, -1e30)
    peak = jnp.max(logits, axis=3, keepdims=True)
    weights = jnp.exp(logits - peak)
    probs = weights / jnp.sum(weights, axis=3, keepdims=True)
    probs_win = probs.astype(jnp.bfloat16)
    win_out = jnp.einsum(
        "nhij,njhd->nihd", probs_win, values_tiled, preferred_element_type=jnp.float32
    )
    delta = jnp.sum(grad_heads.astype(jnp.float32) * win_out, axis=3)
    grad_probs = jnp.einsum(
        "nihd,njhd->nhij", grad_heads, values_tiled, preferred_element_type=jnp.float32
    )
    grad_logits = (probs * (grad_probs - jnp.transpose(delta, (0, 2, 1))[:, :, :, None])).astype(
        jnp.bfloat16
    )
    grad_query_win = scale_win * jnp.einsum(
        "nhij,njhd->nihd", grad_logits, keys_tiled, preferred_element_type=jnp.float32
    )
    key_parts = scale_win * jnp.einsum(
        "nhij,nihd->njhd", grad_logits, queries_win, preferred_element_type=jnp.float32
    )
    value_parts = jnp.einsum(
        "nhij,nihd->njhd", probs_win, grad_heads, preferred_element_type=jnp.float32
    )
    blank = jnp.zeros((span, width_here), jnp.float32)

    def spread(parts):
        first_half = parts[:, :span].reshape(tokens_here, width_here)
        second_half = parts[:, span:].reshape(tokens_here, width_here)
        return jnp.concatenate([first_half, blank], 0) + jnp.concatenate([blank, second_half], 0)

    key_terms = spread(key_parts)
    value_terms = spread(value_parts)
    back_keys, back_values = from_behind((key_terms[:span], value_terms[:span]), "ctx", -1)

    def settle(terms, returned):
        own = terms[span:]
        return jnp.concatenate([own[: tokens_here - span], own + returned], 0).astype(jnp.bfloat16)

    return (
        grad_query.reshape(tokens_here, width_here).astype(jnp.bfloat16),
        grad_key.reshape(tokens_here, width_here).astype(jnp.bfloat16),
        grad_value.reshape(tokens_here, width_here).astype(jnp.bfloat16),
        grad_query_win.reshape(tokens_here, width_here).astype(jnp.bfloat16),
        settle(key_terms, back_keys),
        settle(value_terms, back_values),
    )


def solution(mesh):
    placed = (
        P("ctx", "head"),
        P("ctx", "head"),
        P("ctx", "head"),
        P("head"),
        P("ctx", "head"),
        P("ctx", "head"),
        P("ctx", "head"),
        P("ctx", "head"),
        P("ctx", "head"),
    )
    return jax.shard_map(
        local,
        mesh=mesh,
        in_specs=placed,
        out_specs=(
            P("ctx", "head"),
            P("ctx", "head"),
            P("ctx", "head"),
            P("ctx", "head"),
            P("ctx", "head"),
            P("ctx", "head"),
        ),
        check_vma=False,
    )
```

profile of v0, /device:TPU:1, one launch (start us, length us, event | category | flops | bytes accessed | tf_op | source)
XLA Modules:
  0.0 339.6 jit_solution(6543478323209587104)
XLA Ops:
  7.2 1.9 fusion.36
  9.2 1.0 copy.15
  10.2 1.3 fusion.5
  11.5 1.3 convolution_bitcast_fusion.3
  12.8 97.6 %all-gather.5.cloned.1.call-done = f32[8192,128]{1,0:T(8,128)} async-done(((f32[128,128]{1,0:T(8,128)}), f32[8192,128]{1,0:T(8,128)}) %all-gather.5.cloned.1.call-update) | async-done | bytes 4194320 | tf_op jit(solution)/shard_map/all_gather | solution.py:20
  111.7 19.9 %all-reduce.4 = (f32[512]{0:T(512)S(1)}, f32[512]{0:T(512)S(1)}) all-reduce(f32[512]{0:T(512)S(1)} %get-tuple-element.102, f32[512]{0:T(512)S(1)} %get-tuple-element.101), channel_id=1, replica_groups=mesh['ctx'=64,'head'=12] {'head'}, use_global_device_ids=true, to_apply=%region_3.4 | all-reduce | flops 1024 | bytes 8192 | tf_op jit(solution)/shard_map/psum | solution.py:63
  132.6 8.1 %collective-permute-start = (bf16[512,128]{1,0:T(8,128)(2,1)S(1)}, bf16[512,128]{1,0:T(8,128)(2,1)S(1)}, u32[]{:S(2)}, u32[]{:S(2)}) collective-permute-start(bf16[512,128]{1,0:T(8,128)(2,1)S(1)} %copy-done.6), channel_id=1, source_target_pairs={{0,12},{12,24},{24,36},{36,48},{48,60},{60,72},{72,84},{84,96},{96... | collective-permute-start | bytes 393224 | tf_op jit(solution)/shard_map/ppermute | solution.py:33
  140.7 1.9 collective-permute-start.1
  146.0 2.2 collective-permute-start.2
  148.7 2.1 collective-permute-start.3
  151.9 3.2 collective-permute-done.2
  155.8 2.1 collective-permute-done.3
  159.2 1.0 fusion.17
  160.8 109.8 %all-gather.7.cloned.1.call-done = f32[8192,128]{0,1:T(8,128)} async-done(((f32[128,128]{0,1:T(8,128)}), f32[8192,128]{0,1:T(8,128)}) %all-gather.7.cloned.1.call-update) | async-done | bytes 4194320 | tf_op jit(solution)/shard_map/all_gather | solution.py:20
  270.6 5.6 %copy.25 = f32[8192,128]{1,0:T(8,128)} copy(f32[8192,128]{0,1:T(8,128)} %all-gather.7.cloned.1.call-done) | data formatting | bytes 8388608 | tf_op jit(solution)/shard_map/while | solution.py:27
  276.2 54.5 %while.23 = (s32[]{:T(128)}, f32[1,128,128]{2,1,0:T(8,128)S(1)}, s32[]{:T(128)}, f32[64,1,128,128]{3,2,1,0:T(8,128)}, s32[]{:T(128)}, /*index=5*/s32[]{:T(128)}, s32[]{:T(128)}, s32[]{:T(128)}) while((s32[]{:T(128)}, f32[1,128,128]{2,1,0:T(8,128)S(1)}, s32[]{:T(128)}, f32[64,1,128,128]{3,2,1,0:T(8,128)}, s32[]{:T(128)}, /*index=5*/s32[]{:T(128)}, ...), condition=%wide.region_7.8_spmd, body=%wide.region_6.7_spmd.sunk | while | flops 16390 | bytes 196751 | solution.py:27
  277.1 0.9 bitcast_add_fusion.5
  278.0 0.9 bitcast_add_fusion.5
  278.8 0.9 bitcast_add_fusion.5
  279.7 0.9 bitcast_add_fusion.5
  280.6 0.9 bitcast_add_fusion.5
  281.5 0.9 bitcast_add_fusion.5
  282.4 0.9 bitcast_add_fusion.5
  283.2 0.9 bitcast_add_fusion.5
  284.1 0.9 bitcast_add_fusion.5
  288.5 0.9 bitcast_add_fusion.5
  291.2 0.9 bitcast_add_fusion.5
  305.2 0.9 bitcast_add_fusion.5
  307.9 0.9 bitcast_add_fusion.5
  321.9 0.9 bitcast_add_fusion.5
  324.6 0.9 bitcast_add_fusion.5
  331.8 0.9 fusion.16
  (107 shorter events, 51.9 us)
Async XLA Ops:
  7.2 135.6 %copy-start = (bf16[512,128]{1,0:T(8,128)(2,1)S(1)}, bf16[512,128]{1,0:T(8,128)(2,1)}, u32[]{:S(2)}) copy-start(bf16[512,128]{1,0:T(8,128)(2,1)} %param.18) | copy-start | bytes 393220
  7.2 104.1 %copy-start.1 = (bf16[512,128]{1,0:T(8,128)(2,1)S(1)}, bf16[512,128]{1,0:T(8,128)(2,1)}, u32[]{:S(2)}) copy-start(bf16[512,128]{1,0:T(8,128)(2,1)} %param.13) | copy-start | bytes 393220
  7.2 104.1 %copy-start.10 = (f32[128]{0:T(128)S(1)}, f32[128]{0:T(128)}, u32[]{:S(2)}) copy-start(f32[128]{0:T(128)} %param.16) | copy-start | bytes 1540
  7.2 103.2 %all-gather.5.cloned.1.call-start = ((), (), s32[]{:S(2)}) async-start(), calls=%async_computation | async-start | bytes 4259840 | tf_op jit(solution)/shard_map/all_gather | solution.py:20
  9.1 261.5 %all-gather.7.cloned.1.call-start = ((), (), s32[]{:S(2)}) async-start(), calls=%async_computation.1 | async-start | bytes 4259840 | tf_op jit(solution)/shard_map/all_gather | solution.py:20
  11.5 121.1 %copy-start.6 = (bf16[512,128]{1,0:T(8,128)(2,1)S(1)}, bf16[512,128]{1,0:T(8,128)(2,1)}, u32[]{:S(2)}) copy-start(bf16[512,128]{1,0:T(8,128)(2,1)} %param.19) | copy-start | bytes 393220
  11.5 129.2 %copy-start.5 = (bf16[512,128]{1,0:T(8,128)(2,1)S(1)}, bf16[512,128]{1,0:T(8,128)(2,1)}, u32[]{:S(2)}) copy-start(bf16[512,128]{1,0:T(8,128)(2,1)} %param.20) | copy-start | bytes 393220
  11.5 131.1 %copy-start.4 = (bf16[512,128]{1,0:T(8,128)(2,1)S(1)}, bf16[512,128]{1,0:T(8,128)(2,1)}, u32[]{:S(2)}) copy-start(bf16[512,128]{1,0:T(8,128)(2,1)} %param.21) | copy-start | bytes 393220
  132.6 10.2 %collective-permute-start = (bf16[512,128]{1,0:T(8,128)(2,1)S(1)}, bf16[512,128]{1,0:T(8,128)(2,1)S(1)}, u32[]{:S(2)}, u32[]{:S(2)}) collective-permute-start(bf16[512,128]{1,0:T(8,128)(2,1)S(1)} %copy-done.6), channel_id=1, source_target_pairs={{0,12},{12,24},{24,36},{36,48},{48,60},{60,72},{72,84},{84,96},{96... | collective-permute-start | bytes 393224 | tf_op jit(solution)/shard_map/ppermute | solution.py:33
  140.7 3.9 %collective-permute-start.1 = (bf16[512,128]{1,0:T(8,128)(2,1)S(1)}, bf16[512,128]{1,0:T(8,128)(2,1)S(1)}, u32[]{:S(2)}, u32[]{:S(2)}) collective-permute-start(bf16[512,128]{1,0:T(8,128)(2,1)S(1)} %copy-done.5), channel_id=1, source_target_pairs={{0,12},{12,24},{24,36},{36,48},{48,60},{60,72},{72,84},{84,96},{96... | collective-permute-start | bytes 393224 | tf_op jit(solution)/shard_map/ppermute | solution.py:33
  142.8 0.7 copy-start.8
  145.9 4.8 %copy-start.7 = (bf16[512,128]{1,0:T(8,128)(2,1)S(1)}, bf16[512,128]{1,0:T(8,128)(2,1)}, u32[]{:S(2)}) copy-start(bf16[512,128]{1,0:T(8,128)(2,1)} %param.19) | copy-start | bytes 393220
  146.0 4.8 %copy-start.9 = (bf16[512,128]{1,0:T(8,128)(2,1)S(1)}, bf16[512,128]{1,0:T(8,128)(2,1)}, u32[]{:S(2)}) copy-start(bf16[512,128]{1,0:T(8,128)(2,1)} %copy-done.8) | copy-start | bytes 393220
  146.0 9.1 %collective-permute-start.2 = (f32[512,128]{1,0:T(8,128)S(1)}, f32[512,128]{1,0:T(8,128)S(1)}, u32[]{:S(2)}, u32[]{:S(2)}) collective-permute-start(f32[512,128]{1,0:T(8,128)S(1)} %pad_add_fusion.1), channel_id=1, source_target_pairs={{12,0},{24,12},{36,24},{48,36},{60,48},{72,60},{84,72},{96,84},{10... | collective-permute-start | bytes 786440 | tf_op jit(solution)/shard_map/ppermute | solution.py:33
  148.7 9.9 %copy-start.3 = (bf16[512,128]{1,0:T(8,128)(2,1)S(1)}, bf16[512,128]{1,0:T(8,128)(2,1)}, u32[]{:S(2)}) copy-start(bf16[512,128]{1,0:T(8,128)(2,1)} %param.15) | copy-start | bytes 393220
  148.7 10.2 %copy-start.2 = (bf16[512,128]{1,0:T(8,128)(2,1)S(1)}, bf16[512,128]{1,0:T(8,128)(2,1)}, u32[]{:S(2)}) copy-start(bf16[512,128]{1,0:T(8,128)(2,1)} %param.14) | copy-start | bytes 393220
  148.7 9.2 %collective-permute-start.3 = (f32[512,128]{1,0:T(8,128)S(1)}, f32[512,128]{1,0:T(8,128)S(1)}, u32[]{:S(2)}, u32[]{:S(2)}) collective-permute-start(f32[512,128]{1,0:T(8,128)S(1)} %pad_add_fusion), channel_id=1, source_target_pairs={{12,0},{24,12},{36,24},{48,36},{60,48},{72,60},{84,72},{96,84},{10... | collective-permute-start | bytes 786440 | tf_op jit(solution)/shard_map/ppermute | solution.py:33
Sparse Core Ops, SparseCore 0:
  12.5 97.8 all-gather.4
  132.7 137.8 all-gather.6
where the time goes:
time: 343 us; the launch traced here: 340 us
  waiting for transfers between devices  213 us (62%)
  other arithmetic  56.2 us (16%)
  blocking collectives  19.9 us (6%)
  between operations  14.4 us (4%)
  starting transfers between devices  14.3 us (4%)
  matrix products  11.7 us (3%)
  local copies, waits for them, and re-layouts  8.4 us (2%)
    all_gather x2, waiting for transfers between devices, carried_in(): gathered = lax.all_gather(part, axis)  207 us
    add x63, other arithmetic, add_states(): return earlier + later  54 us
    psum x1, blocking collectives, local(): lax.psum((jnp.sum(flat_out * flat_out, axis=1), jnp.sum(scaled * flat_out...  19.9 us
    ppermute x4, starting transfers between devices, from_behind(): lax.ppermute(value, axis, [(source, source + steps) for source in range(f...  14.2 us
  transfers between devices with their start and end apart: 6, of which 5 were waited for; matrix products, arithmetic and copies ran while one was open for 3% of the time, Pallas kernels for 0%

commit v1 on v0

v1 whole, which is shorter than its diff:
```python
import functools
import math

import jax
import jax.numpy as jnp
from jax import lax
from jax.experimental import pallas as pl
from jax.experimental.pallas import tpu as pltpu
from jax.sharding import PartitionSpec as P

DH = 128
WINDOW = 512
TILE = 128
ROW = 8
NORM_EPS = 1e-06
HIDDEN = -1e30

f32 = jnp.float32
bf16 = jnp.bfloat16


def dot(left, right, dims):
    return lax.dot_general(left, right, (dims, ((), ())), preferred_element_type=f32)


def dot_nn(left, right):
    return dot(left, right, ((1,), (0,)))


def dot_nt(left, right):
    return dot(left, right, ((1,), (1,)))


def dot_tn(left, right):
    return dot(left, right, ((0,), (0,)))


def halves(value):
    high = value.astype(bf16)
    return high, (value - high.astype(f32)).astype(bf16)


def kernel_call(body, outs, flops, moved, exps=0, scratch=(), limit=12, specs=None):
    return pl.pallas_call(
        body,
        out_shape=outs,
        scratch_shapes=list(scratch),
        compiler_params=pltpu.CompilerParams(vmem_limit_bytes=limit << 20),
        cost_estimate=pl.CostEstimate(
            flops=int(flops), bytes_accessed=int(moved), transcendentals=int(exps)
        ),
        **({"in_specs": specs} if specs else {}),
    )


def shaped(shape, dtype):
    return jax.ShapeDtypeStruct(shape, dtype)


def diagonal_tiles():
    rows = lax.broadcasted_iota(jnp.int32, (TILE, TILE), 0)
    cols = lax.broadcasted_iota(jnp.int32, (TILE, TILE), 1)
    return rows <= cols, rows >= cols


def state_body(key_ref, value_ref, out_ref):
    state = dot_tn(key_ref[...], value_ref[...]).astype(bf16)
    for place in range(out_ref.shape[0]):
        out_ref[place] = state


def total_body(parts_ref, out_ref):
    total = parts_ref[0].astype(f32)
    for place in range(1, parts_ref.shape[0]):
        total = total + parts_ref[place].astype(f32)
    total = total.astype(bf16)
    for place in range(out_ref.shape[0]):
        out_ref[place] = total


def chosen_sum(where_ref, rows_ref, parts_ref, later):
    row, col = where_ref[0], where_ref[1]
    total = None
    for ref, mine in ((rows_ref, row), (parts_ref, col)):
        for place in range(ref.shape[0]):
            wanted = place > mine if later else place < mine
            term = jnp.where(wanted, ref[place].astype(f32), 0.0)
            total = term if total is None else total + term
    return total


def inner_body(query_ref, key_ref, value_ref, out_ref):
    tokens = query_ref.shape[0]
    _, lower = diagonal_tiles()
    for start in range(0, tokens, TILE):
        stop = start + TILE
        query = query_ref[start:stop]
        scores = dot_nt(query, key_ref[start:stop])
        probs = jnp.where(lower, scores, 0.0).astype(bf16)
        result = dot_nn(probs, value_ref[start:stop])
        if start:
            probs = dot_nt(query, key_ref[:start]).astype(bf16)
            result = result + dot_nn(probs, value_ref[:start])
        out_ref[start:stop] = result


def normed_body(
    where_ref, rows_ref, parts_ref, inner_ref, query_ref, grad_ref, gain_ref,
    lin_ref, prior_ref, sums_ref,
):
    prior = chosen_sum(where_ref, rows_ref, parts_ref, False)
    prior_ref[...] = prior
    high, low = halves(prior)
    query = query_ref[...]
    lin_out = inner_ref[...] + dot_nn(query, high) + dot_nn(query, low)
    lin_ref[...] = lin_out
    scaled = grad_ref[...].astype(f32) * gain_ref[...]
    squares, crosses = lin_out * lin_out, scaled * lin_out
    pieces = []
    for terms in (squares, crosses):
        for start in range(0, terms.shape[0], TILE):
            turned = jnp.transpose(terms[start : start + TILE])
            pieces.append(jnp.sum(turned, axis=0, keepdims=True))
    packed = jnp.concatenate(pieces, 0)
    for place in range(sums_ref.shape[0]):
        sums_ref[place] = packed


def grad_out_body(sums_ref, lin_ref, grad_ref, gain_ref, query_ref, out_ref, state_ref, *, width):
    total = sums_ref[0]
    for place in range(1, sums_ref.shape[0]):
        total = total + sums_ref[place]
    groups = total.shape[0] // 2
    inverse = 1.0 / jnp.sqrt(total[:groups] / width + NORM_EPS)
    weight = total[groups:] * inverse * inverse * inverse / width
    turned = jnp.transpose(jnp.concatenate([inverse, weight], 0))
    for group in range(groups):
        tokens = slice(group * TILE, (group + 1) * TILE)
        scaled = grad_ref[tokens].astype(f32) * gain_ref[...]
        grad_out = (
            scaled * turned[:, group : group + 1]
            - lin_ref[tokens] * turned[:, groups + group : groups + group + 1]
        )
        out_ref[tokens] = grad_out.astype(bf16)
    state = dot_tn(query_ref[...], out_ref[...]).astype(bf16)
    for place in range(state_ref.shape[0]):
        state_ref[place] = state


def mixed_body(
    grad_ref, query_ref, key_ref, value_ref, prior_ref, gq_ref, gk_ref, gv_ref,
):
    tokens = query_ref.shape[0]
    upper, lower = diagonal_tiles()
    high, low = halves(prior_ref[...])
    for start in range(0, tokens, TILE):
        stop = start + TILE
        here = slice(start, stop)
        grad, query, key, value = grad_ref[here], query_ref[here], key_ref[here], value_ref[here]
        mix = jnp.where(lower, dot_nt(grad, value), 0.0).astype(bf16)
        result = dot_nn(mix, key) + dot_nt(grad, high) + dot_nt(grad, low)
        if start:
            mix = dot_nt(grad, value_ref[:start]).astype(bf16)
            result = result + dot_nn(mix, key_ref[:start])
        gq_ref[here] = result.astype(bf16)
        mix = jnp.where(upper, dot_nt(value, grad), 0.0).astype(bf16)
        probs = jnp.where(upper, dot_nt(key, query), 0.0).astype(bf16)
        key_part, value_part = dot_nn(mix, query), dot_nn(probs, grad)
        if stop < tokens:
            mix = dot_nt(value, grad_ref[stop:]).astype(bf16)
            probs = dot_nt(key, query_ref[stop:]).astype(bf16)
            key_part = key_part + dot_nn(mix, query_ref[stop:])
            value_part = value_part + dot_nn(probs, grad_ref[stop:])
        gk_ref[here] = key_part
        gv_ref[here] = value_part


def closing_body(
    where_ref, rows_ref, parts_ref, gk_part_ref, gv_part_ref, key_ref, value_ref, gk_ref, gv_ref,
):
    high, low = halves(chosen_sum(where_ref, rows_ref, parts_ref, True))
    key, value = key_ref[...], value_ref[...]
    gk_ref[...] = (gk_part_ref[...] + dot_nt(value, high) + dot_nt(value, low)).astype(bf16)
    gv_ref[...] = (gv_part_ref[...] + dot_nn(key, high) + dot_nn(key, low)).astype(bf16)


def window_body(
    where_ref, query_ref, key_ref, value_ref, grad_ref, halo_ref,
    gq_ref, back_ref, gk_ref, gv_ref, gk_halo, gv_halo,
):
    span = query_ref.shape[0]
    scale = 1.0 / math.sqrt(DH)
    first = where_ref[2] == 0
    upper, _ = diagonal_tiles()
    for start in range(0, span, TILE):
        stop = start + TILE
        here = slice(start, stop)
        query, grad = query_ref[here], grad_ref[here]
        halo_key, halo_value = halo_ref[start:span], halo_ref[span + start :]
        own_key, own_value = key_ref[:stop], value_ref[:stop]
        behind = dot_nt(halo_key, query)
        edge = jnp.where(upper, HIDDEN, behind[:TILE])
        if stop < span:
            behind = jnp.concatenate([edge, behind[TILE:]], 0)
        else:
            behind = edge
        behind = jnp.where(first, HIDDEN, behind)
        own = dot_nt(own_key, query)
        edge = jnp.where(upper, own[start:], HIDDEN)
        own = jnp.concatenate([own[:start], edge], 0) if start else edge
        peak = jnp.maximum(
            jnp.max(behind, axis=0, keepdims=True), jnp.max(own, axis=0, keepdims=True)
        )
        behind = jnp.exp((behind - peak) * scale)
        own = jnp.exp((own - peak) * scale)
        total = jnp.sum(behind, axis=0, keepdims=True) + jnp.sum(own, axis=0, keepdims=True)
        inverse = 1.0 / total
        behind, own = behind * inverse, own * inverse
        behind_win, own_win = behind.astype(bf16), own.astype(bf16)
        behind_grad = dot_nt(halo_value, grad)
        own_grad = dot_nt(own_value, grad)
        delta = jnp.sum(behind_win.astype(f32) * behind_grad, axis=0, keepdims=True) + jnp.sum(
            own_win.astype(f32) * own_grad, axis=0, keepdims=True
        )
        behind_logit = (behind * (behind_grad - delta)).astype(bf16)
        own_logit = (own * (own_grad - delta)).astype(bf16)
        result = dot_tn(halo_key, behind_logit) + dot_tn(own_key, own_logit)
        gq_ref[here] = (jnp.transpose(result) * scale).astype(bf16)
        for out, rows, terms in (
            (gk_halo, slice(start, span), dot_nn(behind_logit, query) * scale),
            (gv_halo, slice(start, span), dot_nn(behind_win, grad)),
            (gk_ref, slice(0, stop), dot_nn(own_logit, query) * scale),
            (gv_ref, slice(0, stop), dot_nn(own_win, grad)),
        ):
            if out is gk_halo or out is gv_halo:
                if start:
                    out[rows] += terms
                else:
                    out[rows] = terms
            else:
                if start:
                    out[:start] += terms[:start]
                out[here] = terms[start:]
    back_ref[:span] = gk_halo[...].astype(bf16)
    back_ref[span:] = gv_halo[...].astype(bf16)


def settle_body(gk_ref, gv_ref, back_ref, gk_out, gv_out):
    span = gk_ref.shape[0]
    gk_out[...] = (gk_ref[...] + back_ref[:span].astype(f32)).astype(bf16)
    gv_out[...] = (gv_ref[...] + back_ref[span:].astype(f32)).astype(bf16)


def local(
    query_lin, key_lin, value_lin, norm_gain, grad_normed, query_win, key_win, value_win, grad_win
):
    tokens, width = query_lin.shape
    blocks, heads = lax.axis_size("ctx"), lax.axis_size("head")
    rows = blocks // ROW
    my_index = lax.axis_index("ctx")
    where = jnp.stack([my_index // ROW, my_index % ROW, my_index]).astype(jnp.int32)
    row_groups = [[row * ROW + col for col in range(ROW)] for row in range(rows)]
    col_groups = [[row * ROW + col for row in range(rows)] for col in range(ROW)]
    gain = norm_gain.reshape(1, width)
    state = (DH, DH)
    block = (tokens, width)
    macs = tokens * DH * DH
    square = tokens * tokens * DH
    size = tokens * DH * 2
    in_smem = pl.BlockSpec(memory_space=pltpu.SMEM)
    in_vmem = pl.BlockSpec(memory_space=pltpu.VMEM)

    def along_row(value):
        return lax.all_to_all(value, "ctx", 0, 0, axis_index_groups=row_groups)

    def along_col(value):
        return lax.all_to_all(value, "ctx", 0, 0, axis_index_groups=col_groups)

    def row_total(parts):
        return kernel_call(
            total_body, shaped((rows,) + state, bf16), 8 * DH * DH, 16 * DH * DH * 2
        )(parts)

    def shift(value, steps):
        first, last = max(0, -steps), min(blocks, blocks - steps)
        return lax.ppermute(value, "ctx", [(at, at + steps) for at in range(first, last)])

    own_state = kernel_call(
        state_body, shaped((ROW,) + state, bf16), 2 * macs, 2 * size + ROW * DH * DH * 2
    )(key_lin, value_lin)
    parts = along_row(own_state)
    halo = shift(jnp.concatenate([key_win, value_win], 0), 1)
    inner = kernel_call(inner_body, shaped(block, f32), 2.5 * square, 5 * size)(
        query_lin, key_lin, value_lin
    )
    row_parts = along_col(row_total(parts))
    gq_win, back, gk_own, gv_own = kernel_call(
        window_body,
        (shaped(block, bf16), shaped((2 * tokens, width), bf16), shaped(block, f32), shaped(block, f32)),
        12.5 * square,
        13 * size,
        tokens * tokens,
        (pltpu.VMEM(block, f32), pltpu.VMEM(block, f32)),
        16,
        [in_smem] + [in_vmem] * 5,
    )(where, query_win, key_win, value_win, grad_win, halo)
    lin_out, prior, sums = kernel_call(
        normed_body,
        (shaped(block, f32), shaped(state, f32), shaped((heads, 8, TILE), f32)),
        4 * macs,
        8 * size,
        specs=[in_smem] + [in_vmem] * 6,
    )(where, row_parts, parts, inner, query_lin, grad_normed, gain)
    all_sums = lax.all_to_all(sums, "head", 0, 0)
    returned = shift(back, -1)
    grad_out, later_state = kernel_call(
        functools.partial(grad_out_body, width=float(width * heads)),
        (shaped(block, bf16), shaped((ROW,) + state, bf16)),
        2 * macs,
        8 * size,
    )(all_sums, lin_out, grad_normed, gain, query_lin)
    later_parts = along_row(later_state)
    gq_lin, gk_part, gv_part = kernel_call(
        mixed_body, (shaped(block, bf16), shaped(block, f32), shaped(block, f32)), 7 * square, 10 * size
    )(grad_out, query_lin, key_lin, value_lin, prior)
    later_rows = along_col(row_total(later_parts))
    gk_win, gv_win = kernel_call(settle_body, (shaped(block, bf16),) * 2, tokens * DH, 8 * size)(
        gk_own, gv_own, returned
    )
    gk_lin, gv_lin = kernel_call(
        closing_body,
        (shaped(block, bf16),) * 2,
        8 * macs,
        8 * size,
        specs=[in_smem] + [in_vmem] * 6,
    )(where, later_rows, later_parts, gk_part, gv_part, key_lin, value_lin)
    return gq_lin, gk_lin, gv_lin, gq_win, gk_win, gv_win


def solution(mesh):
    placed = P("ctx", "head")
    return jax.shard_map(
        local,
        mesh=mesh,
        in_specs=(placed, placed, placed, P("head")) + (placed,) * 5,
        out_specs=(placed,) * 6,
        check_vma=False,
    )
```

time: 343 us -> 94.9 us (0.28)
  waiting for transfers between devices: 213 us -> 17.1 us
  other arithmetic: 56.2 us -> 0.1 us
  blocking collectives: 19.9 us -> 39.9 us
  between operations: 14.4 us -> 0.79 us
  Pallas kernels: 0 us -> 13 us
  matrix products: 11.7 us -> 0 us
  starting transfers between devices: 14.3 us -> 21.2 us
  local copies, waits for them, and re-layouts: 8.4 us -> 1.84 us
    all_gather x2 -> x0, waiting for transfers between devices: 207 us -> none  [carried_in(): gathered = lax.all_gather(part, axis)]
    add x66 -> x0, other arithmetic: 54 us -> none  [the longest x63 54 us: add_states(): return earlier + later]
    all_to_all x0 -> x2, blocking collectives: none -> 39.9 us  [the longest x1 20.5 us: local(): all_sums = lax.all_to_all(sums, 'head', 0, 0)]
    psum x1 -> x0, blocking collectives: 19.9 us -> none  [local(): lax.psum((jnp.sum(flat_out * flat_out, axis=1), jnp.sum(scaled * flat_out...]
    all_to_all x0 -> x3, starting transfers between devices: none -> 14.7 us  [the longest x1 7.61 us: along_row(): return lax.all_to_all(value, 'ctx', 0, 0, axis_index_groups=row_groups)]
    pallas_call x0 -> x10, Pallas kernels: none -> 13 us  [the longest x1 3.55 us: local(): kernel_call(window_body, (shaped(block, bf16), shaped((2 * tokens, width)...]
    all_to_all x0 -> x3, waiting for transfers between devices: none -> 12.1 us  [the longest x2 9.13 us: along_col(): return lax.all_to_all(value, 'ctx', 0, 0, axis_index_groups=col_groups)]
    dot_general x18 -> x0, matrix products: 11.7 us -> none  [the longest x1 1.87 us: local(): jnp.einsum('tha,thb->hab', keys_lin, values_lin, preferred_element_type=j...]
  transfers between devices with their start and end apart: 6 -> 5, of which waited for: 5 -> 3; matrix products, arithmetic and copies ran while one was open for 3% -> 0% of each run, Pallas kernels for 0% -> 9%
where the time goes in v1:
time: 94.9 us; the launch traced here: 93.9 us
  blocking collectives  39.9 us (42%)
  starting transfers between devices  21.2 us (22%)
  waiting for transfers between devices  17.1 us (18%)
  Pallas kernels  13 us (14%)
  local copies, waits for them, and re-layouts  1.84 us (2%)
    all_to_all x1, blocking collectives, local(): all_sums = lax.all_to_all(sums, 'head', 0, 0)  20.5 us
    all_to_all x1, blocking collectives, along_row(): return lax.all_to_all(value, 'ctx', 0, 0, axis_index_groups=row_groups)  19.4 us
    all_to_all x2, waiting for transfers between devices, along_col(): return lax.all_to_all(value, 'ctx', 0, 0, axis_index_groups=col_groups)  9.13 us
    all_to_all x1, starting transfers between devices, along_row(): return lax.all_to_all(value, 'ctx', 0, 0, axis_index_groups=row_groups)  7.61 us
    all_to_all x2, starting transfers between devices, along_col(): return lax.all_to_all(value, 'ctx', 0, 0, axis_index_groups=col_groups)  7.08 us
    ppermute x2, starting transfers between devices, shift(): lax.ppermute(value, 'ctx', [(at, at + steps) for at in range(first, last)])  6.47 us
    ppermute x2, waiting for transfers between devices, shift(): lax.ppermute(value, 'ctx', [(at, at + steps) for at in range(first, last)])  5.04 us
    pallas_call x1, Pallas kernels, local(): kernel_call(window_body, (shaped(block, bf16), shaped((2 * tokens, width)...  3.55 us
  transfers between devices with their start and end apart: 5, of which 3 were waited for; matrix products, arithmetic and copies ran while one was open for 0% of the time, Pallas kernels for 9%

profile of v1, /device:TPU:1, one launch (start us, length us, event | category | flops | bytes accessed | tf_op | source)
XLA Modules:
  0.0 93.9 jit_solution(7199414811031985820)
XLA Ops:
  0.6 0.0 copy-start.1
  0.6 0.9 copy-done.1
  1.5 0.9 copy-done.3
  2.4 0.2 shard_map.136
  2.7 19.4 %all_to_all.25.parts_ref = bf16[8,128,128]{2,1,0:T(8,128)(2,1)S(1)} all-to-all(bf16[8,128,128]{2,1,0:T(8,128)(2,1)S(1)} %shard_map.136), channel_id=1, replica_groups={{0,12,24,36,48,60,72,84},{96,108,120,132,144,156,168,180},{192,204,216,..., dimensions={0} | all-to-all | bytes 524288 | tf_op jit(solution)/shard_map/all_to_all | solution.py:274
  22.1 0.8 shard_map.137
  22.9 3.5 %all-to-all-start.1 = ((bf16[8,128,128]{2,1,0:T(8,128)(2,1)}), bf16[8,128,128]{2,1,0:T(8,128)(2,1)S(1)}, u32[]{:S(2)}, u32[]{:S(2)}) async-start(bf16[8,128,128]{2,1,0:T(8,128)(2,1)} %shard_map.137), calls=%async_computation.1 | async-start | bytes 524288 | tf_op jit(solution)/shard_map/all_to_all | solution.py:277
  26.4 0.0 copy-done
  26.4 0.0 copy-done.2
  26.5 0.0 copy-done.4
  26.5 0.0 copy-start.5
  26.5 0.8 shard_map.138.inner_ref
  27.3 0.1 pad_add_fusion.where_ref
  27.4 9.1 %all-to-all-done.1.rows_ref = bf16[8,128,128]{2,1,0:T(8,128)(2,1)S(1)} async-done(((bf16[8,128,128]{2,1,0:T(8,128)(2,1)}), bf16[8,128,128]{2,1,0:T(8,128)(2,1)S(1)}, u32[]{:S(2)}, u32[]{:S(2)}) %all-to-all-start.1) | async-done | bytes 262176 | tf_op jit(solution)/shard_map/all_to_all | solution.py:277
  36.5 0.0 copy-done.5
  36.5 0.0 copy-done.8
  36.5 1.0 %shard_map.139 = (f32[512,128]{1,0:T(8,128)S(1)}, f32[128,128]{1,0:T(8,128)S(1)}, f32[12,8,128]{2,1,0:T(8,128)S(1)}) custom-call(s32[3]{0:T(128)S(1)} %pad_add_fusion.where_ref, bf16[8,128,128]{2,1,0:T(8,128)(2,1)S(1)} %all-to-all-done.1.rows_ref, bf16[8,128,128]{2,1,0:T(8,128)(2,1)S(1)} %all_to_all.25.parts_ref, f32[512,128]{1,0:T(8,128)S(1)} %shard_map.138.inner_ref, ...), custom_call_target="tpu_custom_call" | custom-call | flops 33554432 | bytes 1048576 | tf_op jit(solution)/shard_map/pallas_call | solution.py:307
  37.5 20.5 %all_to_all.26.sums_ref = f32[12,8,128]{2,1,0:T(8,128)S(1)} all-to-all(f32[12,8,128]{2,1,0:T(8,128)S(1)} %get-tuple-element.22), channel_id=1, replica_groups=mesh['ctx'=64,'head'=12] {'head'}, dimensions={0} | all-to-all | bytes 98304 | tf_op jit(solution)/shard_map/all_to_all | solution.py:314
  58.0 1.3 %shard_map.140 = (bf16[512,128]{1,0:T(8,128)(2,1)S(1)}, bf16[8,128,128]{2,1,0:T(8,128)(2,1)}) custom-call(f32[12,8,128]{2,1,0:T(8,128)S(1)} %all_to_all.26.sums_ref, f32[512,128]{1,0:T(8,128)S(1)} %get-tuple-element.23.lin_ref, bf16[512,128]{1,0:T(8,128)(2,1)S(1)} %copy-done.5, f32[1,128]{1,0:T(1,128)S(1)} %bitcast.5, bf16[512,128]{1,0:T(8,128)(2,1)S(1)} %copy-done), custom_call_target="tpu_custom_call" | custom-call | flops 16777216 | bytes 1048576 | tf_op jit(solution)/shard_map/pallas_call | solution.py:316
  59.3 7.6 %all-to-all-start.3 = ((bf16[8,128,128]{2,1,0:T(8,128)(2,1)}), bf16[8,128,128]{2,1,0:T(8,128)(2,1)S(1)}, u32[]{:S(2)}, u32[]{:S(2)}) async-start(bf16[8,128,128]{2,1,0:T(8,128)(2,1)} %get-tuple-element.27), calls=%async_computation.3 | async-start | bytes 524288 | tf_op jit(solution)/shard_map/all_to_all | solution.py:274
  67.0 3.5 %collective-permute-start = (bf16[1024,128]{1,0:T(8,128)(2,1)S(1)}, bf16[1024,128]{1,0:T(8,128)(2,1)S(1)}, u32[]{:S(2)}, u32[]{:S(2)}) collective-permute-start(bf16[1024,128]{1,0:T(8,128)(2,1)S(1)} %pad_maximum_fusion), channel_id=1, source_target_pairs={{0,12},{12,24},{24,36},{36,48},{48,60},{60,72},{72,84},{84,96},{96... | collective-permute-start | bytes 786440 | tf_op jit(solution)/shard_map/ppermute | solution.py:286
  70.5 2.9 %all-to-all-done.3.parts_ref = bf16[8,128,128]{2,1,0:T(8,128)(2,1)S(1)} async-done(((bf16[8,128,128]{2,1,0:T(8,128)(2,1)}), bf16[8,128,128]{2,1,0:T(8,128)(2,1)S(1)}, u32[]{:S(2)}, u32[]{:S(2)}) %all-to-all-start.3) | async-done | bytes 262176 | tf_op jit(solution)/shard_map/all_to_all | solution.py:274
  73.4 0.8 shard_map.142
  74.2 3.5 %all-to-all-start.4 = ((bf16[8,128,128]{2,1,0:T(8,128)(2,1)}), bf16[8,128,128]{2,1,0:T(8,128)(2,1)S(1)}, u32[]{:S(2)}, u32[]{:S(2)}) async-start(bf16[8,128,128]{2,1,0:T(8,128)(2,1)} %shard_map.142), calls=%async_computation.4 | async-start | bytes 524288 | tf_op jit(solution)/shard_map/all_to_all | solution.py:277
  77.7 0.0 collective-permute-done.halo_ref
  77.8 3.6 %shard_map.144 = (bf16[512,128]{1,0:T(8,128)(2,1)}, bf16[1024,128]{1,0:T(8,128)(2,1)S(1)}, f32[512,128]{1,0:T(8,128)S(1)}, f32[512,128]{1,0:T(8,128)S(1)}) custom-call(s32[3]{0:T(128)S(1)} %pad_add_fusion.where_ref, bf16[512,128]{1,0:T(8,128)(2,1)S(1)} %copy-done.9, bf16[512,128]{1,0:T(8,128)(2,1)S(1)} %copy-done.6, bf16[512,128]{1,0:T(8,128)(2,1)S(1)} %copy-done.7, ...), custom_call_target="tpu_custom_call" | custom-call | flops 419430400 | bytes 1703936 | tf_op jit(solution)/shard_map/pallas_call | solution.py:297
  81.3 2.9 %collective-permute-start.1 = (bf16[1024,128]{1,0:T(8,128)(2,1)S(1)}, bf16[1024,128]{1,0:T(8,128)(2,1)S(1)}, u32[]{:S(2)}, u32[]{:S(2)}) collective-permute-start(bf16[1024,128]{1,0:T(8,128)(2,1)S(1)} %get-tuple-element.35), channel_id=1, source_target_pairs={{12,0},{24,12},{36,24},{48,36},{60,48},{72,60},{84,72},{96,84},{10... | collective-permute-start | bytes 786440 | tf_op jit(solution)/shard_map/ppermute | solution.py:286
  84.3 5.0 %collective-permute-done.1.back_ref = bf16[1024,128]{1,0:T(8,128)(2,1)S(1)} collective-permute-done((bf16[1024,128]{1,0:T(8,128)(2,1)S(1)}, bf16[1024,128]{1,0:T(8,128)(2,1)S(1)}, u32[]{:S(2)}, u32[]{:S(2)}) %collective-permute-start.1) | collective-permute-done | bytes 262176 | tf_op jit(solution)/shard_map/ppermute | solution.py:286
  89.3 0.7 shard_map.145
  90.0 2.2 %shard_map.141 = (bf16[512,128]{1,0:T(8,128)(2,1)}, f32[512,128]{1,0:T(8,128)S(1)}, f32[512,128]{1,0:T(8,128)S(1)}) custom-call(bf16[512,128]{1,0:T(8,128)(2,1)S(1)} %get-tuple-element.24.grad_ref, bf16[512,128]{1,0:T(8,128)(2,1)S(1)} %copy-done, bf16[512,128]{1,0:T(8,128)(2,1)S(1)} %copy-done.2, bf16[512,128]{1,0:T(8,128)(2,1)S(1)} %copy-done.4, ...), custom_call_target="tpu_custom_call" | custom-call | flops 234881024 | bytes 1310720 | tf_op jit(solution)/shard_map/pallas_call | solution.py:323
  92.2 0.0 all-to-all-done.4.rows_ref
  92.2 1.6 %shard_map.143 = (bf16[512,128]{1,0:T(8,128)(2,1)}, bf16[512,128]{1,0:T(8,128)(2,1)}) custom-call(s32[3]{0:T(128)S(1)} %pad_add_fusion.where_ref, bf16[8,128,128]{2,1,0:T(8,128)(2,1)S(1)} %all-to-all-done.4.rows_ref, bf16[8,128,128]{2,1,0:T(8,128)(2,1)S(1)} %all-to-all-done.3.parts_ref, f32[512,128]{1,0:T(8,128)S(1)} %get-tuple-element.28.gk_part_ref, ...), custom_call_target="tpu_custom_call" | custom-call | flops 67108864 | bytes 1048576 | tf_op jit(solution)/shard_map/pallas_call | solution.py:330
  (14 shorter events, 0.0 us)
Async XLA Ops:
  0.6 0.9 copy-start.1
  1.5 0.9 copy-start.3
  22.9 3.6 %copy-start = (bf16[512,128]{1,0:T(8,128)(2,1)S(1)}, bf16[512,128]{1,0:T(8,128)(2,1)}, u32[]{:S(2)}) copy-start(bf16[512,128]{1,0:T(8,128)(2,1)} %query_ref.8) | copy-start | bytes 393220
  22.9 3.6 %copy-start.2 = (bf16[512,128]{1,0:T(8,128)(2,1)S(1)}, bf16[512,128]{1,0:T(8,128)(2,1)}, u32[]{:S(2)}) copy-start(bf16[512,128]{1,0:T(8,128)(2,1)} %key_ref.8) | copy-start | bytes 393220
  22.9 3.6 %copy-start.4 = (bf16[512,128]{1,0:T(8,128)(2,1)S(1)}, bf16[512,128]{1,0:T(8,128)(2,1)}, u32[]{:S(2)}) copy-start(bf16[512,128]{1,0:T(8,128)(2,1)} %value_ref.8) | copy-start | bytes 393220
  22.9 13.6 %all-to-all-start.1 = ((bf16[8,128,128]{2,1,0:T(8,128)(2,1)}), bf16[8,128,128]{2,1,0:T(8,128)(2,1)S(1)}, u32[]{:S(2)}, u32[]{:S(2)}) async-start(bf16[8,128,128]{2,1,0:T(8,128)(2,1)} %shard_map.137), calls=%async_computation.1 | async-start | bytes 524288 | tf_op jit(solution)/shard_map/all_to_all | solution.py:277
  26.5 10.0 %copy-start.5 = (bf16[512,128]{1,0:T(8,128)(2,1)S(1)}, bf16[512,128]{1,0:T(8,128)(2,1)}, u32[]{:S(2)}) copy-start(bf16[512,128]{1,0:T(8,128)(2,1)} %grad_ref.4) | copy-start | bytes 393220
  27.4 9.1 %copy-start.8 = (f32[128]{0:T(128)S(1)}, f32[128]{0:T(128)}, u32[]{:S(2)}) copy-start(f32[128]{0:T(128)} %param.12) | copy-start | bytes 1540
  59.3 7.6 %copy-start.6 = (bf16[512,128]{1,0:T(8,128)(2,1)S(1)}, bf16[512,128]{1,0:T(8,128)(2,1)}, u32[]{:S(2)}) copy-start(bf16[512,128]{1,0:T(8,128)(2,1)} %key_ref.9) | copy-start | bytes 393220
  59.3 7.6 %copy-start.7 = (bf16[512,128]{1,0:T(8,128)(2,1)S(1)}, bf16[512,128]{1,0:T(8,128)(2,1)}, u32[]{:S(2)}) copy-start(bf16[512,128]{1,0:T(8,128)(2,1)} %value_ref.9) | copy-start | bytes 393220
  59.3 14.1 %all-to-all-start.3 = ((bf16[8,128,128]{2,1,0:T(8,128)(2,1)}), bf16[8,128,128]{2,1,0:T(8,128)(2,1)S(1)}, u32[]{:S(2)}, u32[]{:S(2)}) async-start(bf16[8,128,128]{2,1,0:T(8,128)(2,1)} %get-tuple-element.27), calls=%async_computation.3 | async-start | bytes 524288 | tf_op jit(solution)/shard_map/all_to_all | solution.py:274
  67.0 10.8 %collective-permute-start = (bf16[1024,128]{1,0:T(8,128)(2,1)S(1)}, bf16[1024,128]{1,0:T(8,128)(2,1)S(1)}, u32[]{:S(2)}, u32[]{:S(2)}) collective-permute-start(bf16[1024,128]{1,0:T(8,128)(2,1)S(1)} %pad_maximum_fusion), channel_id=1, source_target_pairs={{0,12},{12,24},{24,36},{36,48},{48,60},{60,72},{72,84},{84,96},{96... | collective-permute-start | bytes 786440 | tf_op jit(solution)/shard_map/ppermute | solution.py:286
  74.2 3.6 %copy-start.9 = (bf16[512,128]{1,0:T(8,128)(2,1)S(1)}, bf16[512,128]{1,0:T(8,128)(2,1)}, u32[]{:S(2)}) copy-start(bf16[512,128]{1,0:T(8,128)(2,1)} %query_ref.9) | copy-start | bytes 393220
  74.2 3.6 %copy-start.10 = (bf16[512,128]{1,0:T(8,128)(2,1)S(1)}, bf16[512,128]{1,0:T(8,128)(2,1)}, u32[]{:S(2)}) copy-start(bf16[512,128]{1,0:T(8,128)(2,1)} %grad_ref.5) | copy-start | bytes 393220
  74.2 18.0 %all-to-all-start.4 = ((bf16[8,128,128]{2,1,0:T(8,128)(2,1)}), bf16[8,128,128]{2,1,0:T(8,128)(2,1)S(1)}, u32[]{:S(2)}, u32[]{:S(2)}) async-start(bf16[8,128,128]{2,1,0:T(8,128)(2,1)} %shard_map.142), calls=%async_computation.4 | async-start | bytes 524288 | tf_op jit(solution)/shard_map/all_to_all | solution.py:277
  81.3 8.0 %collective-permute-start.1 = (bf16[1024,128]{1,0:T(8,128)(2,1)S(1)}, bf16[1024,128]{1,0:T(8,128)(2,1)S(1)}, u32[]{:S(2)}, u32[]{:S(2)}) collective-permute-start(bf16[1024,128]{1,0:T(8,128)(2,1)S(1)} %get-tuple-element.35), channel_id=1, source_target_pairs={{12,0},{24,12},{36,24},{48,36},{60,48},{72,60},{84,72},{96,84},{10... | collective-permute-start | bytes 786440 | tf_op jit(solution)/shard_map/ppermute | solution.py:286

commit v2 on v1

v2 whole, which is shorter than its diff:
```python
import functools
import math

import jax
import jax.numpy as jnp
from jax import lax
from jax.experimental import pallas as pl
from jax.experimental.pallas import tpu as pltpu
from jax.sharding import PartitionSpec as P

DH = 128
WINDOW = 512
TILE = 128
ROW = 8
NORM_EPS = 1e-06
HIDDEN = -1e30
LONG = 4e9

f32 = jnp.float32
bf16 = jnp.bfloat16


def dot(left, right, dims):
    return lax.dot_general(left, right, (dims, ((), ())), preferred_element_type=f32)


def dot_nn(left, right):
    return dot(left, right, ((1,), (0,)))


def dot_nt(left, right):
    return dot(left, right, ((1,), (1,)))


def dot_tn(left, right):
    return dot(left, right, ((0,), (0,)))


def halves(value):
    high = value.astype(bf16)
    return high, (value - high.astype(f32)).astype(bf16)


def kernel_call(
    body, outs, flops, moved, exps=0, scratch=(), limit=12, specs=None, out_specs=None, ahead=0
):
    def run(*refs):
        inputs = len(specs)
        body(*refs[: inputs - ahead], *refs[inputs:])

    return pl.pallas_call(
        run if ahead else body,
        name=getattr(body, "func", body).__name__,
        out_shape=outs,
        scratch_shapes=list(scratch),
        compiler_params=pltpu.CompilerParams(vmem_limit_bytes=limit << 20),
        cost_estimate=pl.CostEstimate(
            flops=int(flops), bytes_accessed=int(moved), transcendentals=int(exps)
        ),
        **({"in_specs": specs} if specs else {}),
        **({"out_specs": out_specs} if out_specs else {}),
    )


def shaped(shape, dtype):
    return jax.ShapeDtypeStruct(shape, dtype)


def diagonal_tiles():
    rows = lax.broadcasted_iota(jnp.int32, (TILE, TILE), 0)
    cols = lax.broadcasted_iota(jnp.int32, (TILE, TILE), 1)
    return rows <= cols, rows >= cols


def state_body(key_hbm, value_hbm, out_ref, done_ref, key_ref, value_ref, arrived):
    copies = []
    for start in range(0, key_ref.shape[0], TILE):
        here = pl.ds(start, TILE)
        for far, local_ref in ((key_hbm, key_ref), (value_hbm, value_ref)):
            copy = pltpu.make_async_copy(far.at[here], local_ref.at[here], arrived.at[len(copies)])
            copy.start()
            copies.append(copy)
    for copy in copies:
        copy.wait()
    state = dot_tn(key_ref[...], value_ref[...]).astype(bf16)
    for place in range(out_ref.shape[0]):
        out_ref[place] = state
    done_ref[...] = jnp.zeros_like(done_ref)


def spread(value, near, far, sent):
    near[...] = value
    copies = [
        pltpu.make_async_copy(near, far.at[place], sent.at[place]) for place in range(far.shape[0])
    ]
    for copy in copies:
        copy.start()
    return copies


def total_body(parts_ref, out_hbm, near, sent):
    total = parts_ref[0].astype(f32)
    for place in range(1, parts_ref.shape[0]):
        total = total + parts_ref[place].astype(f32)
    for copy in spread(total.astype(bf16), near, out_hbm, sent):
        copy.wait()


def pack_body(key_ref, value_ref, out_ref):
    span = key_ref.shape[0]
    out_ref[:span] = key_ref[...]
    out_ref[span:] = value_ref[...]


def chosen_sum(where_ref, rows_ref, parts_ref, later):
    row, col = where_ref[0], where_ref[1]
    total = None
    for ref, mine in ((rows_ref, row), (parts_ref, col)):
        for place in range(ref.shape[0]):
            wanted = place > mine if later else place < mine
            term = jnp.where(wanted, ref[place].astype(f32), 0.0)
            total = term if total is None else total + term
    return total


def inner_body(query_ref, key_ref, value_ref, grad_ref, gain_ref, out_ref, scaled_ref):
    tokens = query_ref.shape[0]
    _, lower = diagonal_tiles()
    for start in range(0, tokens, TILE):
        stop = start + TILE
        query = query_ref[start:stop]
        scores = dot_nt(query, key_ref[start:stop])
        probs = jnp.where(lower, scores, 0.0).astype(bf16)
        result = dot_nn(probs, value_ref[start:stop])
        if start:
            probs = dot_nt(query, key_ref[:start]).astype(bf16)
            result = result + dot_nn(probs, value_ref[:start])
        out_ref[start:stop] = result
    scaled_ref[...] = grad_ref[...].astype(f32) * gain_ref[...]


def normed_body(
    where_ref, rows_ref, parts_ref, inner_ref, query_ref, scaled_ref,
    lin_ref, prior_ref, sums_hbm, near, sent,
):
    prior = chosen_sum(where_ref, rows_ref, parts_ref, False)
    prior_ref[...] = prior
    high, low = halves(prior)
    squares, crosses = [], []
    for start in range(0, query_ref.shape[0], TILE):
        here = slice(start, start + TILE)
        query = query_ref[here]
        lin_out = inner_ref[here] + dot_nn(query, high) + dot_nn(query, low)
        lin_ref[here] = lin_out
        for terms, pieces in ((lin_out, squares), (scaled_ref[here], crosses)):
            turned = jnp.transpose(terms * lin_out)
            pieces.append(jnp.sum(turned, axis=0, keepdims=True))
    for copy in spread(jnp.concatenate(squares + crosses, 0), near, sums_hbm, sent):
        copy.wait()


def grad_out_body(
    sums_ref, lin_ref, scaled_ref, query_ref, out_ref, state_ref, *, width
):
    total = sums_ref[0]
    for place in range(1, sums_ref.shape[0]):
        total = total + sums_ref[place]
    groups = total.shape[0] // 2
    inverse = 1.0 / jnp.sqrt(total[:groups] / width + NORM_EPS)
    weight = total[groups:] * inverse * inverse * inverse / width
    turned = jnp.transpose(jnp.concatenate([inverse, weight], 0))
    for group in range(groups):
        tokens = slice(group * TILE, (group + 1) * TILE)
        grad_out = (
            scaled_ref[tokens] * turned[:, group : group + 1]
            - lin_ref[tokens] * turned[:, groups + group : groups + group + 1]
        )
        out_ref[tokens] = grad_out.astype(bf16)
    state = dot_tn(query_ref[...], out_ref[...]).astype(bf16)
    for place in range(state_ref.shape[0]):
        state_ref[place] = state


def probs_body(query_ref, key_ref, value_ref, out_ref, kept_ref):
    tokens = query_ref.shape[0]
    upper, _ = diagonal_tiles()
    for start in range(0, tokens, TILE):
        stop = start + TILE
        here = slice(start, stop)
        key = key_ref[here]
        out_ref[here, here] = jnp.where(upper, dot_nt(key, query_ref[here]), 0.0).astype(bf16)
        if stop < tokens:
            out_ref[here, stop:] = dot_nt(key, query_ref[stop:]).astype(bf16)
    kept_ref[:tokens] = key_ref[...]
    kept_ref[tokens:] = value_ref[...]


def mixed_body(
    grad_ref, query_ref, kept_ref, probs_ref, prior_ref, gq_ref, gk_ref, gv_ref,
):
    tokens = query_ref.shape[0]
    upper, lower = diagonal_tiles()
    high, low = halves(prior_ref[...])
    for start in range(0, tokens, TILE):
        stop = start + TILE
        here = slice(start, stop)
        grad, query = grad_ref[here], query_ref[here]
        key, value = kept_ref[here], kept_ref[tokens + start : tokens + stop]
        mix = jnp.where(lower, dot_nt(grad, value), 0.0).astype(bf16)
        result = dot_nn(mix, key) + dot_nt(grad, high) + dot_nt(grad, low)
        if start:
            mix = dot_nt(grad, kept_ref[tokens : tokens + start]).astype(bf16)
            result = result + dot_nn(mix, kept_ref[:start])
        gq_ref[here] = result.astype(bf16)
        mix = jnp.where(upper, dot_nt(value, grad), 0.0).astype(bf16)
        key_part = dot_nn(mix, query)
        if stop < tokens:
            mix = dot_nt(value, grad_ref[stop:]).astype(bf16)
            key_part = key_part + dot_nn(mix, query_ref[stop:])
        gk_ref[here] = key_part
        gv_ref[here] = dot_nn(probs_ref[here, start:], grad_ref[start:])


def closing_body(
    where_ref, rows_ref, parts_ref, gk_part_ref, gv_part_ref, kept_ref,
    gk_hbm, gv_hbm, gk_ref, gv_ref, sent,
):
    high, low = halves(chosen_sum(where_ref, rows_ref, parts_ref, True))
    copies = []
    tokens = gk_ref.shape[0]
    for start in range(0, tokens, 2 * TILE):
        here = pl.ds(start, 2 * TILE)
        key, value = kept_ref[here], kept_ref[pl.ds(tokens + start, 2 * TILE)]
        gk_ref[here] = (gk_part_ref[here] + dot_nt(value, high) + dot_nt(value, low)).astype(bf16)
        gv_ref[here] = (gv_part_ref[here] + dot_nn(key, high) + dot_nn(key, low)).astype(bf16)
        for near, far in ((gk_ref, gk_hbm), (gv_ref, gv_hbm)):
            copy = pltpu.make_async_copy(near.at[here], far.at[here], sent.at[len(copies)])
            copy.start()
            copies.append(copy)
    for copy in copies:
        copy.wait()


def window_body(
    where_ref, query_ref, key_ref, value_ref, grad_ref, halo_ref,
    back_ref, behind_logit_ref, own_logit_ref, own_win_ref, behind_win_ref,
):
    span = query_ref.shape[0]
    scale = 1.0 / math.sqrt(DH)
    first = where_ref[2] == 0
    upper, _ = diagonal_tiles()
    for start in range(0, span, TILE):
        stop = start + TILE
        here = slice(start, stop)
        query, grad = query_ref[here], grad_ref[here]
        behind = dot_nt(halo_ref[start:span], query)
        edge = jnp.where(upper, HIDDEN, behind[:TILE])
        behind = jnp.concatenate([edge, behind[TILE:]], 0) if stop < span else edge
        behind = jnp.where(first, HIDDEN, behind)
        own = dot_nt(key_ref[:stop], query)
        edge = jnp.where(upper, own[start:], HIDDEN)
        own = jnp.concatenate([own[:start], edge], 0) if start else edge
        peak = jnp.maximum(
            jnp.max(behind, axis=0, keepdims=True), jnp.max(own, axis=0, keepdims=True)
        )
        behind = jnp.exp((behind - peak) * scale)
        own = jnp.exp((own - peak) * scale)
        total = jnp.sum(behind, axis=0, keepdims=True) + jnp.sum(own, axis=0, keepdims=True)
        inverse = 1.0 / total
        behind, own = behind * inverse, own * inverse
        behind_win, own_win = behind.astype(bf16), own.astype(bf16)
        behind_grad = dot_nt(halo_ref[span + start :], grad)
        own_grad = dot_nt(value_ref[:stop], grad)
        delta = jnp.sum(behind_win.astype(f32) * behind_grad, axis=0, keepdims=True) + jnp.sum(
            own_win.astype(f32) * own_grad, axis=0, keepdims=True
        )
        behind_win_ref[start:, here] = behind_win
        own_win_ref[:stop, here] = own_win
        behind_logit_ref[start:, here] = (behind * (behind_grad - delta)).astype(bf16)
        own_logit_ref[:stop, here] = (own * (own_grad - delta)).astype(bf16)
    for start in range(0, span, TILE):
        stop = start + TILE
        here = slice(start, stop)
        back = dot_nn(behind_logit_ref[here, :stop], query_ref[:stop]) * scale
        back_ref[here] = back.astype(bf16)
        back = dot_nn(behind_win_ref[here, :stop], grad_ref[:stop])
        back_ref[span + start : span + stop] = back.astype(bf16)


def own_body(
    behind_logit_ref, own_logit_ref, own_win_ref, halo_ref, query_ref, key_ref, grad_ref,
    gq_ref, gk_ref, gv_ref,
):
    span = query_ref.shape[0]
    scale = 1.0 / math.sqrt(DH)
    for start in range(0, span, TILE):
        stop = start + TILE
        here = slice(start, stop)
        result = dot_tn(halo_ref[start:span], behind_logit_ref[start:, here])
        result = result + dot_tn(key_ref[:stop], own_logit_ref[:stop, here])
        gq_ref[here] = (jnp.transpose(result) * scale).astype(bf16)
        gk_ref[here] = dot_nn(own_logit_ref[here, start:], query_ref[start:]) * scale
        gv_ref[here] = dot_nn(own_win_ref[here, start:], grad_ref[start:])


def settle_body(gk_ref, gv_ref, back_ref, gk_out, gv_out, done_ref):
    span = gk_ref.shape[0]
    gk_out[...] = (gk_ref[...] + back_ref[:span].astype(f32)).astype(bf16)
    gv_out[...] = (gv_ref[...] + back_ref[span:].astype(f32)).astype(bf16)
    done_ref[...] = jnp.zeros_like(done_ref)


def local(
    query_lin, key_lin, value_lin, norm_gain, grad_normed, query_win, key_win, value_win, grad_win
):
    tokens, width = query_lin.shape
    blocks, heads = lax.axis_size("ctx"), lax.axis_size("head")
    rows = blocks // ROW
    my_index = lax.axis_index("ctx")
    where = jnp.stack([my_index // ROW, my_index % ROW, my_index]).astype(jnp.int32)
    row_groups = [[row * ROW + col for col in range(ROW)] for row in range(rows)]
    col_groups = [[row * ROW + col for row in range(rows)] for col in range(ROW)]
    gain = norm_gain.reshape(1, width)
    state = (DH, DH)
    block = (tokens, width)
    macs = tokens * DH * DH
    square = tokens * tokens * DH
    size = tokens * DH * 2
    in_smem = pl.BlockSpec(memory_space=pltpu.SMEM)
    in_vmem = pl.BlockSpec(memory_space=pltpu.VMEM)
    in_hbm = pl.BlockSpec(memory_space=pltpu.HBM)
    anywhere = pl.BlockSpec(memory_space=pl.ANY)
    copies = pltpu.SemaphoreType.DMA((ROW,))
    spreading = (pltpu.VMEM(state, bf16), pltpu.SemaphoreType.DMA((max(rows, ROW),)))

    def along_row(value):
        return lax.all_to_all(value, "ctx", 0, 0, axis_index_groups=row_groups)

    def along_col(value):
        return lax.all_to_all(value, "ctx", 0, 0, axis_index_groups=col_groups)

    def row_total(parts, flops, *ahead):
        return kernel_call(
            total_body,
            shaped((rows,) + state, bf16),
            flops,
            16 * DH * DH * 2,
            scratch=spreading,
            specs=[in_vmem] + [anywhere] * len(ahead),
            out_specs=in_hbm,
            ahead=len(ahead),
        )(parts, *ahead)

    def shift(value, steps):
        first, last = max(0, -steps), min(blocks, blocks - steps)
        return lax.ppermute(value, "ctx", [(at, at + steps) for at in range(first, last)])

    own_state, started = kernel_call(
        state_body,
        (shaped((ROW,) + state, bf16), shaped((8, TILE), f32)),
        2 * macs,
        2 * size + ROW * DH * DH * 2,
        scratch=(pltpu.VMEM(block, bf16), pltpu.VMEM(block, bf16), copies),
        limit=60,
        specs=[in_hbm] * 2,
    )(key_lin, value_lin)
    parts = along_row(own_state)
    row_sum = row_total(parts, LONG / 4)
    halo_pack = kernel_call(
        pack_body,
        shaped((2 * tokens, width), bf16),
        0,
        4 * size,
        specs=[in_vmem] * 2 + [anywhere],
        ahead=1,
    )(key_win, value_win, started)
    halo = shift(halo_pack, 1)
    inner, scaled = kernel_call(
        inner_body,
        (shaped(block, f32), shaped(block, f32)),
        LONG,
        8 * size,
        specs=[in_vmem] * 5 + [anywhere] * 2,
        ahead=2,
    )(query_lin, key_lin, value_lin, grad_normed, gain, row_sum, halo)
    row_parts = along_col(row_sum)
    lin_out, prior, sums = kernel_call(
        normed_body,
        (shaped(block, f32), shaped(state, f32), shaped((heads, 8, TILE), f32)),
        4 * macs,
        8 * size,
        scratch=(pltpu.VMEM((8, TILE), f32), pltpu.SemaphoreType.DMA((heads,))),
        specs=[in_smem] + [in_vmem] * 5 + [anywhere],
        out_specs=(in_vmem, in_vmem, in_hbm),
        ahead=1,
    )(where, row_parts, parts, inner, query_lin, scaled, halo)
    flat = shaped((tokens, tokens), bf16)
    back, behind_logit, own_logit, own_win = kernel_call(
        window_body,
        (shaped((2 * tokens, width), bf16), flat, flat, flat),
        8 * square,
        20 * size,
        tokens * tokens,
        (pltpu.VMEM((tokens, tokens), bf16),),
        16,
        [in_smem] + [in_vmem] * 5 + [anywhere],
        ahead=1,
    )(where, query_win, key_win, value_win, grad_win, halo, sums)
    gq_win, gk_own, gv_own = kernel_call(
        own_body,
        (shaped(block, bf16), shaped(block, f32), shaped(block, f32)),
        5 * square,
        20 * size,
        specs=[in_vmem] * 7,
    )(behind_logit, own_logit, own_win, halo, query_win, key_win, grad_win)
    all_sums = lax.all_to_all(sums, "head", 0, 0)
    returned = shift(back, -1)
    probs, kept = kernel_call(
        probs_body,
        (shaped((tokens, tokens), bf16), shaped((2 * tokens, width), bf16)),
        LONG,
        8 * size,
        specs=[in_vmem] * 3 + [anywhere],
        ahead=1,
    )(query_lin, key_lin, value_lin, sums)
    grad_out, later_state = kernel_call(
        functools.partial(grad_out_body, width=float(width * heads)),
        (shaped(block, bf16), shaped((ROW,) + state, bf16)),
        2 * macs,
        8 * size,
        specs=[in_vmem] * 4 + [anywhere] * 3,
        ahead=3,
    )(all_sums, lin_out, scaled, query_lin, returned, probs, gk_own)
    later_parts = along_row(later_state)
    later_sum = row_total(later_parts, 8 * DH * DH)
    gq_lin, gk_part, gv_part = kernel_call(
        mixed_body,
        (shaped(block, bf16), shaped(block, f32), shaped(block, f32)),
        5 * square,
        10 * size,
        specs=[in_vmem] * 5 + [anywhere],
        ahead=1,
    )(grad_out, query_lin, kept, probs, prior, later_sum)
    later_rows = along_col(later_sum)
    gk_win, gv_win, settled = kernel_call(
        settle_body,
        (shaped(block, bf16), shaped(block, bf16), shaped((8, TILE), f32)),
        tokens * DH,
        8 * size,
        specs=[in_vmem] * 3 + [anywhere],
        ahead=1,
    )(gk_own, gv_own, returned, later_sum)
    gk_lin, gv_lin = kernel_call(
        closing_body,
        (shaped(block, bf16),) * 2,
        8 * macs,
        8 * size,
        scratch=(pltpu.VMEM(block, bf16), pltpu.VMEM(block, bf16), copies),
        specs=[in_smem] + [in_vmem] * 5 + [anywhere],
        out_specs=(in_hbm, in_hbm),
        ahead=1,
    )(where, later_rows, later_parts, gk_part, gv_part, kept, settled)
    return gq_lin, gk_lin, gv_lin, gq_win, gk_win, gv_win


def solution(mesh):
    placed = P("ctx", "head")
    return jax.shard_map(
        local,
        mesh=mesh,
        in_specs=(placed, placed, placed, P("head")) + (placed,) * 5,
        out_specs=(placed,) * 6,
        check_vma=False,
    )
```

time: 94.9 us -> 89.8 us (0.946)
  blocking collectives: 39.9 us -> 11.3 us
  starting transfers between devices: 21.2 us -> 39.7 us
  waiting for transfers between devices: 17.1 us -> 21.9 us
  Pallas kernels: 13 us -> 14.4 us
  local copies, waits for them, and re-layouts: 1.84 us -> 0.67 us
    all_to_all x1 -> x0, blocking collectives: 20.5 us -> none  [local(): all_sums = lax.all_to_all(sums, 'head', 0, 0)]
    all_to_all x0 -> x1, starting transfers between devices: none -> 10.3 us  [local(): all_sums = lax.all_to_all(sums, 'head', 0, 0)]
    all_to_all x1, blocking collectives: 19.4 us -> 11.3 us  [along_row(): return lax.all_to_all(value, 'ctx', 0, 0, axis_index_groups=row_groups)]
    all_to_all x2, waiting for transfers between devices: 9.13 us -> 16.1 us  [along_col(): return lax.all_to_all(value, 'ctx', 0, 0, axis_index_groups=col_groups)]
    all_to_all x1, starting transfers between devices: 7.61 us -> 14 us  [along_row(): return lax.all_to_all(value, 'ctx', 0, 0, axis_index_groups=row_groups)]
    ppermute x2, waiting for transfers between devices: 5.04 us -> 1.8 us  [shift(): lax.ppermute(value, 'ctx', [(at, at + steps) for at in range(first, last)])]
    ppermute x2, starting transfers between devices: 6.47 us -> 8.48 us  [shift(): lax.ppermute(value, 'ctx', [(at, at + steps) for at in range(first, last)])]
    pallas_call x6 -> x9, Pallas kernels: 6.83 us -> 8.62 us  [the longest x1 2.01 us: local(): kernel_call(window_body, (shaped((2 * tokens, width), bf16), flat, flat,...]
  transfers between devices with their start and end apart: 5 -> 6, of which waited for: 3 -> 5; matrix products, arithmetic and copies ran while one was open for 0% -> 0% of each run, Pallas kernels for 9% -> 9%
where the time goes in v2:
time: 89.8 us; the launch traced here: 88.9 us
  starting transfers between devices  39.7 us (44%)
  waiting for transfers between devices  21.9 us (24%)
  Pallas kernels  14.4 us (16%)
  blocking collectives  11.3 us (13%)
    all_to_all x2, waiting for transfers between devices, along_col(): return lax.all_to_all(value, 'ctx', 0, 0, axis_index_groups=col_groups)  16.1 us
    all_to_all x1, starting transfers between devices, along_row(): return lax.all_to_all(value, 'ctx', 0, 0, axis_index_groups=row_groups)  14 us
    all_to_all x1, blocking collectives, along_row(): return lax.all_to_all(value, 'ctx', 0, 0, axis_index_groups=row_groups)  11.3 us
    all_to_all x1, starting transfers between devices, local(): all_sums = lax.all_to_all(sums, 'head', 0, 0)  10.3 us
    ppermute x2, starting transfers between devices, shift(): lax.ppermute(value, 'ctx', [(at, at + steps) for at in range(first, last)])  8.48 us
    all_to_all x2, starting transfers between devices, along_col(): return lax.all_to_all(value, 'ctx', 0, 0, axis_index_groups=col_groups)  6.98 us
    all_to_all x1, waiting for transfers between devices, along_row(): return lax.all_to_all(value, 'ctx', 0, 0, axis_index_groups=row_groups)  2.9 us
    pallas_call x1, Pallas kernels, local(): kernel_call(window_body, (shaped((2 * tokens, width), bf16), flat, flat,...  2.01 us
  transfers between devices with their start and end apart: 6, of which 5 were waited for; matrix products, arithmetic and copies ran while one was open for 0% of the time, Pallas kernels for 9%

profile of v2, /device:TPU:1, one launch (start us, length us, event | category | flops | bytes accessed | tf_op | source)
XLA Modules:
  0.0 88.9 jit_solution(3255607827356065941)
XLA Ops:
  0.6 1.9 %state_body.1 = (bf16[8,128,128]{2,1,0:T(8,128)(2,1)}, f32[8,128]{1,0:T(8,128)}) custom-call(bf16[512,128]{1,0:T(8,128)(2,1)} %refs_1_.8, bf16[512,128]{1,0:T(8,128)(2,1)} %refs_2_.5), custom_call_target="tpu_custom_call" | custom-call | flops 16777216 | bytes 524288 | tf_op jit(solution)/shard_map/state_body/pallas_call | solution.py:358
  2.5 0.0 copy-start.1
  2.5 0.0 copy-start.6
  2.5 0.0 copy-start.7
  2.6 14.0 %all-to-all-start = ((bf16[8,128,128]{2,1,0:T(8,128)(2,1)}), bf16[8,128,128]{2,1,0:T(8,128)(2,1)S(1)}, u32[]{:S(2)}, u32[]{:S(2)}) async-start(bf16[8,128,128]{2,1,0:T(8,128)(2,1)} %get-tuple-element.32), calls=%async_computation | async-start | bytes 524288 | tf_op jit(solution)/shard_map/all_to_all | solution.py:337
  16.6 3.5 %collective-permute-start = (bf16[1024,128]{1,0:T(8,128)(2,1)S(1)}, bf16[1024,128]{1,0:T(8,128)(2,1)S(1)}, u32[]{:S(2)}, u32[]{:S(2)}) collective-permute-start(bf16[1024,128]{1,0:T(8,128)(2,1)S(1)} %pack_body.1), channel_id=1, source_target_pairs={{0,12},{12,24},{24,36},{36,48},{48,60},{60,72},{72,84},{84,96},{96... | collective-permute-start | bytes 786440 | tf_op jit(solution)/shard_map/ppermute | solution.py:356
  20.1 2.9 %all-to-all-done.parts_ref.refs_2_ = bf16[8,128,128]{2,1,0:T(8,128)(2,1)S(1)} async-done(((bf16[8,128,128]{2,1,0:T(8,128)(2,1)}), bf16[8,128,128]{2,1,0:T(8,128)(2,1)S(1)}, u32[]{:S(2)}, u32[]{:S(2)}) %all-to-all-start) | async-done | bytes 262176 | tf_op jit(solution)/shard_map/all_to_all | solution.py:337
  23.0 0.8 total_body.2.refs_5_
  23.9 0.0 copy-start
  23.9 0.0 copy-start.4
  23.9 0.0 copy-start.5
  23.9 3.6 %all-to-all-start.1 = ((bf16[8,128,128]{2,1,0:T(8,128)(2,1)}), bf16[8,128,128]{2,1,0:T(8,128)(2,1)S(1)}, u32[]{:S(2)}, u32[]{:S(2)}) async-start(bf16[8,128,128]{2,1,0:T(8,128)(2,1)} %total_body.2.refs_5_), calls=%async_computation.1 | async-start | bytes 524288 | tf_op jit(solution)/shard_map/all_to_all | solution.py:340
  27.5 0.1 pad_add_fusion.refs_0_
  27.6 0.6 copy-done.9
  28.2 0.8 inner_body.1
  29.0 8.5 %all-to-all-done.1.refs_1_ = bf16[8,128,128]{2,1,0:T(8,128)(2,1)S(1)} async-done(((bf16[8,128,128]{2,1,0:T(8,128)(2,1)}), bf16[8,128,128]{2,1,0:T(8,128)(2,1)S(1)}, u32[]{:S(2)}, u32[]{:S(2)}) %all-to-all-start.1) | async-done | bytes 262176 | tf_op jit(solution)/shard_map/all_to_all | solution.py:340
  37.6 1.8 %normed_body.1 = (f32[512,128]{1,0:T(8,128)S(1)}, f32[128,128]{1,0:T(8,128)S(1)}, f32[12,8,128]{2,1,0:T(8,128)}) custom-call(s32[3]{0:T(128)S(1)} %pad_add_fusion.refs_0_, bf16[8,128,128]{2,1,0:T(8,128)(2,1)S(1)} %all-to-all-done.1.refs_1_, bf16[8,128,128]{2,1,0:T(8,128)(2,1)S(1)} %all-to-all-done.parts_ref.refs_2_, ...), custom_call_target="tpu_custom_call" | custom-call | flops 33554432 | bytes 1048576 | tf_op jit(solution)/shard_map/normed_body/pallas_call | solution.py:387
  39.3 10.3 %all-to-all-start.2 = ((f32[12,8,128]{2,1,0:T(8,128)}), f32[12,8,128]{2,1,0:T(8,128)S(1)}, u32[]{:S(2)}, u32[]{:S(2)}) async-start(f32[12,8,128]{2,1,0:T(8,128)} %get-tuple-element.36.refs_6_.refs_3_), calls=%async_computation.2 | async-start | bytes 98304 | tf_op jit(solution)/shard_map/all_to_all | solution.py:416
  49.6 2.0 %window_body.1 = (bf16[1024,128]{1,0:T(8,128)(2,1)S(1)}, bf16[512,512]{1,0:T(8,128)(2,1)S(1)}, bf16[512,512]{1,0:T(8,128)(2,1)S(1)}, bf16[512,512]{1,0:T(8,128)(2,1)S(1)}) custom-call(s32[3]{0:T(128)S(1)} %pad_add_fusion.refs_0_, bf16[512,128]{1,0:T(8,128)(2,1)S(1)} %copy-done.2, bf16[512,128]{1,0:T(8,128)(2,1)S(1)} %copy-done.1, ...), custom_call_target="tpu_custom_call" | custom-call | flops 268435456 | bytes 2621440 | tf_op jit(solution)/shard_map/window_body/pallas_call | solution.py:398
  51.6 4.9 %collective-permute-start.1 = (bf16[1024,128]{1,0:T(8,128)(2,1)S(1)}, bf16[1024,128]{1,0:T(8,128)(2,1)S(1)}, u32[]{:S(2)}, u32[]{:S(2)}) collective-permute-start(bf16[1024,128]{1,0:T(8,128)(2,1)S(1)} %get-tuple-element.38), channel_id=1, source_target_pairs={{12,0},{24,12},{36,24},{48,36},{60,48},{72,60},{84,72},{96,84},{10... | collective-permute-start | bytes 786440 | tf_op jit(solution)/shard_map/ppermute | solution.py:356
  56.6 0.3 probs_body.1
  56.9 1.3 %own_body.1 = (bf16[512,128]{1,0:T(8,128)(2,1)}, f32[512,128]{1,0:T(8,128)S(1)}, f32[512,128]{1,0:T(8,128)S(1)}) custom-call(bf16[512,512]{1,0:T(8,128)(2,1)S(1)} %get-tuple-element.40.behind_logit_ref, bf16[512,512]{1,0:T(8,128)(2,1)S(1)} %get-tuple-element.41.own_logit_ref, bf16[512,512]{1,0:T(8,128)(2,1)S(1)} %get-tuple-element.42.own_win_ref, ...), custom_call_target="tpu_custom_call" | custom-call | flops 167772160 | bytes 2621440 | tf_op jit(solution)/shard_map/own_body/pallas_call | solution.py:409
  58.1 1.1 %all-to-all-done.2.refs_0_ = f32[12,8,128]{2,1,0:T(8,128)S(1)} async-done(((f32[12,8,128]{2,1,0:T(8,128)}), f32[12,8,128]{2,1,0:T(8,128)S(1)}, u32[]{:S(2)}, u32[]{:S(2)}) %all-to-all-start.2) | async-done | bytes 49184 | tf_op jit(solution)/shard_map/all_to_all | solution.py:416
  59.3 1.8 %collective-permute-done.1.refs_4_.refs_2_ = bf16[1024,128]{1,0:T(8,128)(2,1)S(1)} collective-permute-done((bf16[1024,128]{1,0:T(8,128)(2,1)S(1)}, bf16[1024,128]{1,0:T(8,128)(2,1)S(1)}, u32[]{:S(2)}, u32[]{:S(2)}) %collective-permute-start.1) | collective-permute-done | bytes 262176 | tf_op jit(solution)/shard_map/ppermute | solution.py:356
  61.1 0.6 grad_out_body.1
  61.7 11.3 %all_to_all.25.parts_ref.refs_2_ = bf16[8,128,128]{2,1,0:T(8,128)(2,1)S(1)} all-to-all(bf16[8,128,128]{2,1,0:T(8,128)(2,1)S(1)} %get-tuple-element.47), channel_id=1, replica_groups={{0,12,24,36,48,60,72,84},{96,108,120,132,144,156,168,180},{192,204,216,..., dimensions={0} | all-to-all | bytes 524288 | tf_op jit(solution)/shard_map/all_to_all | solution.py:337
  73.0 0.8 total_body.3.refs_5_.refs_3_
  73.8 3.4 %all-to-all-start.4 = ((bf16[8,128,128]{2,1,0:T(8,128)(2,1)}), bf16[8,128,128]{2,1,0:T(8,128)(2,1)S(1)}, u32[]{:S(2)}, u32[]{:S(2)}) async-start(bf16[8,128,128]{2,1,0:T(8,128)(2,1)} %total_body.3.refs_5_.refs_3_), calls=%async_computation.4 | async-start | bytes 524288 | tf_op jit(solution)/shard_map/all_to_all | solution.py:340
  77.2 0.7 settle_body.1
  77.9 1.8 %mixed_body.1 = (bf16[512,128]{1,0:T(8,128)(2,1)}, f32[512,128]{1,0:T(8,128)S(1)}, f32[512,128]{1,0:T(8,128)S(1)}) custom-call(bf16[512,128]{1,0:T(8,128)(2,1)S(1)} %get-tuple-element.44.refs_0_, bf16[512,128]{1,0:T(8,128)(2,1)S(1)} %copy-done, bf16[1024,128]{1,0:T(8,128)(2,1)S(1)} %get-tuple-element.45.refs_2_.refs_5_, ...), custom_call_target="tpu_custom_call" | custom-call | flops 167772160 | bytes 1310720 | tf_op jit(solution)/shard_map/mixed_body/pallas_call | solution.py:436
  79.8 7.5 %all-to-all-done.4.refs_1_ = bf16[8,128,128]{2,1,0:T(8,128)(2,1)S(1)} async-done(((bf16[8,128,128]{2,1,0:T(8,128)(2,1)}), bf16[8,128,128]{2,1,0:T(8,128)(2,1)S(1)}, u32[]{:S(2)}, u32[]{:S(2)}) %all-to-all-start.4) | async-done | bytes 262176 | tf_op jit(solution)/shard_map/all_to_all | solution.py:340
  87.3 1.6 %closing_body.1 = (bf16[512,128]{1,0:T(8,128)(2,1)}, bf16[512,128]{1,0:T(8,128)(2,1)}) custom-call(s32[3]{0:T(128)S(1)} %pad_add_fusion.refs_0_, bf16[8,128,128]{2,1,0:T(8,128)(2,1)S(1)} %all-to-all-done.4.refs_1_, bf16[8,128,128]{2,1,0:T(8,128)(2,1)S(1)} %all_to_all.25.parts_ref.refs_2_, f32[512,128]{1,0:T(8,128)S(1)} %get-tuple-element.49.refs_3_, ...), custom_call_target="tpu_custom_call" | custom-call | flops 67108864 | bytes 1048576 | tf_op jit(solution)/shard_map/closing_body/pallas_call | solution.py:453
  (15 shorter events, 0.0 us)
Async XLA Ops:
  2.5 14.0 %copy-start.1 = (bf16[512,128]{1,0:T(8,128)(2,1)S(1)}, bf16[512,128]{1,0:T(8,128)(2,1)}, u32[]{:S(2)}) copy-start(bf16[512,128]{1,0:T(8,128)(2,1)} %key_ref.1) | copy-start | bytes 393220
  2.5 14.0 %copy-start.6 = (bf16[512,128]{1,0:T(8,128)(2,1)S(1)}, bf16[512,128]{1,0:T(8,128)(2,1)}, u32[]{:S(2)}) copy-start(bf16[512,128]{1,0:T(8,128)(2,1)} %refs_3_.4) | copy-start | bytes 393220
  2.5 14.0 %copy-start.7 = (f32[8,128]{1,0:T(8,128)S(1)}, f32[8,128]{1,0:T(8,128)}, u32[]{:S(2)}) copy-start(f32[8,128]{1,0:T(8,128)} %get-tuple-element.33.refs_2_) | copy-start | bytes 12292
  2.6 20.5 %all-to-all-start = ((bf16[8,128,128]{2,1,0:T(8,128)(2,1)}), bf16[8,128,128]{2,1,0:T(8,128)(2,1)S(1)}, u32[]{:S(2)}, u32[]{:S(2)}) async-start(bf16[8,128,128]{2,1,0:T(8,128)(2,1)} %get-tuple-element.32), calls=%async_computation | async-start | bytes 524288 | tf_op jit(solution)/shard_map/all_to_all | solution.py:337
  16.6 11.0 %collective-permute-start = (bf16[1024,128]{1,0:T(8,128)(2,1)S(1)}, bf16[1024,128]{1,0:T(8,128)(2,1)S(1)}, u32[]{:S(2)}, u32[]{:S(2)}) collective-permute-start(bf16[1024,128]{1,0:T(8,128)(2,1)S(1)} %pack_body.1), channel_id=1, source_target_pairs={{0,12},{12,24},{24,36},{36,48},{48,60},{60,72},{72,84},{84,96},{96... | collective-permute-start | bytes 786440 | tf_op jit(solution)/shard_map/ppermute | solution.py:356
  23.9 3.7 %copy-start = (bf16[512,128]{1,0:T(8,128)(2,1)S(1)}, bf16[512,128]{1,0:T(8,128)(2,1)}, u32[]{:S(2)}) copy-start(bf16[512,128]{1,0:T(8,128)(2,1)} %refs_1_.9) | copy-start | bytes 393220
  23.9 3.7 %copy-start.4 = (bf16[512,128]{1,0:T(8,128)(2,1)S(1)}, bf16[512,128]{1,0:T(8,128)(2,1)}, u32[]{:S(2)}) copy-start(bf16[512,128]{1,0:T(8,128)(2,1)} %refs_1_.8) | copy-start | bytes 393220
  23.9 3.7 %copy-start.5 = (bf16[512,128]{1,0:T(8,128)(2,1)S(1)}, bf16[512,128]{1,0:T(8,128)(2,1)}, u32[]{:S(2)}) copy-start(bf16[512,128]{1,0:T(8,128)(2,1)} %refs_2_.5) | copy-start | bytes 393220
  23.9 3.7 %copy-start.8 = (bf16[512,128]{1,0:T(8,128)(2,1)S(1)}, bf16[512,128]{1,0:T(8,128)(2,1)}, u32[]{:S(2)}) copy-start(bf16[512,128]{1,0:T(8,128)(2,1)} %refs_3_.3) | copy-start | bytes 393220
  23.9 13.6 %all-to-all-start.1 = ((bf16[8,128,128]{2,1,0:T(8,128)(2,1)}), bf16[8,128,128]{2,1,0:T(8,128)(2,1)S(1)}, u32[]{:S(2)}, u32[]{:S(2)}) async-start(bf16[8,128,128]{2,1,0:T(8,128)(2,1)} %total_body.2.refs_5_), calls=%async_computation.1 | async-start | bytes 524288 | tf_op jit(solution)/shard_map/all_to_all | solution.py:340
  27.6 0.7 copy-start.9
  37.6 12.0 %copy-start.2 = (bf16[512,128]{1,0:T(8,128)(2,1)S(1)}, bf16[512,128]{1,0:T(8,128)(2,1)}, u32[]{:S(2)}) copy-start(bf16[512,128]{1,0:T(8,128)(2,1)} %query_ref.1) | copy-start | bytes 393220
  37.6 12.0 %copy-start.3 = (bf16[512,128]{1,0:T(8,128)(2,1)S(1)}, bf16[512,128]{1,0:T(8,128)(2,1)}, u32[]{:S(2)}) copy-start(bf16[512,128]{1,0:T(8,128)(2,1)} %grad_ref.1) | copy-start | bytes 393220
  39.3 19.9 %all-to-all-start.2 = ((f32[12,8,128]{2,1,0:T(8,128)}), f32[12,8,128]{2,1,0:T(8,128)S(1)}, u32[]{:S(2)}, u32[]{:S(2)}) async-start(f32[12,8,128]{2,1,0:T(8,128)} %get-tuple-element.36.refs_6_.refs_3_), calls=%async_computation.2 | async-start | bytes 98304 | tf_op jit(solution)/shard_map/all_to_all | solution.py:416
  51.6 9.4 %collective-permute-start.1 = (bf16[1024,128]{1,0:T(8,128)(2,1)S(1)}, bf16[1024,128]{1,0:T(8,128)(2,1)S(1)}, u32[]{:S(2)}, u32[]{:S(2)}) collective-permute-start(bf16[1024,128]{1,0:T(8,128)(2,1)S(1)} %get-tuple-element.38), channel_id=1, source_target_pairs={{12,0},{24,12},{36,24},{48,36},{60,48},{72,60},{84,72},{96,84},{10... | collective-permute-start | bytes 786440 | tf_op jit(solution)/shard_map/ppermute | solution.py:356
  73.8 13.5 %all-to-all-start.4 = ((bf16[8,128,128]{2,1,0:T(8,128)(2,1)}), bf16[8,128,128]{2,1,0:T(8,128)(2,1)S(1)}, u32[]{:S(2)}, u32[]{:S(2)}) async-start(bf16[8,128,128]{2,1,0:T(8,128)(2,1)} %total_body.3.refs_5_.refs_3_), calls=%async_computation.4 | async-start | bytes 524288 | tf_op jit(solution)/shard_map/all_to_all | solution.py:340

commit v3 on v2

--- a/solution.py
+++ b/solution.py
@@ -72,20 +72,14 @@
     return rows <= cols, rows >= cols
 
 
-def state_body(key_hbm, value_hbm, out_ref, done_ref, key_ref, value_ref, arrived):
-    copies = []
-    for start in range(0, key_ref.shape[0], TILE):
-        here = pl.ds(start, TILE)
-        for far, local_ref in ((key_hbm, key_ref), (value_hbm, value_ref)):
-            copy = pltpu.make_async_copy(far.at[here], local_ref.at[here], arrived.at[len(copies)])
-            copy.start()
-            copies.append(copy)
-    for copy in copies:
-        copy.wait()
+def warm_body(where_ref, out_ref):
+    out_ref[...] = jnp.zeros_like(out_ref) + where_ref[0].astype(f32)
+
+
+def state_body(key_ref, value_ref, out_ref):
     state = dot_tn(key_ref[...], value_ref[...]).astype(bf16)
     for place in range(out_ref.shape[0]):
         out_ref[place] = state
-    done_ref[...] = jnp.zeros_like(done_ref)
 
 
 def spread(value, near, far, sent):
@@ -355,17 +349,17 @@
         first, last = max(0, -steps), min(blocks, blocks - steps)
         return lax.ppermute(value, "ctx", [(at, at + steps) for at in range(first, last)])
 
-    own_state, started = kernel_call(
+    warm = kernel_call(warm_body, shaped((8, TILE), f32), LONG, 0, specs=[in_smem])(where)
+    own_state = kernel_call(
         state_body,
-        (shaped((ROW,) + state, bf16), shaped((8, TILE), f32)),
+        shaped((ROW,) + state, bf16),
         2 * macs,
         2 * size + ROW * DH * DH * 2,
-        scratch=(pltpu.VMEM(block, bf16), pltpu.VMEM(block, bf16), copies),
-        limit=60,
-        specs=[in_hbm] * 2,
-    )(key_lin, value_lin)
+        specs=[in_vmem] * 2 + [anywhere],
+        ahead=1,
+    )(key_lin, value_lin, warm)
     parts = along_row(own_state)
-    row_sum = row_total(parts, LONG / 4)
+    row_sum = row_total(parts, 8 * DH * DH)
     halo_pack = kernel_call(
         pack_body,
         shaped((2 * tokens, width), bf16),
@@ -373,16 +367,16 @@
         4 * size,
         specs=[in_vmem] * 2 + [anywhere],
         ahead=1,
-    )(key_win, value_win, started)
+    )(key_win, value_win, row_sum)
     halo = shift(halo_pack, 1)
     inner, scaled = kernel_call(
         inner_body,
         (shaped(block, f32), shaped(block, f32)),
-        LONG,
-        8 * size,
-        specs=[in_vmem] * 5 + [anywhere] * 2,
-        ahead=2,
-    )(query_lin, key_lin, value_lin, grad_normed, gain, row_sum, halo)
+        2.5 * square,
+        8 * size,
+        specs=[in_vmem] * 5 + [anywhere],
+        ahead=1,
+    )(query_lin, key_lin, value_lin, grad_normed, gain, row_sum)
     row_parts = along_col(row_sum)
     lin_out, prior, sums = kernel_call(
         normed_body,
@@ -390,10 +384,9 @@
         4 * macs,
         8 * size,
         scratch=(pltpu.VMEM((8, TILE), f32), pltpu.SemaphoreType.DMA((heads,))),
-        specs=[in_smem] + [in_vmem] * 5 + [anywhere],
+        specs=[in_smem] + [in_vmem] * 5,
         out_specs=(in_vmem, in_vmem, in_hbm),
-        ahead=1,
-    )(where, row_parts, parts, inner, query_lin, scaled, halo)
+    )(where, row_parts, parts, inner, query_lin, scaled)
     flat = shaped((tokens, tokens), bf16)
     back, behind_logit, own_logit, own_win = kernel_call(
         window_body,

time: 89.8 us -> 88.7 us (0.988)
  blocking collectives: 11.3 us -> 30.7 us
  starting transfers between devices: 39.7 us -> 26.2 us
  waiting for transfers between devices: 21.9 us -> 16.3 us
  Pallas kernels: 14.4 us -> 13.3 us
    all_to_all x1 -> x2, blocking collectives: 11.3 us -> 30.7 us  [along_row(): return lax.all_to_all(value, 'ctx', 0, 0, axis_index_groups=row_groups)]
    all_to_all x1 -> x0, starting transfers between devices: 14 us -> none  [along_row(): return lax.all_to_all(value, 'ctx', 0, 0, axis_index_groups=row_groups)]
    all_to_all x1 -> x0, waiting for transfers between devices: 2.9 us -> none  [along_row(): return lax.all_to_all(value, 'ctx', 0, 0, axis_index_groups=row_groups)]
    all_to_all x2, waiting for transfers between devices: 16.1 us -> 13.4 us  [along_col(): return lax.all_to_all(value, 'ctx', 0, 0, axis_index_groups=col_groups)]
    pallas_call x2 -> x3, Pallas kernels: 2.67 us -> 1.57 us  [the longest x1 0.8 us: local(): kernel_call(inner_body, (shaped(block, f32), shaped(block, f32)), 2.5 * s...]
  transfers between devices with their start and end apart: 6 -> 5, of which waited for: 5 -> 4; matrix products, arithmetic and copies ran while one was open for 0% -> 0% of each run, Pallas kernels for 9% -> 10%
where the time goes in v3:
time: 88.7 us; the launch traced here: 88 us
  blocking collectives  30.7 us (35%)
  starting transfers between devices  26.2 us (30%)
  waiting for transfers between devices  16.3 us (18%)
  Pallas kernels  13.3 us (15%)
    all_to_all x2, blocking collectives, along_row(): return lax.all_to_all(value, 'ctx', 0, 0, axis_index_groups=row_groups)  30.7 us
    all_to_all x2, waiting for transfers between devices, along_col(): return lax.all_to_all(value, 'ctx', 0, 0, axis_index_groups=col_groups)  13.4 us
    all_to_all x1, starting transfers between devices, local(): all_sums = lax.all_to_all(sums, 'head', 0, 0)  11 us
    ppermute x2, starting transfers between devices, shift(): lax.ppermute(value, 'ctx', [(at, at + steps) for at in range(first, last)])  8.2 us
    all_to_all x2, starting transfers between devices, along_col(): return lax.all_to_all(value, 'ctx', 0, 0, axis_index_groups=col_groups)  6.98 us
    pallas_call x1, Pallas kernels, local(): kernel_call(window_body, (shaped((2 * tokens, width), bf16), flat, flat,...  1.99 us
    pallas_call x1, Pallas kernels, local(): kernel_call(mixed_body, (shaped(block, bf16), shaped(block, f32), shaped(...  1.82 us
    ppermute x2, waiting for transfers between devices, shift(): lax.ppermute(value, 'ctx', [(at, at + steps) for at in range(first, last)])  1.78 us
  transfers between devices with their start and end apart: 5, of which 4 were waited for; matrix products, arithmetic and copies ran while one was open for 0% of the time, Pallas kernels for 10%

profile of v3, /device:TPU:1, one launch (start us, length us, event | category | flops | bytes accessed | tf_op | source)
XLA Modules:
  0.0 88.0 jit_solution(12432960091016739327)
XLA Ops:
  0.7 0.1 pad_add_fusion.where_ref.refs_0_
  0.7 0.5 warm_body.1.refs_2_
  1.3 0.3 copy-done.2
  1.6 0.1 copy-done.3
  1.7 0.2 state_body.1
  1.9 19.4 %all_to_all.25.parts_ref = bf16[8,128,128]{2,1,0:T(8,128)(2,1)S(1)} all-to-all(bf16[8,128,128]{2,1,0:T(8,128)(2,1)S(1)} %state_body.1), channel_id=1, replica_groups={{0,12,24,36,48,60,72,84},{96,108,120,132,144,156,168,180},{192,204,216,..., dimensions={0} | all-to-all | bytes 524288 | tf_op jit(solution)/shard_map/all_to_all | solution.py:331
  21.4 0.8 total_body.2.refs_5_.refs_2_
  22.2 0.0 copy-start.1
  22.2 0.0 copy-start.7
  22.2 3.6 %all-to-all-start.1 = ((bf16[8,128,128]{2,1,0:T(8,128)(2,1)}), bf16[8,128,128]{2,1,0:T(8,128)(2,1)S(1)}, u32[]{:S(2)}, u32[]{:S(2)}) async-start(bf16[8,128,128]{2,1,0:T(8,128)(2,1)} %total_body.2.refs_5_.refs_2_), calls=%async_computation.1 | async-start | bytes 524288 | tf_op jit(solution)/shard_map/all_to_all | solution.py:334
  25.8 0.0 copy-start
  25.8 0.0 copy-start.6
  25.8 0.0 copy-start.8
  25.8 3.3 %collective-permute-start = (bf16[1024,128]{1,0:T(8,128)(2,1)S(1)}, bf16[1024,128]{1,0:T(8,128)(2,1)S(1)}, u32[]{:S(2)}, u32[]{:S(2)}) collective-permute-start(bf16[1024,128]{1,0:T(8,128)(2,1)S(1)} %pack_body.1), channel_id=1, source_target_pairs={{0,12},{12,24},{24,36},{36,48},{48,60},{60,72},{72,84},{84,96},{96... | collective-permute-start | bytes 786440 | tf_op jit(solution)/shard_map/ppermute | solution.py:350
  29.1 0.8 inner_body.1
  29.9 5.9 %all-to-all-done.1.rows_ref = bf16[8,128,128]{2,1,0:T(8,128)(2,1)S(1)} async-done(((bf16[8,128,128]{2,1,0:T(8,128)(2,1)}), bf16[8,128,128]{2,1,0:T(8,128)(2,1)S(1)}, u32[]{:S(2)}, u32[]{:S(2)}) %all-to-all-start.1) | async-done | bytes 262176 | tf_op jit(solution)/shard_map/all_to_all | solution.py:334
  35.8 1.8 %normed_body.1 = (f32[512,128]{1,0:T(8,128)S(1)}, f32[128,128]{1,0:T(8,128)S(1)}, f32[12,8,128]{2,1,0:T(8,128)}) custom-call(s32[3]{0:T(128)S(1)} %pad_add_fusion.where_ref.refs_0_, bf16[8,128,128]{2,1,0:T(8,128)(2,1)S(1)} %all-to-all-done.1.rows_ref, bf16[8,128,128]{2,1,0:T(8,128)(2,1)S(1)} %all_to_all.25.parts_ref, ...), custom_call_target="tpu_custom_call" | custom-call | flops 33554432 | bytes 1048576 | tf_op jit(solution)/shard_map/normed_body/pallas_call | solution.py:381
  37.6 11.0 %all-to-all-start.2 = ((f32[12,8,128]{2,1,0:T(8,128)}), f32[12,8,128]{2,1,0:T(8,128)S(1)}, u32[]{:S(2)}, u32[]{:S(2)}) async-start(f32[12,8,128]{2,1,0:T(8,128)} %get-tuple-element.32.refs_6_.refs_3_), calls=%async_computation.2 | async-start | bytes 98304 | tf_op jit(solution)/shard_map/all_to_all | solution.py:409
  48.6 2.0 %window_body.1 = (bf16[1024,128]{1,0:T(8,128)(2,1)S(1)}, bf16[512,512]{1,0:T(8,128)(2,1)S(1)}, bf16[512,512]{1,0:T(8,128)(2,1)S(1)}, bf16[512,512]{1,0:T(8,128)(2,1)S(1)}) custom-call(s32[3]{0:T(128)S(1)} %pad_add_fusion.where_ref.refs_0_, bf16[512,128]{1,0:T(8,128)(2,1)S(1)} %copy-done.4, bf16[512,128]{1,0:T(8,128)(2,1)S(1)} %copy-done.1, ...), custom_call_target="tpu_custom_call" | custom-call | flops 268435456 | bytes 2621440 | tf_op jit(solution)/shard_map/window_body/pallas_call | solution.py:391
  50.6 4.9 %collective-permute-start.1 = (bf16[1024,128]{1,0:T(8,128)(2,1)S(1)}, bf16[1024,128]{1,0:T(8,128)(2,1)S(1)}, u32[]{:S(2)}, u32[]{:S(2)}) collective-permute-start(bf16[1024,128]{1,0:T(8,128)(2,1)S(1)} %get-tuple-element.34), channel_id=1, source_target_pairs={{12,0},{24,12},{36,24},{48,36},{60,48},{72,60},{84,72},{96,84},{10... | collective-permute-start | bytes 786440 | tf_op jit(solution)/shard_map/ppermute | solution.py:350
  55.6 0.3 probs_body.1
  55.9 1.3 %own_body.1 = (bf16[512,128]{1,0:T(8,128)(2,1)}, f32[512,128]{1,0:T(8,128)S(1)}, f32[512,128]{1,0:T(8,128)S(1)}) custom-call(bf16[512,512]{1,0:T(8,128)(2,1)S(1)} %get-tuple-element.36.behind_logit_ref, bf16[512,512]{1,0:T(8,128)(2,1)S(1)} %get-tuple-element.37.own_logit_ref, bf16[512,512]{1,0:T(8,128)(2,1)S(1)} %get-tuple-element.38.own_win_ref, ...), custom_call_target="tpu_custom_call" | custom-call | flops 167772160 | bytes 2621440 | tf_op jit(solution)/shard_map/own_body/pallas_call | solution.py:402
  57.2 1.1 %all-to-all-done.2.refs_0_ = f32[12,8,128]{2,1,0:T(8,128)S(1)} async-done(((f32[12,8,128]{2,1,0:T(8,128)}), f32[12,8,128]{2,1,0:T(8,128)S(1)}, u32[]{:S(2)}, u32[]{:S(2)}) %all-to-all-start.2) | async-done | bytes 49184 | tf_op jit(solution)/shard_map/all_to_all | solution.py:409
  58.3 1.8 %collective-permute-done.1.refs_4_.refs_2_ = bf16[1024,128]{1,0:T(8,128)(2,1)S(1)} collective-permute-done((bf16[1024,128]{1,0:T(8,128)(2,1)S(1)}, bf16[1024,128]{1,0:T(8,128)(2,1)S(1)}, u32[]{:S(2)}, u32[]{:S(2)}) %collective-permute-start.1) | collective-permute-done | bytes 262176 | tf_op jit(solution)/shard_map/ppermute | solution.py:350
  60.1 0.6 grad_out_body.1
  60.7 11.3 %all_to_all.26.parts_ref.refs_2_ = bf16[8,128,128]{2,1,0:T(8,128)(2,1)S(1)} all-to-all(bf16[8,128,128]{2,1,0:T(8,128)(2,1)S(1)} %get-tuple-element.43), channel_id=1, replica_groups={{0,12,24,36,48,60,72,84},{96,108,120,132,144,156,168,180},{192,204,216,..., dimensions={0} | all-to-all | bytes 524288 | tf_op jit(solution)/shard_map/all_to_all | solution.py:331
  72.0 0.8 total_body.3.refs_5_.refs_3_
  72.8 3.4 %all-to-all-start.4 = ((bf16[8,128,128]{2,1,0:T(8,128)(2,1)}), bf16[8,128,128]{2,1,0:T(8,128)(2,1)S(1)}, u32[]{:S(2)}, u32[]{:S(2)}) async-start(bf16[8,128,128]{2,1,0:T(8,128)(2,1)} %total_body.3.refs_5_.refs_3_), calls=%async_computation.4 | async-start | bytes 524288 | tf_op jit(solution)/shard_map/all_to_all | solution.py:334
  76.2 0.7 settle_body.1
  77.0 1.8 %mixed_body.1 = (bf16[512,128]{1,0:T(8,128)(2,1)}, f32[512,128]{1,0:T(8,128)S(1)}, f32[512,128]{1,0:T(8,128)S(1)}) custom-call(bf16[512,128]{1,0:T(8,128)(2,1)S(1)} %get-tuple-element.40.refs_0_, bf16[512,128]{1,0:T(8,128)(2,1)S(1)} %copy-done, bf16[1024,128]{1,0:T(8,128)(2,1)S(1)} %get-tuple-element.41.refs_2_.refs_5_, ...), custom_call_target="tpu_custom_call" | custom-call | flops 167772160 | bytes 1310720 | tf_op jit(solution)/shard_map/mixed_body/pallas_call | solution.py:429
  78.8 7.5 %all-to-all-done.4.refs_1_ = bf16[8,128,128]{2,1,0:T(8,128)(2,1)S(1)} async-done(((bf16[8,128,128]{2,1,0:T(8,128)(2,1)}), bf16[8,128,128]{2,1,0:T(8,128)(2,1)S(1)}, u32[]{:S(2)}, u32[]{:S(2)}) %all-to-all-start.4) | async-done | bytes 262176 | tf_op jit(solution)/shard_map/all_to_all | solution.py:334
  86.3 1.6 %closing_body.1 = (bf16[512,128]{1,0:T(8,128)(2,1)}, bf16[512,128]{1,0:T(8,128)(2,1)}) custom-call(s32[3]{0:T(128)S(1)} %pad_add_fusion.where_ref.refs_0_, bf16[8,128,128]{2,1,0:T(8,128)(2,1)S(1)} %all-to-all-done.4.refs_1_, bf16[8,128,128]{2,1,0:T(8,128)(2,1)S(1)} %all_to_all.26.parts_ref.refs_2_, f32[512,128]{1,0:T(8,128)S(1)} %get-tuple-element.45.refs_3_, ...), custom_call_target="tpu_custom_call" | custom-call | flops 67108864 | bytes 1048576 | tf_op jit(solution)/shard_map/closing_body/pallas_call | solution.py:446
  (13 shorter events, 0.0 us)
Async XLA Ops:
  0.7 0.9 %copy-start.2 = (bf16[512,128]{1,0:T(8,128)(2,1)S(1)}, bf16[512,128]{1,0:T(8,128)(2,1)}, u32[]{:S(2)}) copy-start(bf16[512,128]{1,0:T(8,128)(2,1)} %refs_1_.10) | copy-start | bytes 393220
  0.7 1.0 %copy-start.3 = (bf16[512,128]{1,0:T(8,128)(2,1)S(1)}, bf16[512,128]{1,0:T(8,128)(2,1)}, u32[]{:S(2)}) copy-start(bf16[512,128]{1,0:T(8,128)(2,1)} %refs_2_.5) | copy-start | bytes 393220
  22.2 3.6 %copy-start.1 = (bf16[512,128]{1,0:T(8,128)(2,1)S(1)}, bf16[512,128]{1,0:T(8,128)(2,1)}, u32[]{:S(2)}) copy-start(bf16[512,128]{1,0:T(8,128)(2,1)} %key_ref.1) | copy-start | bytes 393220
  22.2 3.6 %copy-start.7 = (bf16[512,128]{1,0:T(8,128)(2,1)S(1)}, bf16[512,128]{1,0:T(8,128)(2,1)}, u32[]{:S(2)}) copy-start(bf16[512,128]{1,0:T(8,128)(2,1)} %refs_3_.4) | copy-start | bytes 393220
  22.2 13.6 %all-to-all-start.1 = ((bf16[8,128,128]{2,1,0:T(8,128)(2,1)}), bf16[8,128,128]{2,1,0:T(8,128)(2,1)S(1)}, u32[]{:S(2)}, u32[]{:S(2)}) async-start(bf16[8,128,128]{2,1,0:T(8,128)(2,1)} %total_body.2.refs_5_.refs_2_), calls=%async_computation.1 | async-start | bytes 524288 | tf_op jit(solution)/shard_map/all_to_all | solution.py:334
  25.8 3.3 %copy-start = (bf16[512,128]{1,0:T(8,128)(2,1)S(1)}, bf16[512,128]{1,0:T(8,128)(2,1)}, u32[]{:S(2)}) copy-start(bf16[512,128]{1,0:T(8,128)(2,1)} %refs_1_.11) | copy-start | bytes 393220
  25.8 3.3 %copy-start.6 = (bf16[512,128]{1,0:T(8,128)(2,1)S(1)}, bf16[512,128]{1,0:T(8,128)(2,1)}, u32[]{:S(2)}) copy-start(bf16[512,128]{1,0:T(8,128)(2,1)} %refs_3_.3) | copy-start | bytes 393220
  25.8 3.3 %copy-start.8 = (f32[128]{0:T(128)S(1)}, f32[128]{0:T(128)}, u32[]{:S(2)}) copy-start(f32[128]{0:T(128)} %param.12) | copy-start | bytes 1540
  25.8 22.8 %collective-permute-start = (bf16[1024,128]{1,0:T(8,128)(2,1)S(1)}, bf16[1024,128]{1,0:T(8,128)(2,1)S(1)}, u32[]{:S(2)}, u32[]{:S(2)}) collective-permute-start(bf16[1024,128]{1,0:T(8,128)(2,1)S(1)} %pack_body.1), channel_id=1, source_target_pairs={{0,12},{12,24},{24,36},{36,48},{48,60},{60,72},{72,84},{84,96},{96... | collective-permute-start | bytes 786440 | tf_op jit(solution)/shard_map/ppermute | solution.py:350
  35.8 12.8 %copy-start.4 = (bf16[512,128]{1,0:T(8,128)(2,1)S(1)}, bf16[512,128]{1,0:T(8,128)(2,1)}, u32[]{:S(2)}) copy-start(bf16[512,128]{1,0:T(8,128)(2,1)} %query_ref.3) | copy-start | bytes 393220
  35.8 12.8 %copy-start.5 = (bf16[512,128]{1,0:T(8,128)(2,1)S(1)}, bf16[512,128]{1,0:T(8,128)(2,1)}, u32[]{:S(2)}) copy-start(bf16[512,128]{1,0:T(8,128)(2,1)} %grad_ref.1) | copy-start | bytes 393220
  37.6 20.7 %all-to-all-start.2 = ((f32[12,8,128]{2,1,0:T(8,128)}), f32[12,8,128]{2,1,0:T(8,128)S(1)}, u32[]{:S(2)}, u32[]{:S(2)}) async-start(f32[12,8,128]{2,1,0:T(8,128)} %get-tuple-element.32.refs_6_.refs_3_), calls=%async_computation.2 | async-start | bytes 98304 | tf_op jit(solution)/shard_map/all_to_all | solution.py:409
  50.6 9.4 %collective-permute-start.1 = (bf16[1024,128]{1,0:T(8,128)(2,1)S(1)}, bf16[1024,128]{1,0:T(8,128)(2,1)S(1)}, u32[]{:S(2)}, u32[]{:S(2)}) collective-permute-start(bf16[1024,128]{1,0:T(8,128)(2,1)S(1)} %get-tuple-element.34), channel_id=1, source_target_pairs={{12,0},{24,12},{36,24},{48,36},{60,48},{72,60},{84,72},{96,84},{10... | collective-permute-start | bytes 786440 | tf_op jit(solution)/shard_map/ppermute | solution.py:350
  72.8 13.5 %all-to-all-start.4 = ((bf16[8,128,128]{2,1,0:T(8,128)(2,1)}), bf16[8,128,128]{2,1,0:T(8,128)(2,1)S(1)}, u32[]{:S(2)}, u32[]{:S(2)}) async-start(bf16[8,128,128]{2,1,0:T(8,128)(2,1)} %total_body.3.refs_5_.refs_3_), calls=%async_computation.4 | async-start | bytes 524288 | tf_op jit(solution)/shard_map/all_to_all | solution.py:334

commit v4 on v3

--- a/solution.py
+++ b/solution.py
@@ -72,8 +72,12 @@
     return rows <= cols, rows >= cols
 
 
-def warm_body(where_ref, out_ref):
-    out_ref[...] = jnp.zeros_like(out_ref) + where_ref[0].astype(f32)
+def chosen_body(where_ref, out_ref):
+    row, col, index = where_ref[0], where_ref[1], where_ref[2]
+    place = lax.broadcasted_iota(jnp.int32, (ROW, TILE), 0)
+    for group, wanted in enumerate((place < row, place < col, place > row, place > col)):
+        out_ref[group * ROW : (group + 1) * ROW] = jnp.where(wanted, 1.0, 0.0)
+    out_ref[4 * ROW :] = jnp.where(place >= index * ROW, 1.0, 0.0)
 
 
 def state_body(key_ref, value_ref, out_ref):
@@ -106,93 +110,83 @@
     out_ref[span:] = value_ref[...]
 
 
-def chosen_sum(where_ref, rows_ref, parts_ref, later):
-    row, col = where_ref[0], where_ref[1]
+def chosen_sum(chosen_ref, rows_ref, parts_ref, later):
     total = None
-    for ref, mine in ((rows_ref, row), (parts_ref, col)):
+    base = 2 * ROW if later else 0
+    for ref, first in ((rows_ref, base), (parts_ref, base + ROW)):
         for place in range(ref.shape[0]):
-            wanted = place > mine if later else place < mine
-            term = jnp.where(wanted, ref[place].astype(f32), 0.0)
+            wanted = chosen_ref[first + place : first + place + 1, :]
+            term = ref[place].astype(f32) * wanted
             total = term if total is None else total + term
     return total
 
 
-def inner_body(query_ref, key_ref, value_ref, grad_ref, gain_ref, out_ref, scaled_ref):
+def inner_body(
+    query_ref, key_ref, value_ref, grad_ref, gain_ref,
+    probs_ref, kept_ref, inner_ref, scaled_ref,
+):
     tokens = query_ref.shape[0]
-    _, lower = diagonal_tiles()
+    kept_ref[:tokens] = key_ref[...]
+    kept_ref[tokens:] = value_ref[...]
+    upper, _ = diagonal_tiles()
     for start in range(0, tokens, TILE):
         stop = start + TILE
-        query = query_ref[start:stop]
-        scores = dot_nt(query, key_ref[start:stop])
-        probs = jnp.where(lower, scores, 0.0).astype(bf16)
-        result = dot_nn(probs, value_ref[start:stop])
+        here = slice(start, stop)
+        query = query_ref[here]
+        edge = jnp.where(upper, dot_nt(key_ref[here], query), 0.0).astype(bf16)
+        probs_ref[here, here] = edge
+        result = dot_tn(value_ref[here], edge)
         if start:
-            probs = dot_nt(query, key_ref[:start]).astype(bf16)
-            result = result + dot_nn(probs, value_ref[:start])
-        out_ref[start:stop] = result
-    scaled_ref[...] = grad_ref[...].astype(f32) * gain_ref[...]
+            probs = dot_nt(key_ref[:start], query).astype(bf16)
+            probs_ref[:start, here] = probs
+            result = result + dot_tn(value_ref[:start], probs)
+        inner_ref[:, here] = result
+        scaled_ref[:, here] = jnp.transpose(grad_ref[here].astype(f32) * gain_ref[...])
 
 
 def normed_body(
-    where_ref, rows_ref, parts_ref, inner_ref, query_ref, scaled_ref,
+    chosen_ref, rows_ref, parts_ref, inner_ref, query_ref, scaled_ref,
     lin_ref, prior_ref, sums_hbm, near, sent,
 ):
-    prior = chosen_sum(where_ref, rows_ref, parts_ref, False)
+    prior = chosen_sum(chosen_ref, rows_ref, parts_ref, False)
     prior_ref[...] = prior
-    high, low = halves(prior)
+    high, low = halves(jnp.transpose(prior))
     squares, crosses = [], []
     for start in range(0, query_ref.shape[0], TILE):
         here = slice(start, start + TILE)
         query = query_ref[here]
-        lin_out = inner_ref[here] + dot_nn(query, high) + dot_nn(query, low)
-        lin_ref[here] = lin_out
-        for terms, pieces in ((lin_out, squares), (scaled_ref[here], crosses)):
-            turned = jnp.transpose(terms * lin_out)
-            pieces.append(jnp.sum(turned, axis=0, keepdims=True))
+        lin_out = inner_ref[:, here] + dot_nt(high, query) + dot_nt(low, query)
+        lin_ref[:, here] = lin_out
+        squares.append(jnp.sum(lin_out * lin_out, axis=0, keepdims=True))
+        crosses.append(jnp.sum(scaled_ref[:, here] * lin_out, axis=0, keepdims=True))
     for copy in spread(jnp.concatenate(squares + crosses, 0), near, sums_hbm, sent):
         copy.wait()
 
 
-def grad_out_body(
-    sums_ref, lin_ref, scaled_ref, query_ref, out_ref, state_ref, *, width
-):
+def grad_out_body(sums_ref, lin_ref, scaled_ref, query_ref, out_ref, state_ref, *, width):
     total = sums_ref[0]
     for place in range(1, sums_ref.shape[0]):
         total = total + sums_ref[place]
     groups = total.shape[0] // 2
     inverse = 1.0 / jnp.sqrt(total[:groups] / width + NORM_EPS)
     weight = total[groups:] * inverse * inverse * inverse / width
-    turned = jnp.transpose(jnp.concatenate([inverse, weight], 0))
     for group in range(groups):
         tokens = slice(group * TILE, (group + 1) * TILE)
-        grad_out = (
-            scaled_ref[tokens] * turned[:, group : group + 1]
-            - lin_ref[tokens] * turned[:, groups + group : groups + group + 1]
-        )
-        out_ref[tokens] = grad_out.astype(bf16)
-    state = dot_tn(query_ref[...], out_ref[...]).astype(bf16)
+        here = slice(group, group + 1)
+        grad_out = scaled_ref[:, tokens] * inverse[here] - lin_ref[:, tokens] * weight[here]
+        out_ref[:, tokens] = grad_out.astype(bf16)
+    state = jnp.transpose(dot_nn(out_ref[...], query_ref[...])).astype(bf16)
     for place in range(state_ref.shape[0]):
         state_ref[place] = state
 
 
-def probs_body(query_ref, key_ref, value_ref, out_ref, kept_ref):
+def mixed_body(
+    turned_ref, query_ref, kept_ref, probs_ref, prior_ref, gq_ref, gk_ref, gv_ref, grad_ref,
+):
     tokens = query_ref.shape[0]
-    upper, _ = diagonal_tiles()
     for start in range(0, tokens, TILE):
-        stop = start + TILE
-        here = slice(start, stop)
-        key = key_ref[here]
-        out_ref[here, here] = jnp.where(upper, dot_nt(key, query_ref[here]), 0.0).astype(bf16)
-        if stop < tokens:
-            out_ref[here, stop:] = dot_nt(key, query_ref[stop:]).astype(bf16)
-    kept_ref[:tokens] = key_ref[...]
-    kept_ref[tokens:] = value_ref[...]
-
-
-def mixed_body(
-    grad_ref, query_ref, kept_ref, probs_ref, prior_ref, gq_ref, gk_ref, gv_ref,
-):
-    tokens = query_ref.shape[0]
+        here = slice(start, start + TILE)
+        grad_ref[here] = jnp.transpose(turned_ref[:, here].astype(f32)).astype(bf16)
     upper, lower = diagonal_tiles()
     high, low = halves(prior_ref[...])
     for start in range(0, tokens, TILE):
@@ -216,10 +210,10 @@
 
 
 def closing_body(
-    where_ref, rows_ref, parts_ref, gk_part_ref, gv_part_ref, kept_ref,
+    chosen_ref, rows_ref, parts_ref, gk_part_ref, gv_part_ref, kept_ref,
     gk_hbm, gv_hbm, gk_ref, gv_ref, sent,
 ):
-    high, low = halves(chosen_sum(where_ref, rows_ref, parts_ref, True))
+    high, low = halves(chosen_sum(chosen_ref, rows_ref, parts_ref, True))
     copies = []
     tokens = gk_ref.shape[0]
     for start in range(0, tokens, 2 * TILE):
@@ -236,12 +230,12 @@
 
 
 def window_body(
-    where_ref, query_ref, key_ref, value_ref, grad_ref, halo_ref,
+    chosen_ref, query_ref, key_ref, value_ref, grad_ref, halo_ref,
     back_ref, behind_logit_ref, own_logit_ref, own_win_ref, behind_win_ref,
 ):
     span = query_ref.shape[0]
     scale = 1.0 / math.sqrt(DH)
-    first = where_ref[2] == 0
+    first = chosen_ref[4 * ROW : 4 * ROW + 1, :] > 0.5
     upper, _ = diagonal_tiles()
     for start in range(0, span, TILE):
         stop = start + TILE
@@ -320,7 +314,6 @@
     macs = tokens * DH * DH
     square = tokens * tokens * DH
     size = tokens * DH * 2
-    in_smem = pl.BlockSpec(memory_space=pltpu.SMEM)
     in_vmem = pl.BlockSpec(memory_space=pltpu.VMEM)
     in_hbm = pl.BlockSpec(memory_space=pltpu.HBM)
     anywhere = pl.BlockSpec(memory_space=pl.ANY)
@@ -349,7 +342,13 @@
         first, last = max(0, -steps), min(blocks, blocks - steps)
         return lax.ppermute(value, "ctx", [(at, at + steps) for at in range(first, last)])
 
-    warm = kernel_call(warm_body, shaped((8, TILE), f32), LONG, 0, specs=[in_smem])(where)
+    chosen = kernel_call(
+        chosen_body,
+        shaped((5 * ROW, TILE), f32),
+        LONG,
+        0,
+        specs=[pl.BlockSpec(memory_space=pltpu.SMEM)],
+    )(where)
     own_state = kernel_call(
         state_body,
         shaped((ROW,) + state, bf16),
@@ -357,7 +356,7 @@
         2 * size + ROW * DH * DH * 2,
         specs=[in_vmem] * 2 + [anywhere],
         ahead=1,
-    )(key_lin, value_lin, warm)
+    )(key_lin, value_lin, chosen)
     parts = along_row(own_state)
     row_sum = row_total(parts, 8 * DH * DH)
     halo_pack = kernel_call(
@@ -369,9 +368,15 @@
         ahead=1,
     )(key_win, value_win, row_sum)
     halo = shift(halo_pack, 1)
-    inner, scaled = kernel_call(
+    turned = (width, tokens)
+    probs, kept, inner, scaled = kernel_call(
         inner_body,
-        (shaped(block, f32), shaped(block, f32)),
+        (
+            shaped((tokens, tokens), bf16),
+            shaped((2 * tokens, width), bf16),
+            shaped(turned, f32),
+            shaped(turned, f32),
+        ),
         2.5 * square,
         8 * size,
         specs=[in_vmem] * 5 + [anywhere],
@@ -380,13 +385,13 @@
     row_parts = along_col(row_sum)
     lin_out, prior, sums = kernel_call(
         normed_body,
-        (shaped(block, f32), shaped(state, f32), shaped((heads, 8, TILE), f32)),
+        (shaped(turned, f32), shaped(state, f32), shaped((heads, 8, TILE), f32)),
         4 * macs,
         8 * size,
         scratch=(pltpu.VMEM((8, TILE), f32), pltpu.SemaphoreType.DMA((heads,))),
-        specs=[in_smem] + [in_vmem] * 5,
+        specs=[in_vmem] + [in_vmem] * 5,
         out_specs=(in_vmem, in_vmem, in_hbm),
-    )(where, row_parts, parts, inner, query_lin, scaled)
+    )(chosen, row_parts, parts, inner, query_lin, scaled)
     flat = shaped((tokens, tokens), bf16)
     back, behind_logit, own_logit, own_win = kernel_call(
         window_body,
@@ -396,34 +401,27 @@
         tokens * tokens,
         (pltpu.VMEM((tokens, tokens), bf16),),
         16,
-        [in_smem] + [in_vmem] * 5 + [anywhere],
-        ahead=1,
-    )(where, query_win, key_win, value_win, grad_win, halo, sums)
+        [in_vmem] + [in_vmem] * 5 + [anywhere],
+        ahead=1,
+    )(chosen, query_win, key_win, value_win, grad_win, halo, sums)
     gq_win, gk_own, gv_own = kernel_call(
         own_body,
         (shaped(block, bf16), shaped(block, f32), shaped(block, f32)),
-        5 * square,
+        LONG,
         20 * size,
-        specs=[in_vmem] * 7,
-    )(behind_logit, own_logit, own_win, halo, query_win, key_win, grad_win)
+        specs=[in_vmem] * 7 + [anywhere],
+        ahead=1,
+    )(behind_logit, own_logit, own_win, halo, query_win, key_win, grad_win, sums)
     all_sums = lax.all_to_all(sums, "head", 0, 0)
     returned = shift(back, -1)
-    probs, kept = kernel_call(
-        probs_body,
-        (shaped((tokens, tokens), bf16), shaped((2 * tokens, width), bf16)),
-        LONG,
-        8 * size,
-        specs=[in_vmem] * 3 + [anywhere],
-        ahead=1,
-    )(query_lin, key_lin, value_lin, sums)
     grad_out, later_state = kernel_call(
         functools.partial(grad_out_body, width=float(width * heads)),
-        (shaped(block, bf16), shaped((ROW,) + state, bf16)),
+        (shaped(turned, bf16), shaped((ROW,) + state, bf16)),
         2 * macs,
         8 * size,
-        specs=[in_vmem] * 4 + [anywhere] * 3,
-        ahead=3,
-    )(all_sums, lin_out, scaled, query_lin, returned, probs, gk_own)
+        specs=[in_vmem] * 4 + [anywhere] * 2,
+        ahead=2,
+    )(all_sums, lin_out, scaled, query_lin, returned, gk_own)
     later_parts = along_row(later_state)
     later_sum = row_total(later_parts, 8 * DH * DH)
     gq_lin, gk_part, gv_part = kernel_call(
@@ -431,6 +429,7 @@
         (shaped(block, bf16), shaped(block, f32), shaped(block, f32)),
         5 * square,
         10 * size,
+        scratch=(pltpu.VMEM(block, bf16),),
         specs=[in_vmem] * 5 + [anywhere],
         ahead=1,
     )(grad_out, query_lin, kept, probs, prior, later_sum)
@@ -449,10 +448,10 @@
         8 * macs,
         8 * size,
         scratch=(pltpu.VMEM(block, bf16), pltpu.VMEM(block, bf16), copies),
-        specs=[in_smem] + [in_vmem] * 5 + [anywhere],
+        specs=[in_vmem] + [in_vmem] * 5 + [anywhere],
         out_specs=(in_hbm, in_hbm),
         ahead=1,
-    )(where, later_rows, later_parts, gk_part, gv_part, kept, settled)
+    )(chosen, later_rows, later_parts, gk_part, gv_part, kept, settled)
     return gq_lin, gk_lin, gv_lin, gq_win, gk_win, gv_win
 
 

time: 88.7 us -> 87.3 us (0.984)
  Pallas kernels: 13.3 us -> 11.3 us
    pallas_call x4 -> x3, Pallas kernels: 3.39 us -> 2.65 us  [the longest x1 1.16 us: local(): kernel_call(normed_body, (shaped(turned, f32), shaped(state, f32), shaped...]
  transfers between devices with their start and end apart: 5 -> 5, of which waited for: 4 -> 4; matrix products, arithmetic and copies ran while one was open for 0% -> 0% of each run, Pallas kernels for 10% -> 9%
where the time goes in v4:
time: 87.3 us; the launch traced here: 86.5 us
  blocking collectives  31.2 us (36%)
  starting transfers between devices  26.1 us (30%)
  waiting for transfers between devices  16.5 us (19%)
  Pallas kernels  11.3 us (13%)
  between operations  0.89 us (1%)
    all_to_all x2, blocking collectives, along_row(): return lax.all_to_all(value, 'ctx', 0, 0, axis_index_groups=row_groups)  31.2 us
    all_to_all x2, waiting for transfers between devices, along_col(): return lax.all_to_all(value, 'ctx', 0, 0, axis_index_groups=col_groups)  13.2 us
    all_to_all x1, starting transfers between devices, local(): all_sums = lax.all_to_all(sums, 'head', 0, 0)  11 us
    ppermute x2, starting transfers between devices, shift(): lax.ppermute(value, 'ctx', [(at, at + steps) for at in range(first, last)])  8.18 us
    all_to_all x2, starting transfers between devices, along_col(): return lax.all_to_all(value, 'ctx', 0, 0, axis_index_groups=col_groups)  6.98 us
    all_to_all x1, waiting for transfers between devices, local(): all_sums = lax.all_to_all(sums, 'head', 0, 0)  1.93 us
    pallas_call x1, Pallas kernels, local(): kernel_call(mixed_body, (shaped(block, bf16), shaped(block, f32), shaped(...  1.86 us
  transfers between devices with their start and end apart: 5, of which 4 were waited for; matrix products, arithmetic and copies ran while one was open for 0% of the time, Pallas kernels for 9%

profile of v4, /device:TPU:1, one launch (start us, length us, event | category | flops | bytes accessed | tf_op | source)
XLA Modules:
  0.0 86.5 jit_solution(16422761789225122060)
XLA Ops:
  0.7 0.1 pad_add_fusion.where_ref
  0.7 0.5 chosen_body.1.refs_2_.chosen_ref.refs_0_
  1.3 0.3 copy-done.1
  1.6 0.1 copy-done.2
  1.7 0.2 state_body.1
  1.9 19.4 %all_to_all.25.parts_ref = bf16[8,128,128]{2,1,0:T(8,128)(2,1)S(1)} all-to-all(bf16[8,128,128]{2,1,0:T(8,128)(2,1)S(1)} %state_body.1), channel_id=1, replica_groups={{0,12,24,36,48,60,72,84},{96,108,120,132,144,156,168,180},{192,204,216,..., dimensions={0} | all-to-all | bytes 524288 | tf_op jit(solution)/shard_map/all_to_all | solution.py:324
  21.4 0.8 total_body.2.refs_5_.refs_2_
  22.2 0.0 copy-start.4
  22.2 0.0 copy-start.5
  22.2 3.6 %all-to-all-start.1 = ((bf16[8,128,128]{2,1,0:T(8,128)(2,1)}), bf16[8,128,128]{2,1,0:T(8,128)(2,1)S(1)}, u32[]{:S(2)}, u32[]{:S(2)}) async-start(bf16[8,128,128]{2,1,0:T(8,128)(2,1)} %total_body.2.refs_5_.refs_2_), calls=%async_computation.1 | async-start | bytes 524288 | tf_op jit(solution)/shard_map/all_to_all | solution.py:327
  25.8 0.0 copy-start
  25.8 0.0 copy-start.3
  25.8 0.0 copy-start.6
  25.8 3.3 %collective-permute-start = (bf16[1024,128]{1,0:T(8,128)(2,1)S(1)}, bf16[1024,128]{1,0:T(8,128)(2,1)S(1)}, u32[]{:S(2)}, u32[]{:S(2)}) collective-permute-start(bf16[1024,128]{1,0:T(8,128)(2,1)S(1)} %pack_body.1), channel_id=1, source_target_pairs={{0,12},{12,24},{24,36},{36,48},{48,60},{60,72},{72,84},{84,96},{96... | collective-permute-start | bytes 786440 | tf_op jit(solution)/shard_map/ppermute | solution.py:343
  29.1 0.9 %inner_body.1 = (bf16[512,512]{1,0:T(8,128)(2,1)S(1)}, bf16[1024,128]{1,0:T(8,128)(2,1)S(1)}, f32[128,512]{1,0:T(8,128)S(1)}, f32[128,512]{1,0:T(8,128)S(1)}) custom-call(bf16[512,128]{1,0:T(8,128)(2,1)S(1)} %copy-done, bf16[512,128]{1,0:T(8,128)(2,1)S(1)} %copy-done.1, bf16[512,128]{1,0:T(8,128)(2,1)S(1)} %copy-done.2, bf16[512,128]{1,0:T(8,128)(2,1)S(1)} %copy-done.3, ...), custom_call_target="tpu_custom_call" | custom-call | flops 83886080 | bytes 1048576 | tf_op jit(solution)/shard_map/inner_body/pallas_call | solution.py:372
  30.1 5.8 %all-to-all-done.1.rows_ref = bf16[8,128,128]{2,1,0:T(8,128)(2,1)S(1)} async-done(((bf16[8,128,128]{2,1,0:T(8,128)(2,1)}), bf16[8,128,128]{2,1,0:T(8,128)(2,1)S(1)}, u32[]{:S(2)}, u32[]{:S(2)}) %all-to-all-start.1) | async-done | bytes 262176 | tf_op jit(solution)/shard_map/all_to_all | solution.py:327
  35.8 1.2 %normed_body.1 = (f32[128,512]{1,0:T(8,128)S(1)}, f32[128,128]{1,0:T(8,128)S(1)}, f32[12,8,128]{2,1,0:T(8,128)}) custom-call(f32[40,128]{1,0:T(8,128)S(1)} %chosen_body.1.refs_2_.chosen_ref.refs_0_, bf16[8,128,128]{2,1,0:T(8,128)(2,1)S(1)} %all-to-all-done.1.rows_ref, bf16[8,128,128]{2,1,0:T(8,128)(2,1)S(1)} %all_to_all.25.parts_ref, ...), custom_call_target="tpu_custom_call" | custom-call | flops 33554432 | bytes 1048576 | tf_op jit(solution)/shard_map/normed_body/pallas_call | solution.py:386
  37.0 11.0 %all-to-all-start.2 = ((f32[12,8,128]{2,1,0:T(8,128)}), f32[12,8,128]{2,1,0:T(8,128)S(1)}, u32[]{:S(2)}, u32[]{:S(2)}) async-start(f32[12,8,128]{2,1,0:T(8,128)} %get-tuple-element.32.refs_6_.refs_7_), calls=%async_computation.2 | async-start | bytes 98304 | tf_op jit(solution)/shard_map/all_to_all | solution.py:415
  48.0 0.0 copy-start.9
  48.0 1.5 %window_body.1 = (bf16[1024,128]{1,0:T(8,128)(2,1)S(1)}, bf16[512,512]{1,0:T(8,128)(2,1)S(1)}, bf16[512,512]{1,0:T(8,128)(2,1)S(1)}, bf16[512,512]{1,0:T(8,128)(2,1)S(1)}) custom-call(f32[40,128]{1,0:T(8,128)S(1)} %chosen_body.1.refs_2_.chosen_ref.refs_0_, bf16[512,128]{1,0:T(8,128)(2,1)S(1)} %copy-done.7, bf16[512,128]{1,0:T(8,128)(2,1)S(1)} %copy-done.5, ...), custom_call_target="tpu_custom_call" | custom-call | flops 268435456 | bytes 2621440 | tf_op jit(solution)/shard_map/window_body/pallas_call | solution.py:396
  49.5 4.9 %collective-permute-start.1 = (bf16[1024,128]{1,0:T(8,128)(2,1)S(1)}, bf16[1024,128]{1,0:T(8,128)(2,1)S(1)}, u32[]{:S(2)}, u32[]{:S(2)}) collective-permute-start(bf16[1024,128]{1,0:T(8,128)(2,1)S(1)} %get-tuple-element.34), channel_id=1, source_target_pairs={{12,0},{24,12},{36,24},{48,36},{60,48},{72,60},{84,72},{96,84},{10... | collective-permute-start | bytes 786440 | tf_op jit(solution)/shard_map/ppermute | solution.py:343
  54.5 1.3 %own_body.1 = (bf16[512,128]{1,0:T(8,128)(2,1)}, f32[512,128]{1,0:T(8,128)S(1)}, f32[512,128]{1,0:T(8,128)S(1)}) custom-call(bf16[512,512]{1,0:T(8,128)(2,1)S(1)} %get-tuple-element.35.refs_0_, bf16[512,512]{1,0:T(8,128)(2,1)S(1)} %get-tuple-element.36.refs_1_, bf16[512,512]{1,0:T(8,128)(2,1)S(1)} %get-tuple-element.37.refs_2_, ...), custom_call_target="tpu_custom_call" | custom-call | flops 4000000000 | bytes 2621440 | tf_op jit(solution)/shard_map/own_body/pallas_call | solution.py:407
  55.8 1.9 %all-to-all-done.2.refs_0_ = f32[12,8,128]{2,1,0:T(8,128)S(1)} async-done(((f32[12,8,128]{2,1,0:T(8,128)}), f32[12,8,128]{2,1,0:T(8,128)S(1)}, u32[]{:S(2)}, u32[]{:S(2)}) %all-to-all-start.2) | async-done | bytes 49184 | tf_op jit(solution)/shard_map/all_to_all | solution.py:415
  57.7 1.3 %collective-permute-done.1.refs_4_.refs_2_ = bf16[1024,128]{1,0:T(8,128)(2,1)S(1)} collective-permute-done((bf16[1024,128]{1,0:T(8,128)(2,1)S(1)}, bf16[1024,128]{1,0:T(8,128)(2,1)S(1)}, u32[]{:S(2)}, u32[]{:S(2)}) %collective-permute-start.1) | collective-permute-done | bytes 262176 | tf_op jit(solution)/shard_map/ppermute | solution.py:343
  59.0 0.3 grad_out_body.1
  59.3 11.8 %all_to_all.26.parts_ref.refs_2_ = bf16[8,128,128]{2,1,0:T(8,128)(2,1)S(1)} all-to-all(bf16[8,128,128]{2,1,0:T(8,128)(2,1)S(1)} %get-tuple-element.43), channel_id=1, replica_groups={{0,12,24,36,48,60,72,84},{96,108,120,132,144,156,168,180},{192,204,216,..., dimensions={0} | all-to-all | bytes 524288 | tf_op jit(solution)/shard_map/all_to_all | solution.py:324
  71.1 0.8 total_body.3.refs_5_.refs_3_
  71.9 3.4 %all-to-all-start.4 = ((bf16[8,128,128]{2,1,0:T(8,128)(2,1)}), bf16[8,128,128]{2,1,0:T(8,128)(2,1)S(1)}, u32[]{:S(2)}, u32[]{:S(2)}) async-start(bf16[8,128,128]{2,1,0:T(8,128)(2,1)} %total_body.3.refs_5_.refs_3_), calls=%async_computation.4 | async-start | bytes 524288 | tf_op jit(solution)/shard_map/all_to_all | solution.py:327
  75.3 0.7 settle_body.1
  76.1 1.9 %mixed_body.1 = (bf16[512,128]{1,0:T(8,128)(2,1)}, f32[512,128]{1,0:T(8,128)S(1)}, f32[512,128]{1,0:T(8,128)S(1)}) custom-call(bf16[128,512]{1,0:T(8,128)(2,1)S(1)} %get-tuple-element.39.refs_0_, bf16[512,128]{1,0:T(8,128)(2,1)S(1)} %copy-done, bf16[1024,128]{1,0:T(8,128)(2,1)S(1)} %get-tuple-element.40.refs_2_.refs_5_, ...), custom_call_target="tpu_custom_call" | custom-call | flops 167772160 | bytes 1310720 | tf_op jit(solution)/shard_map/mixed_body/pallas_call | solution.py:427
  77.9 7.5 %all-to-all-done.4.refs_1_ = bf16[8,128,128]{2,1,0:T(8,128)(2,1)S(1)} async-done(((bf16[8,128,128]{2,1,0:T(8,128)(2,1)}), bf16[8,128,128]{2,1,0:T(8,128)(2,1)S(1)}, u32[]{:S(2)}, u32[]{:S(2)}) %all-to-all-start.4) | async-done | bytes 262176 | tf_op jit(solution)/shard_map/all_to_all | solution.py:327
  85.4 1.1 %closing_body.1 = (bf16[512,128]{1,0:T(8,128)(2,1)}, bf16[512,128]{1,0:T(8,128)(2,1)}) custom-call(f32[40,128]{1,0:T(8,128)S(1)} %chosen_body.1.refs_2_.chosen_ref.refs_0_, bf16[8,128,128]{2,1,0:T(8,128)(2,1)S(1)} %all-to-all-done.4.refs_1_, bf16[8,128,128]{2,1,0:T(8,128)(2,1)S(1)} %all_to_all.26.parts_ref.refs_2_, ...), custom_call_target="tpu_custom_call" | custom-call | flops 67108864 | bytes 1048576 | tf_op jit(solution)/shard_map/closing_body/pallas_call | solution.py:445
  (14 shorter events, 0.0 us)
Async XLA Ops:
  0.7 0.9 %copy-start.1 = (bf16[512,128]{1,0:T(8,128)(2,1)S(1)}, bf16[512,128]{1,0:T(8,128)(2,1)}, u32[]{:S(2)}) copy-start(bf16[512,128]{1,0:T(8,128)(2,1)} %refs_1_.6) | copy-start | bytes 393220
  0.7 1.0 %copy-start.2 = (bf16[512,128]{1,0:T(8,128)(2,1)S(1)}, bf16[512,128]{1,0:T(8,128)(2,1)}, u32[]{:S(2)}) copy-start(bf16[512,128]{1,0:T(8,128)(2,1)} %refs_2_.2) | copy-start | bytes 393220
  22.2 3.6 %copy-start.4 = (bf16[512,128]{1,0:T(8,128)(2,1)S(1)}, bf16[512,128]{1,0:T(8,128)(2,1)}, u32[]{:S(2)}) copy-start(bf16[512,128]{1,0:T(8,128)(2,1)} %refs_3_.4) | copy-start | bytes 393220
  22.2 3.6 %copy-start.5 = (bf16[512,128]{1,0:T(8,128)(2,1)S(1)}, bf16[512,128]{1,0:T(8,128)(2,1)}, u32[]{:S(2)}) copy-start(bf16[512,128]{1,0:T(8,128)(2,1)} %refs_5_.1) | copy-start | bytes 393220
  22.2 13.6 %all-to-all-start.1 = ((bf16[8,128,128]{2,1,0:T(8,128)(2,1)}), bf16[8,128,128]{2,1,0:T(8,128)(2,1)S(1)}, u32[]{:S(2)}, u32[]{:S(2)}) async-start(bf16[8,128,128]{2,1,0:T(8,128)(2,1)} %total_body.2.refs_5_.refs_2_), calls=%async_computation.1 | async-start | bytes 524288 | tf_op jit(solution)/shard_map/all_to_all | solution.py:327
  25.8 3.3 %copy-start = (bf16[512,128]{1,0:T(8,128)(2,1)S(1)}, bf16[512,128]{1,0:T(8,128)(2,1)}, u32[]{:S(2)}) copy-start(bf16[512,128]{1,0:T(8,128)(2,1)} %refs_1_.9) | copy-start | bytes 393220
  25.8 3.3 %copy-start.3 = (bf16[512,128]{1,0:T(8,128)(2,1)S(1)}, bf16[512,128]{1,0:T(8,128)(2,1)}, u32[]{:S(2)}) copy-start(bf16[512,128]{1,0:T(8,128)(2,1)} %refs_3_.3) | copy-start | bytes 393220
  25.8 3.3 %copy-start.6 = (f32[128]{0:T(128)S(1)}, f32[128]{0:T(128)}, u32[]{:S(2)}) copy-start(f32[128]{0:T(128)} %param.12) | copy-start | bytes 1540
  25.8 22.2 %collective-permute-start = (bf16[1024,128]{1,0:T(8,128)(2,1)S(1)}, bf16[1024,128]{1,0:T(8,128)(2,1)S(1)}, u32[]{:S(2)}, u32[]{:S(2)}) collective-permute-start(bf16[1024,128]{1,0:T(8,128)(2,1)S(1)} %pack_body.1), channel_id=1, source_target_pairs={{0,12},{12,24},{24,36},{36,48},{48,60},{60,72},{72,84},{84,96},{96... | collective-permute-start | bytes 786440 | tf_op jit(solution)/shard_map/ppermute | solution.py:343
  35.8 12.2 %copy-start.7 = (bf16[512,128]{1,0:T(8,128)(2,1)S(1)}, bf16[512,128]{1,0:T(8,128)(2,1)}, u32[]{:S(2)}) copy-start(bf16[512,128]{1,0:T(8,128)(2,1)} %refs_4_.3) | copy-start | bytes 393220
  35.8 12.2 %copy-start.8 = (bf16[512,128]{1,0:T(8,128)(2,1)S(1)}, bf16[512,128]{1,0:T(8,128)(2,1)}, u32[]{:S(2)}) copy-start(bf16[512,128]{1,0:T(8,128)(2,1)} %refs_6_.1) | copy-start | bytes 393220
  37.0 20.7 %all-to-all-start.2 = ((f32[12,8,128]{2,1,0:T(8,128)}), f32[12,8,128]{2,1,0:T(8,128)S(1)}, u32[]{:S(2)}, u32[]{:S(2)}) async-start(f32[12,8,128]{2,1,0:T(8,128)} %get-tuple-element.32.refs_6_.refs_7_), calls=%async_computation.2 | async-start | bytes 98304 | tf_op jit(solution)/shard_map/all_to_all | solution.py:415
  48.0 6.4 %copy-start.9 = (bf16[512,128]{1,0:T(8,128)(2,1)S(1)}, bf16[512,128]{1,0:T(8,128)(2,1)}, u32[]{:S(2)}) copy-start(bf16[512,128]{1,0:T(8,128)(2,1)} %refs_6_.1) | copy-start | bytes 393220
  49.5 9.5 %collective-permute-start.1 = (bf16[1024,128]{1,0:T(8,128)(2,1)S(1)}, bf16[1024,128]{1,0:T(8,128)(2,1)S(1)}, u32[]{:S(2)}, u32[]{:S(2)}) collective-permute-start(bf16[1024,128]{1,0:T(8,128)(2,1)S(1)} %get-tuple-element.34), channel_id=1, source_target_pairs={{12,0},{24,12},{36,24},{48,36},{60,48},{72,60},{84,72},{96,84},{10... | collective-permute-start | bytes 786440 | tf_op jit(solution)/shard_map/ppermute | solution.py:343
  71.9 13.5 %all-to-all-start.4 = ((bf16[8,128,128]{2,1,0:T(8,128)(2,1)}), bf16[8,128,128]{2,1,0:T(8,128)(2,1)S(1)}, u32[]{:S(2)}, u32[]{:S(2)}) async-start(bf16[8,128,128]{2,1,0:T(8,128)(2,1)} %total_body.3.refs_5_.refs_3_), calls=%async_computation.4 | async-start | bytes 524288 | tf_op jit(solution)/shard_map/all_to_all | solution.py:327

commit v5 on v4

--- a/solution.py
+++ b/solution.py
@@ -110,21 +110,24 @@
     out_ref[span:] = value_ref[...]
 
 
-def chosen_sum(chosen_ref, rows_ref, parts_ref, later):
+def chosen_sum(chosen_ref, group, ref):
     total = None
-    base = 2 * ROW if later else 0
-    for ref, first in ((rows_ref, base), (parts_ref, base + ROW)):
-        for place in range(ref.shape[0]):
-            wanted = chosen_ref[first + place : first + place + 1, :]
-            term = ref[place].astype(f32) * wanted
-            total = term if total is None else total + term
+    for place in range(ref.shape[0]):
+        first = group * ROW + place
+        term = ref[place].astype(f32) * chosen_ref[first : first + 1, :]
+        total = term if total is None else total + term
     return total
 
 
+def twice(value):
+    return jnp.concatenate([value, value], 1)
+
+
 def inner_body(
-    query_ref, key_ref, value_ref, grad_ref, gain_ref,
-    probs_ref, kept_ref, inner_ref, scaled_ref,
-):
+    chosen_ref, parts_ref, query_ref, key_ref, value_ref, grad_ref, gain_ref,
+    probs_ref, kept_ref, inner_ref, scaled_ref, base_ref,
+):
+    base_ref[...] = chosen_sum(chosen_ref, 1, parts_ref)
     tokens = query_ref.shape[0]
     kept_ref[:tokens] = key_ref[...]
     kept_ref[tokens:] = value_ref[...]
@@ -145,17 +148,16 @@
 
 
 def normed_body(
-    chosen_ref, rows_ref, parts_ref, inner_ref, query_ref, scaled_ref,
+    chosen_ref, rows_ref, base_ref, inner_ref, query_ref, scaled_ref,
     lin_ref, prior_ref, sums_hbm, near, sent,
 ):
-    prior = chosen_sum(chosen_ref, rows_ref, parts_ref, False)
+    prior = base_ref[...] + chosen_sum(chosen_ref, 0, rows_ref)
     prior_ref[...] = prior
-    high, low = halves(jnp.transpose(prior))
+    both = jnp.concatenate(halves(jnp.transpose(prior)), 1)
     squares, crosses = [], []
     for start in range(0, query_ref.shape[0], TILE):
         here = slice(start, start + TILE)
-        query = query_ref[here]
-        lin_out = inner_ref[:, here] + dot_nt(high, query) + dot_nt(low, query)
+        lin_out = inner_ref[:, here] + dot_nt(both, twice(query_ref[here]))
         lin_ref[:, here] = lin_out
         squares.append(jnp.sum(lin_out * lin_out, axis=0, keepdims=True))
         crosses.append(jnp.sum(scaled_ref[:, here] * lin_out, axis=0, keepdims=True))
@@ -181,8 +183,10 @@
 
 
 def mixed_body(
-    turned_ref, query_ref, kept_ref, probs_ref, prior_ref, gq_ref, gk_ref, gv_ref, grad_ref,
-):
+    chosen_ref, parts_ref, turned_ref, query_ref, kept_ref, probs_ref, prior_ref,
+    gq_ref, gk_ref, gv_ref, base_ref, grad_ref,
+):
+    base_ref[...] = chosen_sum(chosen_ref, 3, parts_ref)
     tokens = query_ref.shape[0]
     for start in range(0, tokens, TILE):
         here = slice(start, start + TILE)
@@ -210,17 +214,18 @@
 
 
 def closing_body(
-    chosen_ref, rows_ref, parts_ref, gk_part_ref, gv_part_ref, kept_ref,
+    chosen_ref, rows_ref, base_ref, gk_part_ref, gv_part_ref, kept_ref,
     gk_hbm, gv_hbm, gk_ref, gv_ref, sent,
 ):
-    high, low = halves(chosen_sum(chosen_ref, rows_ref, parts_ref, True))
+    high, low = halves(base_ref[...] + chosen_sum(chosen_ref, 2, rows_ref))
+    wide, tall = jnp.concatenate([high, low], 1), jnp.concatenate([high, low], 0)
     copies = []
     tokens = gk_ref.shape[0]
     for start in range(0, tokens, 2 * TILE):
         here = pl.ds(start, 2 * TILE)
         key, value = kept_ref[here], kept_ref[pl.ds(tokens + start, 2 * TILE)]
-        gk_ref[here] = (gk_part_ref[here] + dot_nt(value, high) + dot_nt(value, low)).astype(bf16)
-        gv_ref[here] = (gv_part_ref[here] + dot_nn(key, high) + dot_nn(key, low)).astype(bf16)
+        gk_ref[here] = (gk_part_ref[here] + dot_nt(twice(value), wide)).astype(bf16)
+        gv_ref[here] = (gv_part_ref[here] + dot_nn(twice(key), tall)).astype(bf16)
         for near, far in ((gk_ref, gk_hbm), (gv_ref, gv_hbm)):
             copy = pltpu.make_async_copy(near.at[here], far.at[here], sent.at[len(copies)])
             copy.start()
@@ -241,21 +246,20 @@
         stop = start + TILE
         here = slice(start, stop)
         query, grad = query_ref[here], grad_ref[here]
-        behind = dot_nt(halo_ref[start:span], query)
+        behind = dot_nt(halo_ref[start:span], query) * scale
         edge = jnp.where(upper, HIDDEN, behind[:TILE])
         behind = jnp.concatenate([edge, behind[TILE:]], 0) if stop < span else edge
         behind = jnp.where(first, HIDDEN, behind)
-        own = dot_nt(key_ref[:stop], query)
+        own = dot_nt(key_ref[:stop], query) * scale
         edge = jnp.where(upper, own[start:], HIDDEN)
         own = jnp.concatenate([own[:start], edge], 0) if start else edge
         peak = jnp.maximum(
             jnp.max(behind, axis=0, keepdims=True), jnp.max(own, axis=0, keepdims=True)
         )
-        behind = jnp.exp((behind - peak) * scale)
-        own = jnp.exp((own - peak) * scale)
+        behind = jnp.exp(behind - peak)
+        own = jnp.exp(own - peak)
         total = jnp.sum(behind, axis=0, keepdims=True) + jnp.sum(own, axis=0, keepdims=True)
-        inverse = 1.0 / total
-        behind, own = behind * inverse, own * inverse
+        behind, own = behind / total, own / total
         behind_win, own_win = behind.astype(bf16), own.astype(bf16)
         behind_grad = dot_nt(halo_ref[span + start :], grad)
         own_grad = dot_nt(value_ref[:stop], grad)
@@ -369,19 +373,20 @@
     )(key_win, value_win, row_sum)
     halo = shift(halo_pack, 1)
     turned = (width, tokens)
-    probs, kept, inner, scaled = kernel_call(
+    probs, kept, inner, scaled, base = kernel_call(
         inner_body,
         (
             shaped((tokens, tokens), bf16),
             shaped((2 * tokens, width), bf16),
             shaped(turned, f32),
             shaped(turned, f32),
+            shaped(state, f32),
         ),
         2.5 * square,
         8 * size,
-        specs=[in_vmem] * 5 + [anywhere],
-        ahead=1,
-    )(query_lin, key_lin, value_lin, grad_normed, gain, row_sum)
+        specs=[in_vmem] * 7 + [anywhere],
+        ahead=1,
+    )(chosen, parts, query_lin, key_lin, value_lin, grad_normed, gain, row_sum)
     row_parts = along_col(row_sum)
     lin_out, prior, sums = kernel_call(
         normed_body,
@@ -391,7 +396,7 @@
         scratch=(pltpu.VMEM((8, TILE), f32), pltpu.SemaphoreType.DMA((heads,))),
         specs=[in_vmem] + [in_vmem] * 5,
         out_specs=(in_vmem, in_vmem, in_hbm),
-    )(chosen, row_parts, parts, inner, query_lin, scaled)
+    )(chosen, row_parts, base, inner, query_lin, scaled)
     flat = shaped((tokens, tokens), bf16)
     back, behind_logit, own_logit, own_win = kernel_call(
         window_body,
@@ -424,15 +429,15 @@
     )(all_sums, lin_out, scaled, query_lin, returned, gk_own)
     later_parts = along_row(later_state)
     later_sum = row_total(later_parts, 8 * DH * DH)
-    gq_lin, gk_part, gv_part = kernel_call(
+    gq_lin, gk_part, gv_part, later_base = kernel_call(
         mixed_body,
-        (shaped(block, bf16), shaped(block, f32), shaped(block, f32)),
+        (shaped(block, bf16), shaped(block, f32), shaped(block, f32), shaped(state, f32)),
         5 * square,
         10 * size,
         scratch=(pltpu.VMEM(block, bf16),),
-        specs=[in_vmem] * 5 + [anywhere],
-        ahead=1,
-    )(grad_out, query_lin, kept, probs, prior, later_sum)
+        specs=[in_vmem] * 7 + [anywhere],
+        ahead=1,
+    )(chosen, later_parts, grad_out, query_lin, kept, probs, prior, later_sum)
     later_rows = along_col(later_sum)
     gk_win, gv_win, settled = kernel_call(
         settle_body,
@@ -451,7 +456,7 @@
         specs=[in_vmem] + [in_vmem] * 5 + [anywhere],
         out_specs=(in_hbm, in_hbm),
         ahead=1,
-    )(chosen, later_rows, later_parts, gk_part, gv_part, kept, settled)
+    )(chosen, later_rows, later_base, gk_part, gv_part, kept, settled)
     return gq_lin, gk_lin, gv_lin, gq_win, gk_win, gv_win
 
 

time: 87.3 us -> 87.1 us (level)
  no operation moved by 1% of the time
where the time goes in v5:
time: 87.1 us; the launch traced here: 86.4 us
  blocking collectives  31.3 us (36%)
  starting transfers between devices  26.2 us (30%)
  waiting for transfers between devices  16.4 us (19%)
  Pallas kernels  11.1 us (13%)
  between operations  0.9 us (1%)
    all_to_all x2, blocking collectives, along_row(): return lax.all_to_all(value, 'ctx', 0, 0, axis_index_groups=row_groups)  31.3 us
    all_to_all x2, waiting for transfers between devices, along_col(): return lax.all_to_all(value, 'ctx', 0, 0, axis_index_groups=col_groups)  13.2 us
    all_to_all x1, starting transfers between devices, local(): all_sums = lax.all_to_all(sums, 'head', 0, 0)  11 us
    ppermute x2, starting transfers between devices, shift(): lax.ppermute(value, 'ctx', [(at, at + steps) for at in range(first, last)])  8.2 us
    all_to_all x2, starting transfers between devices, along_col(): return lax.all_to_all(value, 'ctx', 0, 0, axis_index_groups=col_groups)  6.98 us
    all_to_all x1, waiting for transfers between devices, local(): all_sums = lax.all_to_all(sums, 'head', 0, 0)  1.95 us
    pallas_call x1, Pallas kernels, local(): kernel_call(mixed_body, (shaped(block, bf16), shaped(block, f32), shaped(...  1.88 us
  transfers between devices with their start and end apart: 5, of which 4 were waited for; matrix products, arithmetic and copies ran while one was open for 0% of the time, Pallas kernels for 9%

profile of v5, /device:TPU:1, one launch (start us, length us, event | category | flops | bytes accessed | tf_op | source)
XLA Modules:
  0.0 86.4 jit_solution(8057936398165945214)
XLA Ops:
  0.7 0.1 pad_add_fusion.where_ref
  0.7 0.5 chosen_body.1.refs_2_.refs_0_.chosen_ref
  1.3 0.3 copy-done.1
  1.6 0.1 copy-done.2
  1.7 0.2 state_body.1
  1.9 19.4 %all_to_all.25.parts_ref.refs_1_ = bf16[8,128,128]{2,1,0:T(8,128)(2,1)S(1)} all-to-all(bf16[8,128,128]{2,1,0:T(8,128)(2,1)S(1)} %state_body.1), channel_id=1, replica_groups={{0,12,24,36,48,60,72,84},{96,108,120,132,144,156,168,180},{192,204,216,..., dimensions={0} | all-to-all | bytes 524288 | tf_op jit(solution)/shard_map/all_to_all | solution.py:328
  21.4 0.8 total_body.2.refs_7_.refs_2_
  22.2 0.0 copy-start.3
  22.2 0.0 copy-start.4
  22.2 3.6 %all-to-all-start.1 = ((bf16[8,128,128]{2,1,0:T(8,128)(2,1)}), bf16[8,128,128]{2,1,0:T(8,128)(2,1)S(1)}, u32[]{:S(2)}, u32[]{:S(2)}) async-start(bf16[8,128,128]{2,1,0:T(8,128)(2,1)} %total_body.2.refs_7_.refs_2_), calls=%async_computation.1 | async-start | bytes 524288 | tf_op jit(solution)/shard_map/all_to_all | solution.py:331
  25.8 0.0 copy-start
  25.8 0.0 copy-start.5
  25.8 0.0 copy-start.6
  25.8 3.3 %collective-permute-start = (bf16[1024,128]{1,0:T(8,128)(2,1)S(1)}, bf16[1024,128]{1,0:T(8,128)(2,1)S(1)}, u32[]{:S(2)}, u32[]{:S(2)}) collective-permute-start(bf16[1024,128]{1,0:T(8,128)(2,1)S(1)} %pack_body.1), channel_id=1, source_target_pairs={{0,12},{12,24},{24,36},{36,48},{48,60},{60,72},{72,84},{84,96},{96... | collective-permute-start | bytes 786440 | tf_op jit(solution)/shard_map/ppermute | solution.py:347
  29.1 1.0 %inner_body.1 = (bf16[512,512]{1,0:T(8,128)(2,1)S(1)}, bf16[1024,128]{1,0:T(8,128)(2,1)S(1)}, f32[128,512]{1,0:T(8,128)S(1)}, f32[128,512]{1,0:T(8,128)S(1)}, f32[128,128]{1,0:T(8,128)S(1)}) custom-call(f32[40,128]{1,0:T(8,128)S(1)} %chosen_body.1.refs_2_.refs_0_.chosen_ref, bf16[8,128,128]{2,1,0:T(8,128)(2,1)S(1)} %all_to_all.25.parts_ref.refs_1_, ...), custom_call_target="tpu_custom_call" | custom-call | flops 83886080 | bytes 1048576 | tf_op jit(solution)/shard_map/inner_body/pallas_call | solution.py:376
  30.1 5.7 %all-to-all-done.1.rows_ref = bf16[8,128,128]{2,1,0:T(8,128)(2,1)S(1)} async-done(((bf16[8,128,128]{2,1,0:T(8,128)(2,1)}), bf16[8,128,128]{2,1,0:T(8,128)(2,1)S(1)}, u32[]{:S(2)}, u32[]{:S(2)}) %all-to-all-start.1) | async-done | bytes 262176 | tf_op jit(solution)/shard_map/all_to_all | solution.py:331
  35.8 1.1 %normed_body.1 = (f32[128,512]{1,0:T(8,128)S(1)}, f32[128,128]{1,0:T(8,128)S(1)}, f32[12,8,128]{2,1,0:T(8,128)}) custom-call(f32[40,128]{1,0:T(8,128)S(1)} %chosen_body.1.refs_2_.refs_0_.chosen_ref, bf16[8,128,128]{2,1,0:T(8,128)(2,1)S(1)} %all-to-all-done.1.rows_ref, f32[128,128]{1,0:T(8,128)S(1)} %get-tuple-element.32.base_ref, ...), custom_call_target="tpu_custom_call" | custom-call | flops 33554432 | bytes 1048576 | tf_op jit(solution)/shard_map/normed_body/pallas_call | solution.py:391
  36.9 11.0 %all-to-all-start.2 = ((f32[12,8,128]{2,1,0:T(8,128)}), f32[12,8,128]{2,1,0:T(8,128)S(1)}, u32[]{:S(2)}, u32[]{:S(2)}) async-start(f32[12,8,128]{2,1,0:T(8,128)} %get-tuple-element.35.refs_6_.refs_7_), calls=%async_computation.2 | async-start | bytes 98304 | tf_op jit(solution)/shard_map/all_to_all | solution.py:420
  47.9 0.0 copy-start.8
  48.0 1.4 %window_body.1 = (bf16[1024,128]{1,0:T(8,128)(2,1)S(1)}, bf16[512,512]{1,0:T(8,128)(2,1)S(1)}, bf16[512,512]{1,0:T(8,128)(2,1)S(1)}, bf16[512,512]{1,0:T(8,128)(2,1)S(1)}) custom-call(f32[40,128]{1,0:T(8,128)S(1)} %chosen_body.1.refs_2_.refs_0_.chosen_ref, bf16[512,128]{1,0:T(8,128)(2,1)S(1)} %copy-done.7, bf16[512,128]{1,0:T(8,128)(2,1)S(1)} %copy-done.4, ...), custom_call_target="tpu_custom_call" | custom-call | flops 268435456 | bytes 2621440 | tf_op jit(solution)/shard_map/window_body/pallas_call | solution.py:401
  49.4 4.9 %collective-permute-start.1 = (bf16[1024,128]{1,0:T(8,128)(2,1)S(1)}, bf16[1024,128]{1,0:T(8,128)(2,1)S(1)}, u32[]{:S(2)}, u32[]{:S(2)}) collective-permute-start(bf16[1024,128]{1,0:T(8,128)(2,1)S(1)} %get-tuple-element.37), channel_id=1, source_target_pairs={{12,0},{24,12},{36,24},{48,36},{60,48},{72,60},{84,72},{96,84},{10... | collective-permute-start | bytes 786440 | tf_op jit(solution)/shard_map/ppermute | solution.py:347
  54.4 1.3 %own_body.1 = (bf16[512,128]{1,0:T(8,128)(2,1)}, f32[512,128]{1,0:T(8,128)S(1)}, f32[512,128]{1,0:T(8,128)S(1)}) custom-call(bf16[512,512]{1,0:T(8,128)(2,1)S(1)} %get-tuple-element.38.refs_0_, bf16[512,512]{1,0:T(8,128)(2,1)S(1)} %get-tuple-element.39.refs_1_, bf16[512,512]{1,0:T(8,128)(2,1)S(1)} %get-tuple-element.40.refs_2_, ...), custom_call_target="tpu_custom_call" | custom-call | flops 4000000000 | bytes 2621440 | tf_op jit(solution)/shard_map/own_body/pallas_call | solution.py:412
  55.6 1.9 %all-to-all-done.2.refs_0_ = f32[12,8,128]{2,1,0:T(8,128)S(1)} async-done(((f32[12,8,128]{2,1,0:T(8,128)}), f32[12,8,128]{2,1,0:T(8,128)S(1)}, u32[]{:S(2)}, u32[]{:S(2)}) %all-to-all-start.2) | async-done | bytes 49184 | tf_op jit(solution)/shard_map/all_to_all | solution.py:420
  57.6 1.2 %collective-permute-done.1.refs_4_.refs_2_ = bf16[1024,128]{1,0:T(8,128)(2,1)S(1)} collective-permute-done((bf16[1024,128]{1,0:T(8,128)(2,1)S(1)}, bf16[1024,128]{1,0:T(8,128)(2,1)S(1)}, u32[]{:S(2)}, u32[]{:S(2)}) %collective-permute-start.1) | collective-permute-done | bytes 262176 | tf_op jit(solution)/shard_map/ppermute | solution.py:347
  58.8 0.3 grad_out_body.1
  59.1 11.8 %all_to_all.26.parts_ref.refs_1_ = bf16[8,128,128]{2,1,0:T(8,128)(2,1)S(1)} all-to-all(bf16[8,128,128]{2,1,0:T(8,128)(2,1)S(1)} %get-tuple-element.42), channel_id=1, replica_groups={{0,12,24,36,48,60,72,84},{96,108,120,132,144,156,168,180},{192,204,216,..., dimensions={0} | all-to-all | bytes 524288 | tf_op jit(solution)/shard_map/all_to_all | solution.py:328
  71.0 0.8 total_body.3.refs_7_.refs_3_
  71.8 3.4 %all-to-all-start.4 = ((bf16[8,128,128]{2,1,0:T(8,128)(2,1)}), bf16[8,128,128]{2,1,0:T(8,128)(2,1)S(1)}, u32[]{:S(2)}, u32[]{:S(2)}) async-start(bf16[8,128,128]{2,1,0:T(8,128)(2,1)} %total_body.3.refs_7_.refs_3_), calls=%async_computation.4 | async-start | bytes 524288 | tf_op jit(solution)/shard_map/all_to_all | solution.py:331
  75.2 0.7 settle_body.1
  76.0 1.9 %mixed_body.1 = (bf16[512,128]{1,0:T(8,128)(2,1)}, f32[512,128]{1,0:T(8,128)S(1)}, f32[512,128]{1,0:T(8,128)S(1)}, f32[128,128]{1,0:T(8,128)S(1)}) custom-call(f32[40,128]{1,0:T(8,128)S(1)} %chosen_body.1.refs_2_.refs_0_.chosen_ref, bf16[8,128,128]{2,1,0:T(8,128)(2,1)S(1)} %all_to_all.26.parts_ref.refs_1_, bf16[128,512]{1,0:T(8,128)(2,1)S(1)} %get-tuple-element.43.refs_2_, ...), custom_call_target="tpu_custom_call" | custom-call | flops 167772160 | bytes 1310720 | tf_op jit(solution)/shard_map/mixed_body/pallas_call | solution.py:432
  77.8 7.5 %all-to-all-done.4.refs_1_ = bf16[8,128,128]{2,1,0:T(8,128)(2,1)S(1)} async-done(((bf16[8,128,128]{2,1,0:T(8,128)(2,1)}), bf16[8,128,128]{2,1,0:T(8,128)(2,1)S(1)}, u32[]{:S(2)}, u32[]{:S(2)}) %all-to-all-start.4) | async-done | bytes 262176 | tf_op jit(solution)/shard_map/all_to_all | solution.py:331
  85.3 1.1 %closing_body.1 = (bf16[512,128]{1,0:T(8,128)(2,1)}, bf16[512,128]{1,0:T(8,128)(2,1)}) custom-call(f32[40,128]{1,0:T(8,128)S(1)} %chosen_body.1.refs_2_.refs_0_.chosen_ref, bf16[8,128,128]{2,1,0:T(8,128)(2,1)S(1)} %all-to-all-done.4.refs_1_, f32[128,128]{1,0:T(8,128)S(1)} %get-tuple-element.48.refs_2_, f32[512,128]{1,0:T(8,128)S(1)} %get-tuple-element.49.refs_3_, ...), custom_call_target="tpu_custom_call" | custom-call | flops 67108864 | bytes 1048576 | tf_op jit(solution)/shard_map/closing_body/pallas_call | solution.py:450
  (16 shorter events, 0.1 us)
Async XLA Ops:
  0.7 0.9 %copy-start.1 = (bf16[512,128]{1,0:T(8,128)(2,1)S(1)}, bf16[512,128]{1,0:T(8,128)(2,1)}, u32[]{:S(2)}) copy-start(bf16[512,128]{1,0:T(8,128)(2,1)} %refs_3_.4) | copy-start | bytes 393220
  0.7 1.0 %copy-start.2 = (bf16[512,128]{1,0:T(8,128)(2,1)S(1)}, bf16[512,128]{1,0:T(8,128)(2,1)}, u32[]{:S(2)}) copy-start(bf16[512,128]{1,0:T(8,128)(2,1)} %refs_4_.3) | copy-start | bytes 393220
  22.2 3.6 %copy-start.3 = (bf16[512,128]{1,0:T(8,128)(2,1)S(1)}, bf16[512,128]{1,0:T(8,128)(2,1)}, u32[]{:S(2)}) copy-start(bf16[512,128]{1,0:T(8,128)(2,1)} %refs_3_.5) | copy-start | bytes 393220
  22.2 3.6 %copy-start.4 = (bf16[512,128]{1,0:T(8,128)(2,1)S(1)}, bf16[512,128]{1,0:T(8,128)(2,1)}, u32[]{:S(2)}) copy-start(bf16[512,128]{1,0:T(8,128)(2,1)} %refs_5_.3) | copy-start | bytes 393220
  22.2 13.6 %all-to-all-start.1 = ((bf16[8,128,128]{2,1,0:T(8,128)(2,1)}), bf16[8,128,128]{2,1,0:T(8,128)(2,1)S(1)}, u32[]{:S(2)}, u32[]{:S(2)}) async-start(bf16[8,128,128]{2,1,0:T(8,128)(2,1)} %total_body.2.refs_7_.refs_2_), calls=%async_computation.1 | async-start | bytes 524288 | tf_op jit(solution)/shard_map/all_to_all | solution.py:331
  25.8 3.3 %copy-start = (bf16[512,128]{1,0:T(8,128)(2,1)S(1)}, bf16[512,128]{1,0:T(8,128)(2,1)}, u32[]{:S(2)}) copy-start(bf16[512,128]{1,0:T(8,128)(2,1)} %refs_3_.7) | copy-start | bytes 393220
  25.8 3.3 %copy-start.5 = (bf16[512,128]{1,0:T(8,128)(2,1)S(1)}, bf16[512,128]{1,0:T(8,128)(2,1)}, u32[]{:S(2)}) copy-start(bf16[512,128]{1,0:T(8,128)(2,1)} %refs_5_.2) | copy-start | bytes 393220
  25.8 3.3 %copy-start.6 = (f32[128]{0:T(128)S(1)}, f32[128]{0:T(128)}, u32[]{:S(2)}) copy-start(f32[128]{0:T(128)} %param.12) | copy-start | bytes 1540
  25.8 22.1 %collective-permute-start = (bf16[1024,128]{1,0:T(8,128)(2,1)S(1)}, bf16[1024,128]{1,0:T(8,128)(2,1)S(1)}, u32[]{:S(2)}, u32[]{:S(2)}) collective-permute-start(bf16[1024,128]{1,0:T(8,128)(2,1)S(1)} %pack_body.1), channel_id=1, source_target_pairs={{0,12},{12,24},{24,36},{36,48},{48,60},{60,72},{72,84},{84,96},{96... | collective-permute-start | bytes 786440 | tf_op jit(solution)/shard_map/ppermute | solution.py:347
  35.8 12.1 %copy-start.7 = (bf16[512,128]{1,0:T(8,128)(2,1)S(1)}, bf16[512,128]{1,0:T(8,128)(2,1)}, u32[]{:S(2)}) copy-start(bf16[512,128]{1,0:T(8,128)(2,1)} %refs_4_.5) | copy-start | bytes 393220
  35.8 12.1 %copy-start.9 = (bf16[512,128]{1,0:T(8,128)(2,1)S(1)}, bf16[512,128]{1,0:T(8,128)(2,1)}, u32[]{:S(2)}) copy-start(bf16[512,128]{1,0:T(8,128)(2,1)} %refs_6_.1) | copy-start | bytes 393220
  36.9 20.7 %all-to-all-start.2 = ((f32[12,8,128]{2,1,0:T(8,128)}), f32[12,8,128]{2,1,0:T(8,128)S(1)}, u32[]{:S(2)}, u32[]{:S(2)}) async-start(f32[12,8,128]{2,1,0:T(8,128)} %get-tuple-element.35.refs_6_.refs_7_), calls=%async_computation.2 | async-start | bytes 98304 | tf_op jit(solution)/shard_map/all_to_all | solution.py:420
  47.9 6.4 %copy-start.8 = (bf16[512,128]{1,0:T(8,128)(2,1)S(1)}, bf16[512,128]{1,0:T(8,128)(2,1)}, u32[]{:S(2)}) copy-start(bf16[512,128]{1,0:T(8,128)(2,1)} %refs_4_.5) | copy-start | bytes 393220
  47.9 6.4 %copy-start.10 = (bf16[512,128]{1,0:T(8,128)(2,1)S(1)}, bf16[512,128]{1,0:T(8,128)(2,1)}, u32[]{:S(2)}) copy-start(bf16[512,128]{1,0:T(8,128)(2,1)} %refs_6_.1) | copy-start | bytes 393220
  49.4 9.4 %collective-permute-start.1 = (bf16[1024,128]{1,0:T(8,128)(2,1)S(1)}, bf16[1024,128]{1,0:T(8,128)(2,1)S(1)}, u32[]{:S(2)}, u32[]{:S(2)}) collective-permute-start(bf16[1024,128]{1,0:T(8,128)(2,1)S(1)} %get-tuple-element.37), channel_id=1, source_target_pairs={{12,0},{24,12},{36,24},{48,36},{60,48},{72,60},{84,72},{96,84},{10... | collective-permute-start | bytes 786440 | tf_op jit(solution)/shard_map/ppermute | solution.py:347
  71.8 13.5 %all-to-all-start.4 = ((bf16[8,128,128]{2,1,0:T(8,128)(2,1)}), bf16[8,128,128]{2,1,0:T(8,128)(2,1)S(1)}, u32[]{:S(2)}, u32[]{:S(2)}) async-start(bf16[8,128,128]{2,1,0:T(8,128)(2,1)} %total_body.3.refs_7_.refs_3_), calls=%async_computation.4 | async-start | bytes 524288 | tf_op jit(solution)/shard_map/all_to_all | solution.py:331

commit v6 on v5

--- a/solution.py
+++ b/solution.py
@@ -73,7 +73,8 @@
 
 
 def chosen_body(where_ref, out_ref):
-    row, col, index = where_ref[0], where_ref[1], where_ref[2]
+    index = where_ref[0]
+    row, col = lax.div(index, ROW), lax.rem(index, ROW)
     place = lax.broadcasted_iota(jnp.int32, (ROW, TILE), 0)
     for group, wanted in enumerate((place < row, place < col, place > row, place > col)):
         out_ref[group * ROW : (group + 1) * ROW] = jnp.where(wanted, 1.0, 0.0)
@@ -309,7 +310,7 @@
     blocks, heads = lax.axis_size("ctx"), lax.axis_size("head")
     rows = blocks // ROW
     my_index = lax.axis_index("ctx")
-    where = jnp.stack([my_index // ROW, my_index % ROW, my_index]).astype(jnp.int32)
+    where = my_index.astype(jnp.int32).reshape(1)
     row_groups = [[row * ROW + col for col in range(ROW)] for row in range(rows)]
     col_groups = [[row * ROW + col for row in range(rows)] for col in range(ROW)]
     gain = norm_gain.reshape(1, width)

time: 87.1 us -> 87 us (level)
  no operation moved by 1% of the time
where the time goes in v6:
time: 87 us; the launch traced here: 86.3 us
  blocking collectives  31.3 us (36%)
  starting transfers between devices  26.2 us (30%)
  waiting for transfers between devices  16.4 us (19%)
  Pallas kernels  10.6 us (12%)
  local copies, waits for them, and re-layouts  0.99 us (1%)
  between operations  0.9 us (1%)
    all_to_all x2, blocking collectives, along_row(): return lax.all_to_all(value, 'ctx', 0, 0, axis_index_groups=row_groups)  31.3 us
    all_to_all x2, waiting for transfers between devices, along_col(): return lax.all_to_all(value, 'ctx', 0, 0, axis_index_groups=col_groups)  13.2 us
    all_to_all x1, starting transfers between devices, local(): all_sums = lax.all_to_all(sums, 'head', 0, 0)  11 us
    ppermute x2, starting transfers between devices, shift(): lax.ppermute(value, 'ctx', [(at, at + steps) for at in range(first, last)])  8.2 us
    all_to_all x2, starting transfers between devices, along_col(): return lax.all_to_all(value, 'ctx', 0, 0, axis_index_groups=col_groups)  6.98 us
    all_to_all x1, waiting for transfers between devices, local(): all_sums = lax.all_to_all(sums, 'head', 0, 0)  1.95 us
    pallas_call x1, Pallas kernels, local(): kernel_call(mixed_body, (shaped(block, bf16), shaped(block, f32), shaped(...  1.88 us
  transfers between devices with their start and end apart: 5, of which 4 were waited for; matrix products, arithmetic and copies ran while one was open for 0% of the time, Pallas kernels for 9%

profile of v6, /device:TPU:1, one launch (start us, length us, event | category | flops | bytes accessed | tf_op | source)
XLA Modules:
  0.0 86.3 jit_solution(1983630930482586365)
XLA Ops:
  0.7 0.9 %copy-done.1 = bf16[512,128]{1,0:T(8,128)(2,1)S(1)} copy-done((bf16[512,128]{1,0:T(8,128)(2,1)S(1)}, bf16[512,128]{1,0:T(8,128)(2,1)}, u32[]{:S(2)}) %copy-start.1) | copy-done | bytes 131096
  1.5 0.1 copy-done.2
  1.6 0.2 state_body.1
  1.8 19.4 %all_to_all.25.parts_ref.refs_1_ = bf16[8,128,128]{2,1,0:T(8,128)(2,1)S(1)} all-to-all(bf16[8,128,128]{2,1,0:T(8,128)(2,1)S(1)} %state_body.1), channel_id=1, replica_groups={{0,12,24,36,48,60,72,84},{96,108,120,132,144,156,168,180},{192,204,216,..., dimensions={0} | all-to-all | bytes 524288 | tf_op jit(solution)/shard_map/all_to_all | solution.py:329
  21.3 0.8 total_body.2.refs_7_.refs_2_
  22.1 0.0 copy-start.3
  22.1 0.0 copy-start.4
  22.1 3.6 %all-to-all-start.1 = ((bf16[8,128,128]{2,1,0:T(8,128)(2,1)}), bf16[8,128,128]{2,1,0:T(8,128)(2,1)S(1)}, u32[]{:S(2)}, u32[]{:S(2)}) async-start(bf16[8,128,128]{2,1,0:T(8,128)(2,1)} %total_body.2.refs_7_.refs_2_), calls=%async_computation.1 | async-start | bytes 524288 | tf_op jit(solution)/shard_map/all_to_all | solution.py:332
  25.7 0.0 copy-start
  25.7 0.0 copy-start.5
  25.7 0.0 copy-start.6
  25.8 3.3 %collective-permute-start = (bf16[1024,128]{1,0:T(8,128)(2,1)S(1)}, bf16[1024,128]{1,0:T(8,128)(2,1)S(1)}, u32[]{:S(2)}, u32[]{:S(2)}) collective-permute-start(bf16[1024,128]{1,0:T(8,128)(2,1)S(1)} %pack_body.1), channel_id=1, source_target_pairs={{0,12},{12,24},{24,36},{36,48},{48,60},{60,72},{72,84},{84,96},{96... | collective-permute-start | bytes 786440 | tf_op jit(solution)/shard_map/ppermute | solution.py:348
  29.0 1.0 %inner_body.1 = (bf16[512,512]{1,0:T(8,128)(2,1)S(1)}, bf16[1024,128]{1,0:T(8,128)(2,1)S(1)}, f32[128,512]{1,0:T(8,128)S(1)}, f32[128,512]{1,0:T(8,128)S(1)}, f32[128,128]{1,0:T(8,128)S(1)}) custom-call(f32[40,128]{1,0:T(8,128)S(1)} %chosen_body.1.refs_2_.refs_0_.chosen_ref, bf16[8,128,128]{2,1,0:T(8,128)(2,1)S(1)} %all_to_all.25.parts_ref.refs_1_, ...), custom_call_target="tpu_custom_call" | custom-call | flops 83886080 | bytes 1048576 | tf_op jit(solution)/shard_map/inner_body/pallas_call | solution.py:377
  30.0 5.7 %all-to-all-done.1.rows_ref = bf16[8,128,128]{2,1,0:T(8,128)(2,1)S(1)} async-done(((bf16[8,128,128]{2,1,0:T(8,128)(2,1)}), bf16[8,128,128]{2,1,0:T(8,128)(2,1)S(1)}, u32[]{:S(2)}, u32[]{:S(2)}) %all-to-all-start.1) | async-done | bytes 262176 | tf_op jit(solution)/shard_map/all_to_all | solution.py:332
  35.8 1.1 %normed_body.1 = (f32[128,512]{1,0:T(8,128)S(1)}, f32[128,128]{1,0:T(8,128)S(1)}, f32[12,8,128]{2,1,0:T(8,128)}) custom-call(f32[40,128]{1,0:T(8,128)S(1)} %chosen_body.1.refs_2_.refs_0_.chosen_ref, bf16[8,128,128]{2,1,0:T(8,128)(2,1)S(1)} %all-to-all-done.1.rows_ref, f32[128,128]{1,0:T(8,128)S(1)} %get-tuple-element.32.base_ref, ...), custom_call_target="tpu_custom_call" | custom-call | flops 33554432 | bytes 1048576 | tf_op jit(solution)/shard_map/normed_body/pallas_call | solution.py:392
  36.8 11.0 %all-to-all-start.2 = ((f32[12,8,128]{2,1,0:T(8,128)}), f32[12,8,128]{2,1,0:T(8,128)S(1)}, u32[]{:S(2)}, u32[]{:S(2)}) async-start(f32[12,8,128]{2,1,0:T(8,128)} %get-tuple-element.35.refs_6_.refs_7_), calls=%async_computation.2 | async-start | bytes 98304 | tf_op jit(solution)/shard_map/all_to_all | solution.py:421
  47.8 0.0 copy-start.8
  47.8 0.0 copy-start.10
  47.8 0.0 collective-permute-done.refs_5_.refs_3_
  47.9 1.4 %window_body.1 = (bf16[1024,128]{1,0:T(8,128)(2,1)S(1)}, bf16[512,512]{1,0:T(8,128)(2,1)S(1)}, bf16[512,512]{1,0:T(8,128)(2,1)S(1)}, bf16[512,512]{1,0:T(8,128)(2,1)S(1)}) custom-call(f32[40,128]{1,0:T(8,128)S(1)} %chosen_body.1.refs_2_.refs_0_.chosen_ref, bf16[512,128]{1,0:T(8,128)(2,1)S(1)} %copy-done.7, bf16[512,128]{1,0:T(8,128)(2,1)S(1)} %copy-done.4, ...), custom_call_target="tpu_custom_call" | custom-call | flops 268435456 | bytes 2621440 | tf_op jit(solution)/shard_map/window_body/pallas_call | solution.py:402
  49.3 4.9 %collective-permute-start.1 = (bf16[1024,128]{1,0:T(8,128)(2,1)S(1)}, bf16[1024,128]{1,0:T(8,128)(2,1)S(1)}, u32[]{:S(2)}, u32[]{:S(2)}) collective-permute-start(bf16[1024,128]{1,0:T(8,128)(2,1)S(1)} %get-tuple-element.37), channel_id=1, source_target_pairs={{12,0},{24,12},{36,24},{48,36},{60,48},{72,60},{84,72},{96,84},{10... | collective-permute-start | bytes 786440 | tf_op jit(solution)/shard_map/ppermute | solution.py:348
  54.3 1.3 %own_body.1 = (bf16[512,128]{1,0:T(8,128)(2,1)}, f32[512,128]{1,0:T(8,128)S(1)}, f32[512,128]{1,0:T(8,128)S(1)}) custom-call(bf16[512,512]{1,0:T(8,128)(2,1)S(1)} %get-tuple-element.38.refs_0_, bf16[512,512]{1,0:T(8,128)(2,1)S(1)} %get-tuple-element.39.refs_1_, bf16[512,512]{1,0:T(8,128)(2,1)S(1)} %get-tuple-element.40.refs_2_, ...), custom_call_target="tpu_custom_call" | custom-call | flops 4000000000 | bytes 2621440 | tf_op jit(solution)/shard_map/own_body/pallas_call | solution.py:413
  55.5 1.9 %all-to-all-done.2.refs_0_ = f32[12,8,128]{2,1,0:T(8,128)S(1)} async-done(((f32[12,8,128]{2,1,0:T(8,128)}), f32[12,8,128]{2,1,0:T(8,128)S(1)}, u32[]{:S(2)}, u32[]{:S(2)}) %all-to-all-start.2) | async-done | bytes 49184 | tf_op jit(solution)/shard_map/all_to_all | solution.py:421
  57.5 1.2 %collective-permute-done.1.refs_4_.refs_2_ = bf16[1024,128]{1,0:T(8,128)(2,1)S(1)} collective-permute-done((bf16[1024,128]{1,0:T(8,128)(2,1)S(1)}, bf16[1024,128]{1,0:T(8,128)(2,1)S(1)}, u32[]{:S(2)}, u32[]{:S(2)}) %collective-permute-start.1) | collective-permute-done | bytes 262176 | tf_op jit(solution)/shard_map/ppermute | solution.py:348
  58.7 0.3 grad_out_body.1
  59.0 11.8 %all_to_all.26.parts_ref.refs_1_ = bf16[8,128,128]{2,1,0:T(8,128)(2,1)S(1)} all-to-all(bf16[8,128,128]{2,1,0:T(8,128)(2,1)S(1)} %get-tuple-element.42), channel_id=1, replica_groups={{0,12,24,36,48,60,72,84},{96,108,120,132,144,156,168,180},{192,204,216,..., dimensions={0} | all-to-all | bytes 524288 | tf_op jit(solution)/shard_map/all_to_all | solution.py:329
  70.9 0.8 total_body.3.refs_7_.refs_3_
  71.7 3.4 %all-to-all-start.4 = ((bf16[8,128,128]{2,1,0:T(8,128)(2,1)}), bf16[8,128,128]{2,1,0:T(8,128)(2,1)S(1)}, u32[]{:S(2)}, u32[]{:S(2)}) async-start(bf16[8,128,128]{2,1,0:T(8,128)(2,1)} %total_body.3.refs_7_.refs_3_), calls=%async_computation.4 | async-start | bytes 524288 | tf_op jit(solution)/shard_map/all_to_all | solution.py:332
  75.1 0.7 settle_body.1
  75.9 1.9 %mixed_body.1 = (bf16[512,128]{1,0:T(8,128)(2,1)}, f32[512,128]{1,0:T(8,128)S(1)}, f32[512,128]{1,0:T(8,128)S(1)}, f32[128,128]{1,0:T(8,128)S(1)}) custom-call(f32[40,128]{1,0:T(8,128)S(1)} %chosen_body.1.refs_2_.refs_0_.chosen_ref, bf16[8,128,128]{2,1,0:T(8,128)(2,1)S(1)} %all_to_all.26.parts_ref.refs_1_, bf16[128,512]{1,0:T(8,128)(2,1)S(1)} %get-tuple-element.43.refs_2_, ...), custom_call_target="tpu_custom_call" | custom-call | flops 167772160 | bytes 1310720 | tf_op jit(solution)/shard_map/mixed_body/pallas_call | solution.py:433
  77.7 7.5 %all-to-all-done.4.refs_1_ = bf16[8,128,128]{2,1,0:T(8,128)(2,1)S(1)} async-done(((bf16[8,128,128]{2,1,0:T(8,128)(2,1)}), bf16[8,128,128]{2,1,0:T(8,128)(2,1)S(1)}, u32[]{:S(2)}, u32[]{:S(2)}) %all-to-all-start.4) | async-done | bytes 262176 | tf_op jit(solution)/shard_map/all_to_all | solution.py:332
  85.2 1.1 %closing_body.1 = (bf16[512,128]{1,0:T(8,128)(2,1)}, bf16[512,128]{1,0:T(8,128)(2,1)}) custom-call(f32[40,128]{1,0:T(8,128)S(1)} %chosen_body.1.refs_2_.refs_0_.chosen_ref, bf16[8,128,128]{2,1,0:T(8,128)(2,1)S(1)} %all-to-all-done.4.refs_1_, f32[128,128]{1,0:T(8,128)S(1)} %get-tuple-element.48.refs_2_, f32[512,128]{1,0:T(8,128)S(1)} %get-tuple-element.49.refs_3_, ...), custom_call_target="tpu_custom_call" | custom-call | flops 67108864 | bytes 1048576 | tf_op jit(solution)/shard_map/closing_body/pallas_call | solution.py:451
  (15 shorter events, 0.1 us)
Async XLA Ops:
  0.6 0.9 %copy-start.1 = (bf16[512,128]{1,0:T(8,128)(2,1)S(1)}, bf16[512,128]{1,0:T(8,128)(2,1)}, u32[]{:S(2)}) copy-start(bf16[512,128]{1,0:T(8,128)(2,1)} %refs_3_.4) | copy-start | bytes 393220
  0.6 1.0 %copy-start.2 = (bf16[512,128]{1,0:T(8,128)(2,1)S(1)}, bf16[512,128]{1,0:T(8,128)(2,1)}, u32[]{:S(2)}) copy-start(bf16[512,128]{1,0:T(8,128)(2,1)} %refs_4_.3) | copy-start | bytes 393220
  22.1 3.6 %copy-start.3 = (bf16[512,128]{1,0:T(8,128)(2,1)S(1)}, bf16[512,128]{1,0:T(8,128)(2,1)}, u32[]{:S(2)}) copy-start(bf16[512,128]{1,0:T(8,128)(2,1)} %refs_3_.5) | copy-start | bytes 393220
  22.1 3.6 %copy-start.4 = (bf16[512,128]{1,0:T(8,128)(2,1)S(1)}, bf16[512,128]{1,0:T(8,128)(2,1)}, u32[]{:S(2)}) copy-start(bf16[512,128]{1,0:T(8,128)(2,1)} %refs_5_.3) | copy-start | bytes 393220
  22.1 13.6 %all-to-all-start.1 = ((bf16[8,128,128]{2,1,0:T(8,128)(2,1)}), bf16[8,128,128]{2,1,0:T(8,128)(2,1)S(1)}, u32[]{:S(2)}, u32[]{:S(2)}) async-start(bf16[8,128,128]{2,1,0:T(8,128)(2,1)} %total_body.2.refs_7_.refs_2_), calls=%async_computation.1 | async-start | bytes 524288 | tf_op jit(solution)/shard_map/all_to_all | solution.py:332
  25.7 3.3 %copy-start = (bf16[512,128]{1,0:T(8,128)(2,1)S(1)}, bf16[512,128]{1,0:T(8,128)(2,1)}, u32[]{:S(2)}) copy-start(bf16[512,128]{1,0:T(8,128)(2,1)} %refs_3_.7) | copy-start | bytes 393220
  25.7 3.3 %copy-start.5 = (bf16[512,128]{1,0:T(8,128)(2,1)S(1)}, bf16[512,128]{1,0:T(8,128)(2,1)}, u32[]{:S(2)}) copy-start(bf16[512,128]{1,0:T(8,128)(2,1)} %refs_5_.2) | copy-start | bytes 393220
  25.7 3.3 %copy-start.6 = (f32[128]{0:T(128)S(1)}, f32[128]{0:T(128)}, u32[]{:S(2)}) copy-start(f32[128]{0:T(128)} %param.12) | copy-start | bytes 1540
  25.8 22.1 %collective-permute-start = (bf16[1024,128]{1,0:T(8,128)(2,1)S(1)}, bf16[1024,128]{1,0:T(8,128)(2,1)S(1)}, u32[]{:S(2)}, u32[]{:S(2)}) collective-permute-start(bf16[1024,128]{1,0:T(8,128)(2,1)S(1)} %pack_body.1), channel_id=1, source_target_pairs={{0,12},{12,24},{24,36},{36,48},{48,60},{60,72},{72,84},{84,96},{96... | collective-permute-start | bytes 786440 | tf_op jit(solution)/shard_map/ppermute | solution.py:348
  35.7 12.1 %copy-start.7 = (bf16[512,128]{1,0:T(8,128)(2,1)S(1)}, bf16[512,128]{1,0:T(8,128)(2,1)}, u32[]{:S(2)}) copy-start(bf16[512,128]{1,0:T(8,128)(2,1)} %refs_4_.5) | copy-start | bytes 393220
  35.8 12.1 %copy-start.9 = (bf16[512,128]{1,0:T(8,128)(2,1)S(1)}, bf16[512,128]{1,0:T(8,128)(2,1)}, u32[]{:S(2)}) copy-start(bf16[512,128]{1,0:T(8,128)(2,1)} %refs_6_.1) | copy-start | bytes 393220
  36.8 20.7 %all-to-all-start.2 = ((f32[12,8,128]{2,1,0:T(8,128)}), f32[12,8,128]{2,1,0:T(8,128)S(1)}, u32[]{:S(2)}, u32[]{:S(2)}) async-start(f32[12,8,128]{2,1,0:T(8,128)} %get-tuple-element.35.refs_6_.refs_7_), calls=%async_computation.2 | async-start | bytes 98304 | tf_op jit(solution)/shard_map/all_to_all | solution.py:421
  47.8 6.4 %copy-start.8 = (bf16[512,128]{1,0:T(8,128)(2,1)S(1)}, bf16[512,128]{1,0:T(8,128)(2,1)}, u32[]{:S(2)}) copy-start(bf16[512,128]{1,0:T(8,128)(2,1)} %refs_4_.5) | copy-start | bytes 393220
  47.8 6.4 %copy-start.10 = (bf16[512,128]{1,0:T(8,128)(2,1)S(1)}, bf16[512,128]{1,0:T(8,128)(2,1)}, u32[]{:S(2)}) copy-start(bf16[512,128]{1,0:T(8,128)(2,1)} %refs_6_.1) | copy-start | bytes 393220
  49.3 9.4 %collective-permute-start.1 = (bf16[1024,128]{1,0:T(8,128)(2,1)S(1)}, bf16[1024,128]{1,0:T(8,128)(2,1)S(1)}, u32[]{:S(2)}, u32[]{:S(2)}) collective-permute-start(bf16[1024,128]{1,0:T(8,128)(2,1)S(1)} %get-tuple-element.37), channel_id=1, source_target_pairs={{12,0},{24,12},{36,24},{48,36},{60,48},{72,60},{84,72},{96,84},{10... | collective-permute-start | bytes 786440 | tf_op jit(solution)/shard_map/ppermute | solution.py:348
  71.7 13.5 %all-to-all-start.4 = ((bf16[8,128,128]{2,1,0:T(8,128)(2,1)}), bf16[8,128,128]{2,1,0:T(8,128)(2,1)S(1)}, u32[]{:S(2)}, u32[]{:S(2)}) async-start(bf16[8,128,128]{2,1,0:T(8,128)(2,1)} %total_body.3.refs_7_.refs_3_), calls=%async_computation.4 | async-start | bytes 524288 | tf_op jit(solution)/shard_map/all_to_all | solution.py:332
